TPU v7x, 256 devices: a whole 4x4x8 slice. The times are simulated.
256 devices in a mesh: dp: 4 (over x), seq: 64 (over y, z, core).
Axes of the slice: x: 4, y: 4, z: 8, core: 2. Of those that a mesh axis runs over, the one named last changes fastest.
Arguments:
- query: bfloat16 [4, 8192, 1024], P('dp', 'seq'), may hold values from -70 to 70
- keys: bfloat16 [4, 8192, 1024], P('dp', 'seq'), may hold values from -70 to 70
- values: bfloat16 [4, 8192, 1024], P('dp', 'seq'), may hold values from -6 to 6
- out_grad: bfloat16 [4, 8192, 2048], P('dp', 'seq'), may hold values from -16 to 16
- out_weight: bfloat16 [2048, 1024], P('seq'), may hold values from -0.125 to 0.125
- lengths: int32 [4, 32], P('dp'), may hold values from 128 to 512, as said below
Outputs:
- query_grad: bfloat16 [4, 8192, 1024], P('dp', 'seq')
- key_grad: bfloat16 [4, 8192, 1024], P('dp', 'seq')
- value_grad: bfloat16 [4, 8192, 1024], P('dp', 'seq')
- weight_grad: float32 [2048, 1024], P(('dp', 'seq'))
Inputs may be any that keep to these rules, and one draw needn't show every extreme that they name: The lengths of a pack sum to 8192, each is a multiple of a quarter of 128, and in every pack one image has exactly 512 tokens.
All inputs are finite; a program needn't handle non-finite values.
Results may differ from a plain program's by a relative error of at most 0.04.
Values may be sent and summed in bfloat16 or wider, within the bound.
No kernel may reach another device: no remote copies, remote signals or barrier semaphores. Data moves between devices by JAX's collectives and lax.ppermute only.
A program may use at most 128 MiB of HBM per device.

v0:
```python
import math

import jax
import jax.numpy as jnp
from jax import lax
from jax.sharding import PartitionSpec as P

HEADS = 8
REACH = 4


def from_behind(block, axis, distance):
    devices = range(lax.axis_size(axis))
    route = [(i - distance, i) for i in devices if i - distance in devices]
    return lax.ppermute(block, axis, route)


def segments(lengths_row, first_pos, row_total, pack_tokens):
    positions = first_pos + jnp.arange(row_total, dtype=jnp.int32)
    image_ends = jnp.cumsum(lengths_row)
    segment = jnp.sum((positions[:, None] >= image_ends[None, :]).astype(jnp.int32), axis=1)
    inside = (positions >= 0) & (positions < pack_tokens)
    return jnp.where(inside, segment, -1)


def scores_for(query3, keys3, segment_query, segment_keys, score_scale):
    scores = (
        jnp.einsum("qhe,khe->hqk", query3, keys3, preferred_element_type=jnp.float32) * score_scale
    )
    return jnp.where((segment_query[:, None] == segment_keys[None, :])[None], scores, -1e30)


def touches(segment_query, segment_keys):
    return jnp.any(segment_query[:, None] == segment_keys[None, :])


def gradient_tile(
    query3, grad3, keys3, values3, segment_query, segment_keys, log_norm, row_delta, score_scale
):
    scores = scores_for(query3, keys3, segment_query, segment_keys, score_scale)
    probs = jnp.exp(scores - log_norm[:, :, None])
    probs_low = probs.astype(jnp.bfloat16)
    dprobs = jnp.einsum("qhe,khe->hqk", grad3, values3, preferred_element_type=jnp.float32)
    dscores = (probs * (dprobs - row_delta[:, :, None])).astype(jnp.bfloat16)
    return (probs_low, dscores)


def on_device(query, keys, values, out_grad, out_weight, lengths):
    own_query = query[0]
    own_keys = keys[0]
    own_values = values[0]
    grad_rows = out_grad[0]
    lengths_row = lengths[0]
    row_count = own_query.shape[0]
    feature_width = own_query.shape[1]
    head_size = feature_width // HEADS
    score_scale = 1.0 / math.sqrt(head_size)
    shard_index = lax.axis_index("seq")
    pack_tokens = row_count * lax.axis_size("seq")
    segment_window = segments(
        lengths_row, (shard_index - REACH) * row_count, (2 * REACH + 1) * row_count, pack_tokens
    )

    def segment_at(offset):
        return segment_window[(REACH + offset) * row_count : (REACH + offset + 1) * row_count]

    def shaped(matrix):
        return matrix.reshape(row_count, HEADS, head_size)

    segment_own = segment_at(0)
    columns = grad_rows
    attended_grad = jnp.dot(
        columns,
        lax.all_gather(out_weight, "seq", axis=0, tiled=True),
        preferred_element_type=jnp.float32,
    ).astype(jnp.bfloat16)
    query3 = shaped(own_query)
    grad3 = shaped(attended_grad)
    blocks = [(0, shaped(own_keys), shaped(own_values), segment_own)]
    for hop in range(1, REACH + 1):
        for direction in (hop, -hop):
            near_keys, near_values = from_behind((own_keys, own_values), "seq", direction)
            blocks.append(
                (-direction, shaped(near_keys), shaped(near_values), segment_at(-direction))
            )
    first_scores = scores_for(query3, blocks[0][1], segment_own, segment_own, score_scale)
    peak = jnp.max(first_scores, axis=2)
    total = jnp.sum(jnp.exp(first_scores - peak[:, :, None]), axis=2)
    for offset, keys3, values3, segment_keys in blocks[1:]:

        def refine(state, keys3=keys3, segment_keys=segment_keys):
            old_peak, old_total = state
            scores = scores_for(query3, keys3, segment_own, segment_keys, score_scale)
            new_peak = jnp.maximum(old_peak, jnp.max(scores, axis=2))
            new_total = old_total * jnp.exp(old_peak - new_peak) + jnp.sum(
                jnp.exp(scores - new_peak[:, :, None]), axis=2
            )
            return (new_peak, new_total)

        peak, total = lax.cond(
            touches(segment_own, segment_keys), refine, lambda state: state, (peak, total)
        )
    log_norm = peak + jnp.log(total)
    attended_acc = jnp.zeros((row_count, HEADS, head_size), jnp.float32)
    for offset, keys3, values3, segment_keys in blocks:

        def absorb(running, keys3=keys3, values3=values3, segment_keys=segment_keys):
            scores = scores_for(query3, keys3, segment_own, segment_keys, score_scale)
            probs_low = jnp.exp(scores - log_norm[:, :, None]).astype(jnp.bfloat16)
            return running + jnp.einsum(
                "hqk,khe->qhe", probs_low, values3, preferred_element_type=jnp.float32
            )

        attended_acc = lax.cond(
            touches(segment_own, segment_keys), absorb, lambda running: running, attended_acc
        )
    attended3 = attended_acc.astype(jnp.bfloat16)
    row_delta = jnp.sum(grad3.astype(jnp.float32) * attended3.astype(jnp.float32), axis=2).T
    empty_term = jnp.zeros((row_count, HEADS, head_size), jnp.bfloat16)
    query_acc = jnp.zeros((row_count, HEADS, head_size), jnp.float32)
    key_terms = {}
    value_terms = {}
    for offset, keys3, values3, segment_keys in blocks:
        with_terms = True

        def tile(
            running, keys3=keys3, values3=values3, segment_keys=segment_keys, with_terms=with_terms
        ):
            probs_low, dscores = gradient_tile(
                query3,
                grad3,
                keys3,
                values3,
                segment_own,
                segment_keys,
                log_norm,
                row_delta,
                score_scale,
            )
            running = running + jnp.einsum(
                "hqk,khe->qhe", dscores, keys3, preferred_element_type=jnp.float32
            )
            key_term = (
                score_scale
                * jnp.einsum("hqk,qhe->khe", dscores, query3, preferred_element_type=jnp.float32)
            ).astype(jnp.bfloat16)
            value_term = jnp.einsum(
                "hqk,qhe->khe", probs_low, grad3, preferred_element_type=jnp.float32
            ).astype(jnp.bfloat16)
            return (running, key_term, value_term)

        query_acc, key_terms[offset], value_terms[offset] = lax.cond(
            touches(segment_own, segment_keys),
            tile,
            lambda running: (running, empty_term, empty_term),
            query_acc,
        )
    query_grad = (score_scale * query_acc).reshape(row_count, feature_width).astype(jnp.bfloat16)
    attended_all = attended3.reshape(row_count, feature_width)
    columns = grad_rows
    weight_grad = lax.psum_scatter(
        lax.dot_general(
            columns, attended_all, (((0,), (0,)), ((), ())), preferred_element_type=jnp.float32
        ),
        ("dp", "seq"),
        scatter_dimension=0,
        tiled=True,
    )
    key_total = key_terms[0].astype(jnp.float32)
    value_total = value_terms[0].astype(jnp.float32)
    for hop in range(1, REACH + 1):
        for direction in (hop, -hop):
            offset = -direction
            got_keys, got_values = from_behind(
                (key_terms[offset], value_terms[offset]), "seq", -direction
            )
            key_total = key_total + got_keys.astype(jnp.float32)
            value_total = value_total + got_values.astype(jnp.float32)
    key_grad = key_total.reshape(row_count, feature_width).astype(jnp.bfloat16)
    value_grad = value_total.reshape(row_count, feature_width).astype(jnp.bfloat16)
    return (query_grad[None], key_grad[None], value_grad[None], weight_grad)


def solution(mesh):
    in_specs = (
        P("dp", "seq", None),
        P("dp", "seq", None),
        P("dp", "seq", None),
        P("dp", "seq", None),
        P("seq", None),
        P("dp", None),
    )
    out_specs = (
        P("dp", "seq", None),
        P("dp", "seq", None),
        P("dp", "seq", None),
        P(("dp", "seq"), None),
    )
    return jax.shard_map(
        on_device, mesh=mesh, in_specs=in_specs, out_specs=out_specs, check_vma=False
    )
```

profile of v0, /device:TPU:0, one launch (start us, length us, event | category | flops | bytes accessed | tf_op | source)
XLA Modules:
  0.0 1410.3 jit_solution(556764989849195525)
XLA Ops:
  8.0 1.8 copy.323
  9.8 2.8 collective-permute-start.10
  12.5 1.3 collective-permute-start.9
  13.8 3.0 collective-permute-start.8
  16.9 1.1 copy.303
  18.0 1.3 collective-permute-start.7
  19.3 5.5 collective-permute-start.6
  25.8 1.3 collective-permute-start.5
  27.2 6.7 collective-permute-start.4
  33.8 1.3 collective-permute-start.3
  35.2 4.6 collective-permute-start.2
  39.7 1.3 collective-permute-start.1
  41.0 4.1 collective-permute-start
  45.1 1.1 fusion.218
  46.2 1.1 copy.302
  47.6 1.3 collective-permute-start.15
  48.9 9.6 collective-permute-start.14
  58.6 1.3 collective-permute-start.13
  59.9 6.3 collective-permute-start.12
  66.2 1.3 collective-permute-start.11
  75.1 1.5 conditional.34
  75.2 1.4 convolution_bitcast_fusion
  76.6 1.6 conditional.36
  76.7 1.4 fusion.29
  78.2 3.8 collective-permute-done.11
  82.0 1.5 conditional.38
  82.1 1.5 fusion.51
  83.6 1.6 conditional.40
  83.7 1.5 fusion.73
  85.4 15.3 %all-gather.2.cloned.1.call-done = bf16[2048,1024]{1,0:T(8,128)(2,1)} async-done(((bf16[32,1024]{1,0:T(8,128)(2,1)}), bf16[2048,1024]{1,0:T(8,128)(2,1)}) %all-gather.2.cloned.1.call-update) | async-done | bytes 4194320 | tf_op jit(solution)/shard_map/all_gather | solution.py:74
  100.7 2.9 convolution_convert_fusion.9
  104.5 1.1 copy.392
  105.6 4.5 convolution_bitcast_fusion.18
  110.1 9.3 copy.484
  120.4 2.6 conditional.43
  120.9 1.2 fusion.99
  124.9 2.6 conditional.45
  125.3 1.2 fusion.125
  129.1 2.5 conditional.47
  129.6 1.2 fusion.149
  133.2 2.5 conditional.49
  133.6 1.2 fusion.173
  138.1 2.6 collective-permute-start.23
  140.7 3.2 collective-permute-start.31
  143.9 1.3 collective-permute-start.22
  145.2 1.3 collective-permute-start.30
  146.5 7.3 collective-permute-start.21
  154.5 9.7 collective-permute-start.29
  164.2 1.3 collective-permute-start.20
  165.6 4.5 collective-permute-start.19
  170.1 1.2 collective-permute-done.30
  171.3 1.3 collective-permute-start.18
  172.6 7.8 collective-permute-start.17
  180.4 1.3 collective-permute-start.16
  182.8 1.3 collective-permute-start.28
  184.1 3.8 collective-permute-done.19
  187.9 5.1 collective-permute-start.27
  193.0 1.3 collective-permute-start.26
  194.3 2.6 collective-permute-start.25
  196.9 1.3 collective-permute-start.24
  198.2 1.9 add_convert_fusion.1
  201.1 2.9 collective-permute-done.26
  204.0 1.6 add_convert_fusion
  206.7 1196.8 %reduce-scatter.4.cloned.1.call-done = f32[8,1024]{1,0:T(8,128)} async-done(((f32[2048,1024]{1,0:T(8,128)}), f32[8,1024]{1,0:T(8,128)}) %reduce-scatter.4.cloned.1.call-update) | async-done | bytes 32784
  (187 shorter events, 25.3 us)
Async XLA Ops:
  7.2 93.5 %copy-start = (bf16[1,128,2048]{2,1,0:T(8,128)(2,1)S(1)}, bf16[1,128,2048]{2,1,0:T(8,128)(2,1)}, u32[]{:S(2)}) copy-start(bf16[1,128,2048]{2,1,0:T(8,128)(2,1)} %param.61) | copy-start | bytes 1572868
  7.2 93.5 %all-gather.2.cloned.1.call-start = ((), (), s32[]{:S(2)}) async-start(), calls=%async_computation.1 | async-start | bytes 4259840 | tf_op jit(solution)/shard_map/all_gather | solution.py:74
  7.9 1395.5 %reduce-scatter.4.cloned.1.call-start = ((), (), s32[]{:S(2)}) async-start(), calls=%async_computation.2 | async-start | bytes 8421376
  9.8 16.1 %collective-permute-start.10 = (bf16[128,1024]{0,1:T(8,128)(2,1)}, bf16[128,1024]{0,1:T(8,128)(2,1)}, u32[]{:S(2)}, u32[]{:S(2)}) collective-permute-start(bf16[128,1024]{0,1:T(8,128)(2,1)} %bitcast.49), channel_id=1, source_target_pairs={{0,2},{1,3},{2,4},{3,5},{4,6},{5,7},{6,8},{7,9},{8,10},{9,11},{10,... | collective-permute-start | bytes 786440 | tf_op jit(solution)/shard_map/ppermute | solution.py:15
  12.5 14.6 %collective-permute-start.9 = (bf16[128,1024]{0,1:T(8,128)(2,1)}, bf16[128,1024]{0,1:T(8,128)(2,1)}, u32[]{:S(2)}, u32[]{:S(2)}) collective-permute-start(bf16[128,1024]{0,1:T(8,128)(2,1)} %bitcast.49), channel_id=1, source_target_pairs={{1,0},{2,1},{3,2},{4,3},{5,4},{6,5},{7,6},{8,7},{9,8},{10,9},{11,1... | collective-permute-start | bytes 786440 | tf_op jit(solution)/shard_map/ppermute | solution.py:15
  13.8 20.0 %collective-permute-start.8 = (bf16[128,1024]{0,1:T(8,128)(2,1)}, bf16[128,1024]{0,1:T(8,128)(2,1)S(1)}, u32[]{:S(2)}, u32[]{:S(2)}) collective-permute-start(bf16[128,1024]{0,1:T(8,128)(2,1)} %bitcast.49), channel_id=1, source_target_pairs={{0,1},{1,2},{2,3},{3,4},{4,5},{5,6},{6,7},{7,8},{8,9},{9,10},{10,1... | collective-permute-start | bytes 786440 | tf_op jit(solution)/shard_map/ppermute | solution.py:15
  18.0 17.1 %collective-permute-start.7 = (bf16[128,1024]{0,1:T(8,128)(2,1)S(1)}, bf16[128,1024]{0,1:T(8,128)(2,1)S(1)}, u32[]{:S(2)}, u32[]{:S(2)}) collective-permute-start(bf16[128,1024]{0,1:T(8,128)(2,1)S(1)} %bitcast.289), channel_id=1, source_target_pairs={{4,0},{5,1},{6,2},{7,3},{8,4},{9,5},{10,6},{11,7},{12,8},{13,9},{1... | collective-permute-start | bytes 786440 | tf_op jit(solution)/shard_map/ppermute | solution.py:15
  19.3 20.4 %collective-permute-start.6 = (bf16[128,1024]{0,1:T(8,128)(2,1)S(1)}, bf16[128,1024]{0,1:T(8,128)(2,1)S(1)}, u32[]{:S(2)}, u32[]{:S(2)}) collective-permute-start(bf16[128,1024]{0,1:T(8,128)(2,1)S(1)} %bitcast.290), channel_id=1, source_target_pairs={{0,4},{1,5},{2,6},{3,7},{4,8},{5,9},{6,10},{7,11},{8,12},{9,13},{1... | collective-permute-start | bytes 786440 | tf_op jit(solution)/shard_map/ppermute | solution.py:15
  25.8 15.2 %collective-permute-start.5 = (bf16[128,1024]{0,1:T(8,128)(2,1)S(1)}, bf16[128,1024]{0,1:T(8,128)(2,1)S(1)}, u32[]{:S(2)}, u32[]{:S(2)}) collective-permute-start(bf16[128,1024]{0,1:T(8,128)(2,1)S(1)} %bitcast.291), channel_id=1, source_target_pairs={{3,0},{4,1},{5,2},{6,3},{7,4},{8,5},{9,6},{10,7},{11,8},{12,9},{13... | collective-permute-start | bytes 786440 | tf_op jit(solution)/shard_map/ppermute | solution.py:15
  27.2 20.4 %collective-permute-start.4 = (bf16[128,1024]{0,1:T(8,128)(2,1)S(1)}, bf16[128,1024]{0,1:T(8,128)(2,1)S(1)}, u32[]{:S(2)}, u32[]{:S(2)}) collective-permute-start(bf16[128,1024]{0,1:T(8,128)(2,1)S(1)} %bitcast.292), channel_id=1, source_target_pairs={{0,3},{1,4},{2,5},{3,6},{4,7},{5,8},{6,9},{7,10},{8,11},{9,12},{10... | collective-permute-start | bytes 786440 | tf_op jit(solution)/shard_map/ppermute | solution.py:15
  33.8 11.3 copy-start.9
  33.8 15.1 %collective-permute-start.3 = (bf16[128,1024]{0,1:T(8,128)(2,1)S(1)}, bf16[128,1024]{0,1:T(8,128)(2,1)S(1)}, u32[]{:S(2)}, u32[]{:S(2)}) collective-permute-start(bf16[128,1024]{0,1:T(8,128)(2,1)S(1)} %bitcast.293), channel_id=1, source_target_pairs={{2,0},{3,1},{4,2},{5,3},{6,4},{7,5},{8,6},{9,7},{10,8},{11,9},{12,... | collective-permute-start | bytes 786440 | tf_op jit(solution)/shard_map/ppermute | solution.py:15
  35.2 23.4 %collective-permute-start.2 = (bf16[128,1024]{0,1:T(8,128)(2,1)S(1)}, bf16[128,1024]{0,1:T(8,128)(2,1)S(1)}, u32[]{:S(2)}, u32[]{:S(2)}) collective-permute-start(bf16[128,1024]{0,1:T(8,128)(2,1)S(1)} %bitcast.294), channel_id=1, source_target_pairs={{0,2},{1,3},{2,4},{3,5},{4,6},{5,7},{6,8},{7,9},{8,10},{9,11},{10,... | collective-permute-start | bytes 786440 | tf_op jit(solution)/shard_map/ppermute | solution.py:15
  39.7 20.1 %collective-permute-start.1 = (bf16[128,1024]{0,1:T(8,128)(2,1)S(1)}, bf16[128,1024]{0,1:T(8,128)(2,1)S(1)}, u32[]{:S(2)}, u32[]{:S(2)}) collective-permute-start(bf16[128,1024]{0,1:T(8,128)(2,1)S(1)} %bitcast.295), channel_id=1, source_target_pairs={{1,0},{2,1},{3,2},{4,3},{5,4},{6,5},{7,6},{8,7},{9,8},{10,9},{11,1... | collective-permute-start | bytes 786440 | tf_op jit(solution)/shard_map/ppermute | solution.py:15
  41.0 25.1 %collective-permute-start = (bf16[128,1024]{0,1:T(8,128)(2,1)S(1)}, bf16[128,1024]{0,1:T(8,128)(2,1)}, u32[]{:S(2)}, u32[]{:S(2)}) collective-permute-start(bf16[128,1024]{0,1:T(8,128)(2,1)S(1)} %bitcast.296), channel_id=1, source_target_pairs={{0,1},{1,2},{2,3},{3,4},{4,5},{5,6},{6,7},{7,8},{8,9},{9,10},{10,1... | collective-permute-start | bytes 786440 | tf_op jit(solution)/shard_map/ppermute | solution.py:15
  47.6 37.6 %collective-permute-start.15 = (bf16[128,1024]{0,1:T(8,128)(2,1)}, bf16[128,1024]{0,1:T(8,128)(2,1)}, u32[]{:S(2)}, u32[]{:S(2)}) collective-permute-start(bf16[128,1024]{0,1:T(8,128)(2,1)} %bitcast.49), channel_id=1, source_target_pairs={{4,0},{5,1},{6,2},{7,3},{8,4},{9,5},{10,6},{11,7},{12,8},{13,9},{1... | collective-permute-start | bytes 786440 | tf_op jit(solution)/shard_map/ppermute | solution.py:15
  48.9 36.3 %collective-permute-start.14 = (bf16[128,1024]{0,1:T(8,128)(2,1)}, bf16[128,1024]{0,1:T(8,128)(2,1)}, u32[]{:S(2)}, u32[]{:S(2)}) collective-permute-start(bf16[128,1024]{0,1:T(8,128)(2,1)} %bitcast.49), channel_id=1, source_target_pairs={{0,4},{1,5},{2,6},{3,7},{4,8},{5,9},{6,10},{7,11},{8,12},{9,13},{1... | collective-permute-start | bytes 786440 | tf_op jit(solution)/shard_map/ppermute | solution.py:15
  58.6 25.0 %collective-permute-start.13 = (bf16[128,1024]{0,1:T(8,128)(2,1)}, bf16[128,1024]{0,1:T(8,128)(2,1)}, u32[]{:S(2)}, u32[]{:S(2)}) collective-permute-start(bf16[128,1024]{0,1:T(8,128)(2,1)} %bitcast.49), channel_id=1, source_target_pairs={{3,0},{4,1},{5,2},{6,3},{7,4},{8,5},{9,6},{10,7},{11,8},{12,9},{13... | collective-permute-start | bytes 786440 | tf_op jit(solution)/shard_map/ppermute | solution.py:15
  59.9 16.8 %copy-start.1 = (bf16[128,1024]{0,1:T(8,128)(2,1)}, bf16[128,1024]{0,1:T(8,128)(2,1)S(1)}, u32[]{:S(2)}) copy-start(bf16[128,1024]{0,1:T(8,128)(2,1)S(1)} %collective-permute-done.1) | copy-start | bytes 786436
  59.9 23.7 %collective-permute-start.12 = (bf16[128,1024]{0,1:T(8,128)(2,1)}, bf16[128,1024]{0,1:T(8,128)(2,1)}, u32[]{:S(2)}, u32[]{:S(2)}) collective-permute-start(bf16[128,1024]{0,1:T(8,128)(2,1)} %bitcast.49), channel_id=1, source_target_pairs={{0,3},{1,4},{2,5},{3,6},{4,7},{5,8},{6,9},{7,10},{8,11},{9,12},{10... | collective-permute-start | bytes 786440 | tf_op jit(solution)/shard_map/ppermute | solution.py:15
  66.2 15.8 %collective-permute-start.11 = (bf16[128,1024]{0,1:T(8,128)(2,1)}, bf16[128,1024]{0,1:T(8,128)(2,1)}, u32[]{:S(2)}, u32[]{:S(2)}) collective-permute-start(bf16[128,1024]{0,1:T(8,128)(2,1)} %bitcast.49), channel_id=1, source_target_pairs={{2,0},{3,1},{4,2},{5,3},{6,4},{7,5},{8,6},{9,7},{10,8},{11,9},{12,... | collective-permute-start | bytes 786440 | tf_op jit(solution)/shard_map/ppermute | solution.py:15
  103.6 6.5 copy-start.3
  119.4 0.9 copy-start.4
  123.0 0.9 copy-start.5
  123.0 1.0 copy-start.7
  123.0 1.1 copy-start.2
  124.1 0.8 copy-start.12
  127.4 0.7 copy-start.14
  127.4 0.8 copy-start.16
  128.3 0.7 copy-start.17
  128.3 0.8 copy-start.18
  131.7 0.7 copy-start.20
  131.7 0.8 copy-start.19
  132.5 3.3 copy-start.22
  135.7 0.7 copy-start.24
  135.7 0.8 copy-start.23
  137.3 0.7 copy-start.25
  137.3 43.1 %copy-start.13 = (bf16[128,8,128]{2,0,1:T(8,128)(2,1)S(1)}, bf16[128,8,128]{2,0,1:T(8,128)(2,1)}, u32[]{:S(2)}) copy-start(bf16[128,8,128]{2,0,1:T(8,128)(2,1)} %copy-done.12) | copy-start | bytes 786436
  137.3 57.0 %copy-start.15 = (bf16[128,8,128]{2,0,1:T(8,128)(2,1)S(1)}, bf16[128,8,128]{2,0,1:T(8,128)(2,1)}, u32[]{:S(2)}) copy-start(bf16[128,8,128]{2,0,1:T(8,128)(2,1)} %copy-done.14) | copy-start | bytes 786436
  137.3 59.6 %copy-start.11 = (bf16[128,8,128]{2,0,1:T(8,128)(2,1)S(1)}, bf16[128,8,128]{2,0,1:T(8,128)(2,1)}, u32[]{:S(2)}) copy-start(bf16[128,8,128]{2,0,1:T(8,128)(2,1)} %copy-done.10) | copy-start | bytes 786436
  137.3 60.9 %copy-start.8 = (f32[128,8,128]{2,0,1:T(8,128)S(1)}, f32[128,8,128]{2,0,1:T(8,128)}, u32[]{:S(2)}) copy-start(f32[128,8,128]{2,0,1:T(8,128)} %copy-done.7) | copy-start | bytes 1572868
  138.1 65.9 %copy-start.6 = (f32[128,8,128]{2,0,1:T(8,128)S(1)}, f32[128,8,128]{2,0,1:T(8,128)}, u32[]{:S(2)}) copy-start(f32[128,8,128]{2,0,1:T(8,128)} %copy-done.5) | copy-start | bytes 1572868
  138.1 15.7 %collective-permute-start.23 = (bf16[128,8,128]{2,0,1:T(8,128)(2,1)S(1)}, bf16[128,8,128]{2,0,1:T(8,128)(2,1)S(1)}, u32[]{:S(2)}, u32[]{:S(2)}) collective-permute-start(bf16[128,8,128]{2,0,1:T(8,128)(2,1)S(1)} %get-tuple-element.751), channel_id=1, source_target_pairs={{0,4},{1,5},{2,6},{3,7},{4,8},{5,9},{6,10},{7,11},{8,12},{9,13},{1... | collective-permute-start | bytes 786440 | tf_op jit(solution)/shard_map/ppermute | solution.py:15
  140.7 23.5 %collective-permute-start.31 = (bf16[128,8,128]{2,0,1:T(8,128)(2,1)S(1)}, bf16[128,8,128]{2,0,1:T(8,128)(2,1)S(1)}, u32[]{:S(2)}, u32[]{:S(2)}) collective-permute-start(bf16[128,8,128]{2,0,1:T(8,128)(2,1)S(1)} %get-tuple-element.760), channel_id=1, source_target_pairs={{0,4},{1,5},{2,6},{3,7},{4,8},{5,9},{6,10},{7,11},{8,12},{9,13},{1... | collective-permute-start | bytes 786440 | tf_op jit(solution)/shard_map/ppermute | solution.py:15
  143.9 21.7 %collective-permute-start.22 = (bf16[128,8,128]{2,0,1:T(8,128)(2,1)}, bf16[128,8,128]{2,0,1:T(8,128)(2,1)S(1)}, u32[]{:S(2)}, u32[]{:S(2)}) collective-permute-start(bf16[128,8,128]{2,0,1:T(8,128)(2,1)} %get-tuple-element.750), channel_id=1, source_target_pairs={{4,0},{5,1},{6,2},{7,3},{8,4},{9,5},{10,6},{11,7},{12,8},{13,9},{1... | collective-permute-start | bytes 786440 | tf_op jit(solution)/shard_map/ppermute | solution.py:15
  145.2 26.1 %collective-permute-start.30 = (bf16[128,8,128]{2,0,1:T(8,128)(2,1)}, bf16[128,8,128]{2,0,1:T(8,128)(2,1)S(1)}, u32[]{:S(2)}, u32[]{:S(2)}) collective-permute-start(bf16[128,8,128]{2,0,1:T(8,128)(2,1)} %copy-done.25), channel_id=1, source_target_pairs={{4,0},{5,1},{6,2},{7,3},{8,4},{9,5},{10,6},{11,7},{12,8},{13,9},{1... | collective-permute-start | bytes 786440 | tf_op jit(solution)/shard_map/ppermute | solution.py:15
  146.5 26.1 %collective-permute-start.21 = (bf16[128,8,128]{2,0,1:T(8,128)(2,1)}, bf16[128,8,128]{2,0,1:T(8,128)(2,1)S(1)}, u32[]{:S(2)}, u32[]{:S(2)}) collective-permute-start(bf16[128,8,128]{2,0,1:T(8,128)(2,1)} %copy-done.24), channel_id=1, source_target_pairs={{0,3},{1,4},{2,5},{3,6},{4,7},{5,8},{6,9},{7,10},{8,11},{9,12},{10... | collective-permute-start | bytes 786440 | tf_op jit(solution)/shard_map/ppermute | solution.py:15
  154.5 25.9 %collective-permute-start.29 = (bf16[128,8,128]{2,0,1:T(8,128)(2,1)}, bf16[128,8,128]{2,0,1:T(8,128)(2,1)S(1)}, u32[]{:S(2)}, u32[]{:S(2)}) collective-permute-start(bf16[128,8,128]{2,0,1:T(8,128)(2,1)} %copy-done.23), channel_id=1, source_target_pairs={{0,3},{1,4},{2,5},{3,6},{4,7},{5,8},{6,9},{7,10},{8,11},{9,12},{10... | collective-permute-start | bytes 786440 | tf_op jit(solution)/shard_map/ppermute | solution.py:15
  164.2 17.5 %copy-start.26 = (bf16[128,8,128]{2,0,1:T(8,128)(2,1)}, bf16[128,8,128]{2,0,1:T(8,128)(2,1)S(1)}, u32[]{:S(2)}) copy-start(bf16[128,8,128]{2,0,1:T(8,128)(2,1)S(1)} %collective-permute-done.31) | copy-start | bytes 786436
  164.2 18.6 %collective-permute-start.20 = (bf16[128,8,128]{2,0,1:T(8,128)(2,1)}, bf16[128,8,128]{2,0,1:T(8,128)(2,1)}, u32[]{:S(2)}, u32[]{:S(2)}) collective-permute-start(bf16[128,8,128]{2,0,1:T(8,128)(2,1)} %copy-done.22), channel_id=1, source_target_pairs={{3,0},{4,1},{5,2},{6,3},{7,4},{8,5},{9,6},{10,7},{11,8},{12,9},{13... | collective-permute-start | bytes 786440 | tf_op jit(solution)/shard_map/ppermute | solution.py:15
  165.5 16.2 %copy-start.31 = (bf16[128,8,128]{2,0,1:T(8,128)(2,1)}, bf16[128,8,128]{2,0,1:T(8,128)(2,1)S(1)}, u32[]{:S(2)}) copy-start(bf16[128,8,128]{2,0,1:T(8,128)(2,1)S(1)} %collective-permute-done.22) | copy-start | bytes 786436
  165.6 22.3 %collective-permute-start.19 = (bf16[128,8,128]{2,0,1:T(8,128)(2,1)}, bf16[128,8,128]{2,0,1:T(8,128)(2,1)}, u32[]{:S(2)}, u32[]{:S(2)}) collective-permute-start(bf16[128,8,128]{2,0,1:T(8,128)(2,1)} %copy-done.20), channel_id=1, source_target_pairs={{0,2},{1,3},{2,4},{3,5},{4,6},{5,7},{6,8},{7,9},{8,10},{9,11},{10,... | collective-permute-start | bytes 786440 | tf_op jit(solution)/shard_map/ppermute | solution.py:15
  171.3 10.5 copy-start.28
  171.3 21.7 %collective-permute-start.18 = (bf16[128,8,128]{2,0,1:T(8,128)(2,1)}, bf16[128,8,128]{2,0,1:T(8,128)(2,1)}, u32[]{:S(2)}, u32[]{:S(2)}) collective-permute-start(bf16[128,8,128]{2,0,1:T(8,128)(2,1)} %copy-done.18), channel_id=1, source_target_pairs={{2,0},{3,1},{4,2},{5,3},{6,4},{7,5},{8,6},{9,7},{10,8},{11,9},{12,... | collective-permute-start | bytes 786440 | tf_op jit(solution)/shard_map/ppermute | solution.py:15
  172.6 9.2 copy-start.32
  172.6 21.7 %collective-permute-start.17 = (bf16[128,8,128]{2,0,1:T(8,128)(2,1)}, bf16[128,8,128]{2,0,1:T(8,128)(2,1)}, u32[]{:S(2)}, u32[]{:S(2)}) collective-permute-start(bf16[128,8,128]{2,0,1:T(8,128)(2,1)} %copy-done.16), channel_id=1, source_target_pairs={{0,1},{1,2},{2,3},{3,4},{4,5},{5,6},{6,7},{7,8},{8,9},{9,10},{10,1... | collective-permute-start | bytes 786440 | tf_op jit(solution)/shard_map/ppermute | solution.py:15
  180.4 1.3 copy-start.29
  180.4 16.5 %collective-permute-start.16 = (bf16[128,8,128]{2,0,1:T(8,128)(2,1)S(1)}, bf16[128,8,128]{2,0,1:T(8,128)(2,1)}, u32[]{:S(2)}, u32[]{:S(2)}) collective-permute-start(bf16[128,8,128]{2,0,1:T(8,128)(2,1)S(1)} %copy-done.13), channel_id=1, source_target_pairs={{1,0},{2,1},{3,2},{4,3},{5,4},{6,5},{7,6},{8,7},{9,8},{10,9},{11,1... | collective-permute-start | bytes 786440 | tf_op jit(solution)/shard_map/ppermute | solution.py:15
  182.0 22.0 %copy-start.27 = (bf16[128,8,128]{2,0,1:T(8,128)(2,1)S(1)}, bf16[128,8,128]{2,0,1:T(8,128)(2,1)}, u32[]{:S(2)}) copy-start(bf16[128,8,128]{2,0,1:T(8,128)(2,1)} %copy-done.26) | copy-start | bytes 786436
  182.8 18.2 %collective-permute-start.28 = (bf16[128,8,128]{2,0,1:T(8,128)(2,1)}, bf16[128,8,128]{2,0,1:T(8,128)(2,1)S(1)}, u32[]{:S(2)}, u32[]{:S(2)}) collective-permute-start(bf16[128,8,128]{2,0,1:T(8,128)(2,1)} %copy-done.21), channel_id=1, source_target_pairs={{3,0},{4,1},{5,2},{6,3},{7,4},{8,5},{9,6},{10,7},{11,8},{12,9},{13... | collective-permute-start | bytes 786440 | tf_op jit(solution)/shard_map/ppermute | solution.py:15
  187.9 13.2 collective-permute-start.27
  193.0 11.1 collective-permute-start.26
  194.3 9.7 collective-permute-start.25
  196.9 7.1 collective-permute-start.24
  (3 other events, 2.1 us)
Sparse Core Ops, SparseCore 0:
  10.8 89.8 all-gather.1
  119.6 1283.8 reduce-scatter.3
where the time goes:
time: 1410 us
  waiting for transfers between devices  1220 us (87%)
  starting transfers between devices  106 us (8%)
  local copies, waits for them, and re-layouts  27.2 us (2%)
  matrix products  24.1 us (2%)
  between operations  20.7 us (1%)
    unnamed x3, waiting for transfers between devices  1200 us
    ppermute x32, starting transfers between devices, from_behind(): return lax.ppermute(block, axis, route)  106 us
  transfers between devices with their start and end apart: 34, of which 6 were waited for; matrix products, arithmetic and copies ran while one was open for 2% of the time, Pallas kernels for 0%

commit v1 on v0

v1 whole, which is shorter than its diff:
```python
import math

import jax
import jax.numpy as jnp
from jax import lax
from jax.experimental import pallas as pl
from jax.experimental.pallas import tpu as pltpu
from jax.sharding import Mesh, PartitionSpec as P

HEADS = 8
HEAD = 128
TOK = 128
CHIP = 2 * TOK
HALF = HEADS * HEAD // 2
REACH = 2
OFFSETS = tuple(range(-REACH, REACH + 1))
SUBS = 2 * len(OFFSETS)
SCALE = 1.0 / math.sqrt(HEAD)
SWAP = [(0, 1), (1, 0)]


def nt(a, b):
    return lax.dot_general(a, b, (((1,), (1,)), ((), ())), preferred_element_type=jnp.float32)


def nn(a, b):
    return lax.dot_general(a, b, (((1,), (0,)), ((), ())), preferred_element_type=jnp.float32)


def tn(a, b):
    return lax.dot_general(a, b, (((0,), (0,)), ((), ())), preferred_element_type=jnp.float32)


def block_base(info, sub):
    own = info[0]
    core = info[1]
    parity = core if sub % 2 == 0 else 1 - core
    return own + OFFSETS[sub // 2] * CHIP + parity * TOK


def needed(info, base):
    return jnp.logical_and(base < info[3], base + TOK > info[2])


def masked_scores(keys, query, spans, base):
    scores = nt(keys, query) * SCALE
    position = base + lax.broadcasted_iota(jnp.int32, (TOK, CHIP), 0)
    taken = jnp.logical_and(position >= spans[0:1, :], position < spans[1:2, :])
    return jnp.where(taken, scores, -1e30)


def forward_kernel(info, spans, query, *rest):
    windows = rest[: len(OFFSETS)]
    attended, log_norm, scores, peak, total, acc = rest[len(OFFSETS) :]
    peak[...] = jnp.full((1, CHIP), -1e30, jnp.float32)
    total[...] = jnp.zeros((1, CHIP), jnp.float32)
    acc[...] = jnp.zeros((HEAD, CHIP), jnp.float32)
    for sub in range(SUBS):
        base = block_base(info, sub)
        rows = pl.ds(sub % 2 * TOK, TOK)

        @pl.when(needed(info, base))
        def _(sub=sub, base=base, rows=rows):
            block = masked_scores(windows[sub // 2][0, rows, :], query[...], spans, base)
            scores[sub] = block
            peak[...] = jnp.maximum(peak[...], jnp.max(block, axis=0, keepdims=True))

    for sub in range(SUBS):
        base = block_base(info, sub)
        rows = pl.ds(sub % 2 * TOK, TOK)

        @pl.when(needed(info, base))
        def _(sub=sub, rows=rows):
            weights = jnp.exp(scores[sub] - peak[...])
            total[...] += jnp.sum(weights, axis=0, keepdims=True)
            acc[...] += tn(windows[sub // 2][1, rows, :], weights.astype(jnp.bfloat16))

    attended[...] = (acc[...] * (1.0 / total[...])).T.astype(jnp.bfloat16)
    log_norm[0] = peak[...] + jnp.log(total[...])


def backward_kernel(info, spans, query, attended, log_norm, out_grad, weight, *rest):
    windows = rest[: len(OFFSETS)]
    query_grad = rest[len(OFFSETS)]
    terms = rest[len(OFFSETS) + 1 : 2 * len(OFFSETS) + 1]
    grad_f32, acc = rest[2 * len(OFFSETS) + 1 :]
    grad = nn(out_grad[...], weight[0]).astype(jnp.bfloat16)
    grad_f32[...] = grad
    acc[...] = jnp.zeros((HEAD, CHIP), jnp.float32)
    product = grad.astype(jnp.float32) * attended[...].astype(jnp.float32)
    row_delta = jnp.sum(product.T, axis=0, keepdims=True)
    for sub in range(SUBS):
        base = block_base(info, sub)
        rows = pl.ds(sub % 2 * TOK, TOK)
        touched = needed(info, base)
        term = terms[sub // 2]

        @pl.when(touched)
        def _(sub=sub, base=base, rows=rows, term=term):
            keys = windows[sub // 2][0, rows, :]
            values = windows[sub // 2][1, rows, :]
            grad_low = grad_f32[...]
            probs = jnp.exp(masked_scores(keys, query[...], spans, base) - log_norm[0])
            dprobs = nt(values, grad_low)
            dscores = (probs * (dprobs - row_delta)).astype(jnp.bfloat16)
            acc[...] += tn(keys, dscores)
            term[0, rows, :] = (SCALE * nn(dscores, query[...])).astype(term.dtype)
            term[1, rows, :] = nn(probs.astype(jnp.bfloat16), grad_low).astype(term.dtype)

        @pl.when(jnp.logical_not(touched))
        def _(rows=rows, term=term):
            term[:, rows, :] = jnp.zeros((2, TOK, HEAD), term.dtype)

    query_grad[...] = (SCALE * acc[...]).T.astype(jnp.bfloat16)


def smem():
    return pl.BlockSpec(memory_space=pltpu.SMEM)


def whole(shape):
    return pl.BlockSpec(shape, lambda h: (0,) * len(shape))


def head_columns(rows):
    return pl.BlockSpec((rows, HEAD), lambda h: (0, h))


def window_spec():
    return pl.BlockSpec((2, CHIP, HEAD), lambda h: (0, 0, h))


def forward(info, spans, query, windows):
    return pl.pallas_call(
        forward_kernel,
        grid=(HEADS // 2,),
        in_specs=[smem(), whole((2, CHIP)), head_columns(CHIP)] + [window_spec() for _ in OFFSETS],
        out_specs=[head_columns(CHIP), pl.BlockSpec((1, 1, CHIP), lambda h: (h, 0, 0))],
        out_shape=[
            jax.ShapeDtypeStruct((CHIP, HALF), jnp.bfloat16),
            jax.ShapeDtypeStruct((HEADS // 2, 1, CHIP), jnp.float32),
        ],
        scratch_shapes=[
            pltpu.VMEM((SUBS, TOK, CHIP), jnp.float32),
            pltpu.VMEM((1, CHIP), jnp.float32),
            pltpu.VMEM((1, CHIP), jnp.float32),
            pltpu.VMEM((HEAD, CHIP), jnp.float32),
        ],
        compiler_params=pltpu.CompilerParams(vmem_limit_bytes=24 * 1024 * 1024),
        cost_estimate=pl.CostEstimate(
            flops=4 * HALF * CHIP * SUBS * TOK, bytes_accessed=4 * 1024 * 1024, transcendentals=0
        ),
        name="attended",
    )(info, spans, query, *windows)


def backward(info, spans, query, attended, log_norm, out_grad, weight, windows):
    features = out_grad.shape[1]
    return pl.pallas_call(
        backward_kernel,
        grid=(HEADS // 2,),
        in_specs=[
            smem(),
            whole((2, CHIP)),
            head_columns(CHIP),
            head_columns(CHIP),
            pl.BlockSpec((1, 1, CHIP), lambda h: (h, 0, 0)),
            whole((CHIP, features)),
            pl.BlockSpec((1, features, HEAD), lambda h: (h, 0, 0)),
        ]
        + [window_spec() for _ in OFFSETS],
        out_specs=[head_columns(CHIP)] + [window_spec() for _ in OFFSETS],
        out_shape=[jax.ShapeDtypeStruct((CHIP, HALF), jnp.bfloat16)]
        + [
            jax.ShapeDtypeStruct((2, CHIP, HALF), jnp.float32 if o == 0 else jnp.bfloat16)
            for o in OFFSETS
        ],
        scratch_shapes=[
            pltpu.VMEM((CHIP, HEAD), jnp.bfloat16),
            pltpu.VMEM((HEAD, CHIP), jnp.float32),
        ],
        compiler_params=pltpu.CompilerParams(vmem_limit_bytes=24 * 1024 * 1024),
        cost_estimate=pl.CostEstimate(
            flops=10 * HALF * CHIP * SUBS * TOK,
            bytes_accessed=8 * 1024 * 1024,
            transcendentals=0,
        ),
        name="gradients",
    )(info, spans, query, attended, log_norm, out_grad, weight, *windows)


def to_chip(block, distance):
    chips = lax.axis_size("y") * lax.axis_size("z")
    route = [(i, i + distance) for i in range(chips) if 0 <= i + distance < chips]
    return lax.ppermute(block, ("y", "z"), route)


def halves(core, matrix):
    own = lax.dynamic_slice_in_dim(matrix, core * HALF, HALF, matrix.ndim - 1)
    other = lax.dynamic_slice_in_dim(matrix, (1 - core) * HALF, HALF, matrix.ndim - 1)
    return own, other


def on_device(query, keys, values, out_grad, out_weight, lengths):
    core = lax.axis_index("c")
    along_x = lax.axis_index("x")
    chip = lax.axis_index("y") * lax.axis_size("z") + lax.axis_index("z")
    size_x, size_y, size_z = (lax.axis_size(a) for a in ("x", "y", "z"))
    features = out_grad.shape[2]

    own_kv, other_kv = halves(core, jnp.stack([keys[0], values[0]]))
    chip_kv = jnp.concatenate([own_kv, lax.ppermute(other_kv, "c", SWAP)], axis=1)
    windows = [chip_kv if o == 0 else to_chip(chip_kv, -o) for o in OFFSETS]
    own_query, other_query = halves(core, query[0])
    chip_query = jnp.concatenate([own_query, lax.ppermute(other_query, "c", SWAP)], axis=0)
    chip_grad = jnp.concatenate([out_grad[0], lax.ppermute(out_grad[0], "c", SWAP)], axis=0)

    rows = out_weight.shape[0]
    piece = lax.dynamic_index_in_dim(
        out_weight.reshape(rows, 2, size_x, HEAD), along_x, 2, keepdims=False
    )
    piece = jnp.broadcast_to(piece.transpose(1, 0, 2)[None], (size_z, 2, rows, HEAD))
    piece = lax.all_to_all(piece.reshape(2 * size_z, rows, HEAD), ("z", "c"), 0, 0)
    piece = piece.reshape(1, 2 * size_z * rows, HEAD)
    piece = jnp.broadcast_to(piece, (size_x * size_y,) + piece.shape[1:])
    weight = lax.all_to_all(piece, ("x", "y"), 0, 0).reshape(size_x, features, HEAD)

    ends = jnp.cumsum(lengths[0])
    starts = ends - lengths[0]
    place = jnp.arange(CHIP, dtype=jnp.int32)
    first = chip * CHIP
    positions = first + jnp.where(core == 0, place, (place + TOK) % CHIP)
    image_start = jnp.max(
        jnp.where(starts[:, None] <= positions[None, :], starts[:, None], 0), axis=0
    )
    image_end = jnp.min(
        jnp.where(ends[:, None] > positions[None, :], ends[:, None], jnp.int32(2**30)), axis=0
    )
    spans = jnp.stack([image_start, image_end])
    info = jnp.stack([first, core, jnp.min(image_start), jnp.max(image_end)]).astype(jnp.int32)

    attended, log_norm = forward(info, spans, chip_query, windows)

    partial = tn(chip_grad, attended).astype(jnp.bfloat16)
    partial = partial.reshape(size_x * size_y, features // (size_x * size_y), HALF)
    partial = lax.all_to_all(partial, ("x", "y"), 0, 0)
    partial = jnp.sum(partial.astype(jnp.float32), axis=0).astype(jnp.bfloat16)
    partial = partial.reshape(2 * size_z, -1, HALF)
    partial = lax.all_to_all(partial, ("z", "c"), 0, 0).reshape(size_z, 2, -1, HALF)
    partial = jnp.sum(partial.astype(jnp.float32), axis=0)
    weight_grad = jnp.concatenate([partial[0], partial[1]], axis=1)

    query_grad, *terms = backward(
        info, spans, chip_query, attended, log_norm, chip_grad, weight, windows
    )
    total = terms[REACH]
    for o, term in zip(OFFSETS, terms):
        if o != 0:
            total = total + to_chip(term, o).astype(jnp.float32)
    grads = jnp.concatenate([query_grad[None], total.astype(jnp.bfloat16)], axis=0)
    mine = grads[:, :TOK]
    theirs = lax.ppermute(grads[:, TOK:], "c", SWAP)
    low = jnp.where(core == 0, mine, theirs)
    high = jnp.where(core == 0, theirs, mine)
    grads = jnp.concatenate([low, high], axis=2)
    return (grads[0:1], grads[1:2], grads[2:3], weight_grad)


def solution(mesh):
    fine = Mesh(mesh.devices.reshape(4, 4, 8, 2), ("x", "y", "z", "c"))
    tokens = P("x", ("y", "z", "c"), None)
    return jax.shard_map(
        on_device,
        mesh=fine,
        in_specs=(tokens, tokens, tokens, tokens, P(("y", "z", "c"), None), P("x", None)),
        out_specs=(tokens, tokens, tokens, P(("x", "y", "z", "c"), None)),
        check_vma=False,
    )
```

time: 1410 us -> 180 us (0.13)
  the two profiles are of different devices: /device:TPU:0 before, /device:TPU:13 now
where the time goes in v1:
time: 180 us; the launch traced here: 179 us
  starting transfers between devices  68.7 us (38%)
  waiting for transfers between devices  50.2 us (28%)
  Pallas kernels  20 us (11%)
  blocking collectives  18.1 us (10%)
  other arithmetic  11 us (6%)
  local copies, waits for them, and re-layouts  6.37 us (4%)
  matrix products  3.27 us (2%)
    ppermute x8, waiting for transfers between devices, to_chip(): return lax.ppermute(block, ('y', 'z'), route)  49 us
    ppermute x8, starting transfers between devices, to_chip(): return lax.ppermute(block, ('y', 'z'), route)  33.1 us
    all_to_all x1, blocking collectives, on_device(): lax.all_to_all(piece.reshape(2 * size_z, rows, HEAD), ('z', 'c'), 0, 0)  18.1 us
    all_to_all x1, starting transfers between devices, on_device(): partial = lax.all_to_all(partial, ('x', 'y'), 0, 0)  15.3 us
    pallas_call x1, Pallas kernels, backward(): pl.pallas_call(backward_kernel, grid=(HEADS // 2,), in_specs=[smem(), who...  11.6 us
    pallas_call x1, Pallas kernels, forward(): pl.pallas_call(forward_kernel, grid=(HEADS // 2,), in_specs=[smem(), whol...  8.41 us
    all_to_all x1, starting transfers between devices, on_device(): lax.all_to_all(partial, ('z', 'c'), 0, 0).reshape(size_z, 2, -1, HALF)  8.07 us
    all_to_all x1, starting transfers between devices, on_device(): lax.all_to_all(piece, ('x', 'y'), 0, 0).reshape(size_x, features, HEAD)  6.91 us
  transfers between devices with their start and end apart: 15, of which 6 were waited for; matrix products, arithmetic and copies ran while one was open for 8% of the time, Pallas kernels for 11%

profile of v1, /device:TPU:13, one launch (start us, length us, event | category | flops | bytes accessed | tf_op | source)
XLA Modules:
  0.0 178.6 jit_solution(7060970718468365066)
XLA Ops:
  0.6 0.9 reshape.79
  1.6 18.1 %all_to_all.20 = bf16[16,32,128]{2,1,0:T(8,128)(2,1)S(1)} all-to-all(bf16[16,32,128]{2,1,0:T(8,128)(2,1)S(1)} %bitcast.38), channel_id=1, replica_groups=mesh['x'=4,'y'=4,'z'=8,'c'=2] {'z','c'}, dimensions={0} | all-to-all | bytes 262144 | tf_op jit(solution)/shard_map/all_to_all | solution.py:223
  19.7 1.7 broadcast_in_dim.46
  21.4 0.0 copy-start.7
  21.4 6.9 %all-to-all-start.1 = ((bf16[16,512,128]{2,1,0:T(8,128)(2,1)}), bf16[16,512,128]{2,1,0:T(8,128)(2,1)S(1)}, u32[]{:S(2)}, u32[]{:S(2)}) async-start(bf16[16,512,128]{2,1,0:T(8,128)(2,1)} %broadcast_in_dim.46), calls=%async_computation.1 | async-start | bytes 4194304 | tf_op jit(solution)/shard_map/all_to_all | solution.py:226
  28.4 0.0 copy-start.10
  28.4 0.0 copy-done.7
  28.4 0.0 copy-done.8
  28.5 0.3 collective-permute-start.1
  28.8 0.5 copy-done.9
  29.3 0.7 dynamic-slice_bitcast_fusion.1
  30.0 0.2 collective-permute-start
  30.2 0.3 collective-permute-start.6
  30.5 0.0 copy-done.10
  30.5 0.1 copy.14
  30.6 0.1 reduce-window.7
  30.6 0.1 reduce.1
  30.8 0.0 collective-permute-done.1
  30.8 2.6 %collective-permute-start.5 = (bf16[2,256,512]{2,1,0:T(8,128)(2,1)S(1)}, bf16[2,256,512]{2,1,0:T(8,128)(2,1)S(1)}, u32[]{:S(2)}, u32[]{:S(2)}) collective-permute-start(bf16[2,256,512]{2,1,0:T(8,128)(2,1)S(1)} %pad_maximum_fusion.1.rest_2_), channel_id=1, source_target_pairs={{4,0},{6,2},{8,4},{10,6},{12,8},{14,10},{16,12},{18,14},{20,16},{2... | collective-permute-start | bytes 1572872 | tf_op jit(solution)/shard_map/ppermute | solution.py:195
  33.4 2.6 %collective-permute-start.4 = (bf16[2,256,512]{2,1,0:T(8,128)(2,1)S(1)}, bf16[2,256,512]{2,1,0:T(8,128)(2,1)}, u32[]{:S(2)}, u32[]{:S(2)}) collective-permute-start(bf16[2,256,512]{2,1,0:T(8,128)(2,1)S(1)} %pad_maximum_fusion.1.rest_2_), channel_id=1, source_target_pairs={{2,0},{4,2},{6,4},{8,6},{10,8},{12,10},{14,12},{16,14},{18,16},{20... | collective-permute-start | bytes 1572872 | tf_op jit(solution)/shard_map/ppermute | solution.py:195
  36.0 2.6 %collective-permute-start.3 = (bf16[2,256,512]{2,1,0:T(8,128)(2,1)S(1)}, bf16[2,256,512]{2,1,0:T(8,128)(2,1)}, u32[]{:S(2)}, u32[]{:S(2)}) collective-permute-start(bf16[2,256,512]{2,1,0:T(8,128)(2,1)S(1)} %pad_maximum_fusion.1.rest_2_), channel_id=1, source_target_pairs={{0,2},{2,4},{4,6},{6,8},{8,10},{10,12},{12,14},{14,16},{16,18},{18... | collective-permute-start | bytes 1572872 | tf_op jit(solution)/shard_map/ppermute | solution.py:195
  38.7 0.0 collective-permute-done
  38.7 3.6 %collective-permute-start.2 = (bf16[2,256,512]{2,1,0:T(8,128)(2,1)S(1)}, bf16[2,256,512]{2,1,0:T(8,128)(2,1)}, u32[]{:S(2)}, u32[]{:S(2)}) collective-permute-start(bf16[2,256,512]{2,1,0:T(8,128)(2,1)S(1)} %pad_maximum_fusion.1.rest_2_), channel_id=1, source_target_pairs={{0,4},{2,6},{4,8},{6,10},{8,12},{10,14},{12,16},{14,18},{16,20},{1... | collective-permute-start | bytes 1572872 | tf_op jit(solution)/shard_map/ppermute | solution.py:195
  42.3 0.1 select_reduce_fusion.1
  42.4 0.6 reduce_max.19
  43.1 0.6 reduce_min.18
  43.7 1.4 pad_add_fusion.1.info
  45.1 0.9 pad_maximum_fusion.4.query
  46.0 12.6 %collective-permute-done.5.rest_4_ = bf16[2,256,512]{2,1,0:T(8,128)(2,1)S(1)} collective-permute-done((bf16[2,256,512]{2,1,0:T(8,128)(2,1)S(1)}, bf16[2,256,512]{2,1,0:T(8,128)(2,1)S(1)}, u32[]{:S(2)}, u32[]{:S(2)}) %collective-permute-start.5) | collective-permute-done | bytes 524320 | tf_op jit(solution)/shard_map/ppermute | solution.py:195
  58.6 13.4 %collective-permute-done.4.rest_3_ = bf16[2,256,512]{2,1,0:T(8,128)(2,1)} collective-permute-done((bf16[2,256,512]{2,1,0:T(8,128)(2,1)S(1)}, bf16[2,256,512]{2,1,0:T(8,128)(2,1)}, u32[]{:S(2)}, u32[]{:S(2)}) %collective-permute-start.4) | collective-permute-done | bytes 524320 | tf_op jit(solution)/shard_map/ppermute | solution.py:195
  72.1 0.0 collective-permute-done.3.rest_1_
  72.1 5.2 %collective-permute-done.2.rest_0_ = bf16[2,256,512]{2,1,0:T(8,128)(2,1)} collective-permute-done((bf16[2,256,512]{2,1,0:T(8,128)(2,1)S(1)}, bf16[2,256,512]{2,1,0:T(8,128)(2,1)}, u32[]{:S(2)}, u32[]{:S(2)}) %collective-permute-start.2) | collective-permute-done | bytes 524320 | tf_op jit(solution)/shard_map/ppermute | solution.py:195
  77.3 8.4 %attended.1 = (bf16[256,512]{1,0:T(8,128)(2,1)S(1)}, f32[4,1,256]{2,1,0:T(1,128)S(1)}) custom-call(s32[4]{0:T(128)S(1)} %pad_add_fusion.1.info, s32[2,256]{1,0:T(2,128)S(1)} %pad_add_fusion.spans, bf16[256,512]{1,0:T(8,128)(2,1)S(1)} %pad_maximum_fusion.4.query, bf16[2,256,512]{2,1,0:T(8,128)(2,1)} %collective-permute-done.2.rest_0_, ...), custom_call_target="tpu_custom_call" | custom-call | flops 671088640 | bytes 4194304 | tf_op jit(solution)/shard_map/attended/pallas_call | solution.py:134
  85.7 0.0 collective-permute-done.6
  85.7 3.3 %convolution_convert_fusion = bf16[2048,512]{1,0:T(8,128)(2,1)} fusion(bf16[256,512]{1,0:T(8,128)(2,1)S(1)} %get-tuple-element.12.attended, bf16[128,2048]{1,0:T(8,128)(2,1)} %collective-permute-done.6, bf16[128,2048]{1,0:T(8,128)(2,1)} %bitcast.10), kind=kOutput, calls=%fused_computation | convolution fusion | flops 540016640 | bytes 3407872 | tf_op jit(solution)/shard_map/dot_general | solution.py:31
  89.0 0.7 copy-done.4
  89.7 0.0 all-to-all-done.1
  89.7 15.3 %all-to-all-start.2 = ((bf16[16,128,512]{2,1,0:T(8,128)(2,1)}), bf16[16,128,512]{2,1,0:T(8,128)(2,1)}, u32[]{:S(2)}, u32[]{:S(2)}) async-start(bf16[16,128,512]{2,1,0:T(8,128)(2,1)} %bitcast.35), calls=%async_computation.2 | async-start | bytes 4194304 | tf_op jit(solution)/shard_map/all_to_all | solution.py:246
  105.0 1.3 pad_maximum_fusion.out_grad
  106.3 0.0 copy-done.5
  106.4 11.6 %gradients.1 = (bf16[256,512]{1,0:T(8,128)(2,1)S(1)}, bf16[2,256,512]{2,1,0:T(8,128)(2,1)}, bf16[2,256,512]{2,1,0:T(8,128)(2,1)}, f32[2,256,512]{2,1,0:T(8,128)S...) custom-call(s32[4]{0:T(128)S(1)} %pad_add_fusion.1.info, s32[2,256]{1,0:T(2,128)S(1)} %pad_add_fusion.spans, ...), custom_call_target="tpu_custom_call" | custom-call | flops 1677721600 | bytes 8388608 | tf_op jit(solution)/shard_map/gradients/pallas_call | solution.py:159
  118.0 1.0 copy-done
  118.9 0.7 copy-done.2
  119.6 2.0 %collective-permute-start.7 = (bf16[2,256,512]{2,1,0:T(8,128)(2,1)}, bf16[2,256,512]{2,1,0:T(8,128)(2,1)S(1)}, u32[]{:S(2)}, u32[]{:S(2)}) collective-permute-start(bf16[2,256,512]{2,1,0:T(8,128)(2,1)} %get-tuple-element.16), channel_id=1, source_target_pairs={{4,0},{6,2},{8,4},{10,6},{12,8},{14,10},{16,12},{18,14},{20,16},{2... | collective-permute-start | bytes 1572872 | tf_op jit(solution)/shard_map/ppermute | solution.py:195
  121.7 3.9 %collective-permute-start.8 = (bf16[2,256,512]{2,1,0:T(8,128)(2,1)}, bf16[2,256,512]{2,1,0:T(8,128)(2,1)S(1)}, u32[]{:S(2)}, u32[]{:S(2)}) collective-permute-start(bf16[2,256,512]{2,1,0:T(8,128)(2,1)} %get-tuple-element.17), channel_id=1, source_target_pairs={{2,0},{4,2},{6,4},{8,6},{10,8},{12,10},{14,12},{16,14},{18,16},{20... | collective-permute-start | bytes 1572872 | tf_op jit(solution)/shard_map/ppermute | solution.py:195
  125.6 11.4 %collective-permute-start.9 = (bf16[2,256,512]{2,1,0:T(8,128)(2,1)}, bf16[2,256,512]{2,1,0:T(8,128)(2,1)S(1)}, u32[]{:S(2)}, u32[]{:S(2)}) collective-permute-start(bf16[2,256,512]{2,1,0:T(8,128)(2,1)} %get-tuple-element.18), channel_id=1, source_target_pairs={{0,2},{2,4},{4,6},{6,8},{8,10},{10,12},{12,14},{14,16},{16,18},{18... | collective-permute-start | bytes 1572872 | tf_op jit(solution)/shard_map/ppermute | solution.py:195
  137.1 4.3 %collective-permute-start.10 = (bf16[2,256,512]{2,1,0:T(8,128)(2,1)}, bf16[2,256,512]{2,1,0:T(8,128)(2,1)}, u32[]{:S(2)}, u32[]{:S(2)}) collective-permute-start(bf16[2,256,512]{2,1,0:T(8,128)(2,1)} %get-tuple-element.19), channel_id=1, source_target_pairs={{0,4},{2,6},{4,8},{6,10},{8,12},{10,14},{12,16},{14,18},{16,20},{1... | collective-permute-start | bytes 1572872 | tf_op jit(solution)/shard_map/ppermute | solution.py:195
  141.3 0.0 all-to-all-done.2
  141.3 2.6 %reduce_sum.21 = bf16[128,512]{1,0:T(8,128)(2,1)} reduce(bf16[16,128,512]{2,1,0:T(8,128)(2,1)} %all-to-all-done.2, bf16[]{:T(256)} %constant.62.clone.1), dimensions={0}, to_apply=%region_5.6 | reduce | flops 983040 | bytes 2228226 | tf_op jit(solution)/shard_map/reduce_sum | solution.py:247
  143.9 8.1 %all-to-all-start.3 = ((bf16[16,8,512]{2,1,0:T(8,128)(2,1)}), bf16[16,8,512]{2,1,0:T(8,128)(2,1)S(1)}, u32[]{:S(2)}, u32[]{:S(2)}) async-start(bf16[16,8,512]{2,1,0:T(8,128)(2,1)} %bitcast.18), calls=%async_computation.3 | async-start | bytes 262144 | tf_op jit(solution)/shard_map/all_to_all | solution.py:249
  152.0 0.0 collective-permute-done.7
  152.0 6.9 %collective-permute-done.8 = bf16[2,256,512]{2,1,0:T(8,128)(2,1)S(1)} collective-permute-done((bf16[2,256,512]{2,1,0:T(8,128)(2,1)}, bf16[2,256,512]{2,1,0:T(8,128)(2,1)S(1)}, u32[]{:S(2)}, u32[]{:S(2)}) %collective-permute-start.8) | collective-permute-done | bytes 524320 | tf_op jit(solution)/shard_map/ppermute | solution.py:195
  158.9 0.0 collective-permute-done.9
  158.9 10.8 %collective-permute-done.10 = bf16[2,256,512]{2,1,0:T(8,128)(2,1)} collective-permute-done((bf16[2,256,512]{2,1,0:T(8,128)(2,1)}, bf16[2,256,512]{2,1,0:T(8,128)(2,1)}, u32[]{:S(2)}, u32[]{:S(2)}) %collective-permute-start.10) | collective-permute-done | bytes 524320 | tf_op jit(solution)/shard_map/ppermute | solution.py:195
  169.7 0.0 copy-done.6
  169.7 0.0 copy-done.1
  169.7 1.6 add_convert_fusion
  171.3 0.0 copy-done.3
  171.3 4.4 %collective-permute-start.11 = (bf16[3,128,512]{2,1,0:T(8,128)(2,1)S(1)}, bf16[3,128,512]{2,1,0:T(8,128)(2,1)S(1)}, u32[]{:S(2)}, u32[]{:S(2)}) collective-permute-start(bf16[3,128,512]{2,1,0:T(8,128)(2,1)S(1)} %pad_maximum_fusion.2), channel_id=1, source_target_pairs={{0,1},{1,0},{2,3},{3,2},{4,5},{5,4},{6,7},{7,6},{8,9},{9,8},{10,11... | collective-permute-start | bytes 1179656 | tf_op jit(solution)/shard_map/ppermute | solution.py:262
  175.8 1.2 all-to-all-done.3
  177.0 0.6 pad_maximum_fusion.5
  177.6 0.0 collective-permute-done.11
  177.6 0.1 broadcast_select_fusion
  177.7 0.9 pad_maximum_fusion.3
  (22 shorter events, 0.3 us)
Async XLA Ops:
  21.4 6.9 %copy-start.7 = (bf16[1,128,1024]{2,1,0:T(8,128)(2,1)S(1)}, bf16[1,128,1024]{2,1,0:T(8,128)(2,1)}, u32[]{:S(2)}) copy-start(bf16[1,128,1024]{2,1,0:T(8,128)(2,1)} %param.7) | copy-start | bytes 786436
  21.4 7.0 %copy-start.8 = (bf16[1,128,1024]{2,1,0:T(8,128)(2,1)S(1)}, bf16[1,128,1024]{2,1,0:T(8,128)(2,1)}, u32[]{:S(2)}) copy-start(bf16[1,128,1024]{2,1,0:T(8,128)(2,1)} %param.8) | copy-start | bytes 786436
  21.4 68.2 %all-to-all-start.1 = ((bf16[16,512,128]{2,1,0:T(8,128)(2,1)}), bf16[16,512,128]{2,1,0:T(8,128)(2,1)S(1)}, u32[]{:S(2)}, u32[]{:S(2)}) async-start(bf16[16,512,128]{2,1,0:T(8,128)(2,1)} %broadcast_in_dim.46), calls=%async_computation.1 | async-start | bytes 4194304 | tf_op jit(solution)/shard_map/all_to_all | solution.py:226
  28.3 0.9 copy-start.9
  28.4 2.1 %copy-start.10 = (s32[1,32]{1,0:T(1,128)S(1)}, s32[1,32]{1,0:T(1,128)}, u32[]{:S(2)}) copy-start(s32[1,32]{1,0:T(1,128)} %param.11) | copy-start | bytes 388
  28.5 2.3 %collective-permute-start.1 = (bf16[2,128,512]{2,1,0:T(8,128)(2,1)S(1)}, bf16[2,128,512]{2,1,0:T(8,128)(2,1)S(1)}, u32[]{:S(2)}, u32[]{:S(2)}) collective-permute-start(bf16[2,128,512]{2,1,0:T(8,128)(2,1)S(1)} %get-tuple-element.28), channel_id=1, source_target_pairs={{0,1},{1,0},{2,3},{3,2},{4,5},{5,4},{6,7},{7,6},{8,9},{9,8},{10,11... | collective-permute-start | bytes 786440 | tf_op jit(solution)/shard_map/ppermute | solution.py:212
  30.0 8.7 %collective-permute-start = (bf16[128,512]{1,0:T(8,128)(2,1)}, bf16[128,512]{1,0:T(8,128)(2,1)}, u32[]{:S(2)}, u32[]{:S(2)}) collective-permute-start(bf16[128,512]{1,0:T(8,128)(2,1)} %get-tuple-element.30), channel_id=1, source_target_pairs={{0,1},{1,0},{2,3},{3,2},{4,5},{5,4},{6,7},{7,6},{8,9},{9,8},{10,11... | collective-permute-start | bytes 393224 | tf_op jit(solution)/shard_map/ppermute | solution.py:215
  30.2 55.5 %collective-permute-start.6 = (bf16[128,2048]{1,0:T(8,128)(2,1)}, bf16[128,2048]{1,0:T(8,128)(2,1)}, u32[]{:S(2)}, u32[]{:S(2)}) collective-permute-start(bf16[128,2048]{1,0:T(8,128)(2,1)} %bitcast.10), channel_id=1, source_target_pairs={{0,1},{1,0},{2,3},{3,2},{4,5},{5,4},{6,7},{7,6},{8,9},{9,8},{10,11... | collective-permute-start | bytes 1572872 | tf_op jit(solution)/shard_map/ppermute | solution.py:216
  30.8 27.8 %collective-permute-start.5 = (bf16[2,256,512]{2,1,0:T(8,128)(2,1)S(1)}, bf16[2,256,512]{2,1,0:T(8,128)(2,1)S(1)}, u32[]{:S(2)}, u32[]{:S(2)}) collective-permute-start(bf16[2,256,512]{2,1,0:T(8,128)(2,1)S(1)} %pad_maximum_fusion.1.rest_2_), channel_id=1, source_target_pairs={{4,0},{6,2},{8,4},{10,6},{12,8},{14,10},{16,12},{18,14},{20,16},{2... | collective-permute-start | bytes 1572872 | tf_op jit(solution)/shard_map/ppermute | solution.py:195
  33.4 38.7 %collective-permute-start.4 = (bf16[2,256,512]{2,1,0:T(8,128)(2,1)S(1)}, bf16[2,256,512]{2,1,0:T(8,128)(2,1)}, u32[]{:S(2)}, u32[]{:S(2)}) collective-permute-start(bf16[2,256,512]{2,1,0:T(8,128)(2,1)S(1)} %pad_maximum_fusion.1.rest_2_), channel_id=1, source_target_pairs={{2,0},{4,2},{6,4},{8,6},{10,8},{12,10},{14,12},{16,14},{18,16},{20... | collective-permute-start | bytes 1572872 | tf_op jit(solution)/shard_map/ppermute | solution.py:195
  36.0 36.0 %collective-permute-start.3 = (bf16[2,256,512]{2,1,0:T(8,128)(2,1)S(1)}, bf16[2,256,512]{2,1,0:T(8,128)(2,1)}, u32[]{:S(2)}, u32[]{:S(2)}) collective-permute-start(bf16[2,256,512]{2,1,0:T(8,128)(2,1)S(1)} %pad_maximum_fusion.1.rest_2_), channel_id=1, source_target_pairs={{0,2},{2,4},{4,6},{6,8},{8,10},{10,12},{12,14},{14,16},{16,18},{18... | collective-permute-start | bytes 1572872 | tf_op jit(solution)/shard_map/ppermute | solution.py:195
  38.7 38.6 %collective-permute-start.2 = (bf16[2,256,512]{2,1,0:T(8,128)(2,1)S(1)}, bf16[2,256,512]{2,1,0:T(8,128)(2,1)}, u32[]{:S(2)}, u32[]{:S(2)}) collective-permute-start(bf16[2,256,512]{2,1,0:T(8,128)(2,1)S(1)} %pad_maximum_fusion.1.rest_2_), channel_id=1, source_target_pairs={{0,4},{2,6},{4,8},{6,10},{8,12},{10,14},{12,16},{14,18},{16,20},{1... | collective-permute-start | bytes 1572872 | tf_op jit(solution)/shard_map/ppermute | solution.py:195
  89.0 0.7 copy-start.4
  89.7 51.7 %all-to-all-start.2 = ((bf16[16,128,512]{2,1,0:T(8,128)(2,1)}), bf16[16,128,512]{2,1,0:T(8,128)(2,1)}, u32[]{:S(2)}, u32[]{:S(2)}) async-start(bf16[16,128,512]{2,1,0:T(8,128)(2,1)} %bitcast.35), calls=%async_computation.2 | async-start | bytes 4194304 | tf_op jit(solution)/shard_map/all_to_all | solution.py:246
  105.0 1.4 copy-start.5
  118.0 1.0 copy-start
  118.9 0.7 copy-start.2
  119.6 50.1 %copy-start.1 = (f32[2,256,512]{2,1,0:T(8,128)S(1)}, f32[2,256,512]{2,1,0:T(8,128)}, u32[]{:S(2)}) copy-start(f32[2,256,512]{2,1,0:T(8,128)} %copy-done) | copy-start | bytes 3145732
  119.6 32.4 %collective-permute-start.7 = (bf16[2,256,512]{2,1,0:T(8,128)(2,1)}, bf16[2,256,512]{2,1,0:T(8,128)(2,1)S(1)}, u32[]{:S(2)}, u32[]{:S(2)}) collective-permute-start(bf16[2,256,512]{2,1,0:T(8,128)(2,1)} %get-tuple-element.16), channel_id=1, source_target_pairs={{4,0},{6,2},{8,4},{10,6},{12,8},{14,10},{16,12},{18,14},{20,16},{2... | collective-permute-start | bytes 1572872 | tf_op jit(solution)/shard_map/ppermute | solution.py:195
  121.7 37.2 %collective-permute-start.8 = (bf16[2,256,512]{2,1,0:T(8,128)(2,1)}, bf16[2,256,512]{2,1,0:T(8,128)(2,1)S(1)}, u32[]{:S(2)}, u32[]{:S(2)}) collective-permute-start(bf16[2,256,512]{2,1,0:T(8,128)(2,1)} %get-tuple-element.17), channel_id=1, source_target_pairs={{2,0},{4,2},{6,4},{8,6},{10,8},{12,10},{14,12},{16,14},{18,16},{20... | collective-permute-start | bytes 1572872 | tf_op jit(solution)/shard_map/ppermute | solution.py:195
  125.6 33.3 %collective-permute-start.9 = (bf16[2,256,512]{2,1,0:T(8,128)(2,1)}, bf16[2,256,512]{2,1,0:T(8,128)(2,1)S(1)}, u32[]{:S(2)}, u32[]{:S(2)}) collective-permute-start(bf16[2,256,512]{2,1,0:T(8,128)(2,1)} %get-tuple-element.18), channel_id=1, source_target_pairs={{0,2},{2,4},{4,6},{6,8},{8,10},{10,12},{12,14},{14,16},{16,18},{18... | collective-permute-start | bytes 1572872 | tf_op jit(solution)/shard_map/ppermute | solution.py:195
  137.1 32.7 %collective-permute-start.10 = (bf16[2,256,512]{2,1,0:T(8,128)(2,1)}, bf16[2,256,512]{2,1,0:T(8,128)(2,1)}, u32[]{:S(2)}, u32[]{:S(2)}) collective-permute-start(bf16[2,256,512]{2,1,0:T(8,128)(2,1)} %get-tuple-element.19), channel_id=1, source_target_pairs={{0,4},{2,6},{4,8},{6,10},{8,12},{10,14},{12,16},{14,18},{16,20},{1... | collective-permute-start | bytes 1572872 | tf_op jit(solution)/shard_map/ppermute | solution.py:195
  143.9 27.4 %copy-start.3 = (bf16[256,512]{1,0:T(8,128)(2,1)S(1)}, bf16[256,512]{1,0:T(8,128)(2,1)}, u32[]{:S(2)}) copy-start(bf16[256,512]{1,0:T(8,128)(2,1)} %copy-done.2) | copy-start | bytes 786436
  143.9 33.0 %all-to-all-start.3 = ((bf16[16,8,512]{2,1,0:T(8,128)(2,1)}), bf16[16,8,512]{2,1,0:T(8,128)(2,1)S(1)}, u32[]{:S(2)}, u32[]{:S(2)}) async-start(bf16[16,8,512]{2,1,0:T(8,128)(2,1)} %bitcast.18), calls=%async_computation.3 | async-start | bytes 262144 | tf_op jit(solution)/shard_map/all_to_all | solution.py:249
  158.9 10.8 %copy-start.6 = (bf16[2,256,512]{2,1,0:T(8,128)(2,1)}, bf16[2,256,512]{2,1,0:T(8,128)(2,1)S(1)}, u32[]{:S(2)}) copy-start(bf16[2,256,512]{2,1,0:T(8,128)(2,1)S(1)} %collective-permute-done.9) | copy-start | bytes 1572868
  171.3 6.3 %collective-permute-start.11 = (bf16[3,128,512]{2,1,0:T(8,128)(2,1)S(1)}, bf16[3,128,512]{2,1,0:T(8,128)(2,1)S(1)}, u32[]{:S(2)}, u32[]{:S(2)}) collective-permute-start(bf16[3,128,512]{2,1,0:T(8,128)(2,1)S(1)} %pad_maximum_fusion.2), channel_id=1, source_target_pairs={{0,1},{1,0},{2,3},{3,2},{4,5},{5,4},{6,7},{7,6},{8,9},{9,8},{10,11... | collective-permute-start | bytes 1179656 | tf_op jit(solution)/shard_map/ppermute | solution.py:262

commit v2 on v1

v2 whole, which is shorter than its diff:
```python
import math

import jax
import jax.numpy as jnp
from jax import lax
from jax.experimental import pallas as pl
from jax.experimental.pallas import tpu as pltpu
from jax.sharding import Mesh, PartitionSpec as P

HEADS = 8
HEAD = 128
TOK = 128
CHIP = 2 * TOK
HALF = HEADS * HEAD // 2
REACH = 2
OFFSETS = tuple(range(-REACH, REACH + 1))
SUBS = 2 * len(OFFSETS)
SCALE = 1.0 / math.sqrt(HEAD)
LOG2E = math.log2(math.e)
PER = 2
SWAP = [(0, 1), (1, 0)]


def nt(a, b):
    return lax.dot_general(a, b, (((1,), (1,)), ((), ())), preferred_element_type=jnp.float32)


def nn(a, b):
    return lax.dot_general(a, b, (((1,), (0,)), ((), ())), preferred_element_type=jnp.float32)


def tn(a, b):
    return lax.dot_general(a, b, (((0,), (0,)), ((), ())), preferred_element_type=jnp.float32)


def block_base(info, sub):
    own = info[0]
    core = info[1]
    parity = core if sub % 2 == 0 else 1 - core
    return own + OFFSETS[sub // 2] * CHIP + parity * TOK


def needed(info, base):
    return jnp.logical_and(base < info[3], base + TOK > info[2])


def block_mask(spans, base):
    position = base + lax.broadcasted_iota(jnp.int32, (TOK, CHIP), 0)
    return jnp.logical_and(position >= spans[0:1, :], position < spans[1:2, :])


def masked_scores(keys, query, taken):
    return jnp.where(taken, nt(keys, query) * (SCALE * LOG2E), -1e30)


def by_eights(block):
    return block.reshape(TOK // 8, 8, CHIP)


def forward_kernel(info, spans, query, *rest):
    windows = rest[: len(OFFSETS)]
    attended, log_norm, scores, peak, total, acc = rest[len(OFFSETS) :]
    peak[...] = jnp.full((PER, 8, CHIP), -1e30, jnp.float32)
    total[...] = jnp.zeros((PER, 8, CHIP), jnp.float32)
    acc[...] = jnp.zeros((PER, HEAD, CHIP), jnp.float32)
    heads = [(h, pl.ds(h * HEAD, HEAD)) for h in range(PER)]
    for sub in range(SUBS):
        base = block_base(info, sub)
        rows = pl.ds(sub % 2 * TOK, TOK)

        @pl.when(needed(info, base))
        def _(sub=sub, base=base, rows=rows):
            taken = block_mask(spans, base)
            for h, cols in heads:
                block = masked_scores(windows[sub // 2][0, rows, cols], query[:, cols], taken)
                scores[h, sub] = block
                peak[h] = jnp.maximum(peak[h], jnp.max(by_eights(block), axis=0))

    for h, cols in heads:
        peak[h] = jnp.broadcast_to(jnp.max(peak[h], axis=0, keepdims=True), (8, CHIP))
    for sub in range(SUBS):
        base = block_base(info, sub)
        rows = pl.ds(sub % 2 * TOK, TOK)

        @pl.when(needed(info, base))
        def _(sub=sub, rows=rows):
            for h, cols in heads:
                weights = jnp.exp2(scores[h, sub] - peak[h, 0:1, :])
                total[h] += jnp.sum(by_eights(weights), axis=0)
                acc[h] += tn(windows[sub // 2][1, rows, cols], weights.astype(jnp.bfloat16))

    for h, cols in heads:
        row_total = jnp.sum(total[h], axis=0, keepdims=True)
        attended[:, cols] = (acc[h] * (1.0 / row_total)).T.astype(jnp.bfloat16)
        log_norm[h] = peak[h, 0:1, :] + jnp.log(row_total) * LOG2E


def backward_kernel(info, spans, query, attended, log_norm, out_grad, weight, *rest):
    windows = rest[: len(OFFSETS)]
    query_grad = rest[len(OFFSETS)]
    terms = rest[len(OFFSETS) + 1 : 2 * len(OFFSETS) + 1]
    grad, row_delta, acc = rest[2 * len(OFFSETS) + 1 :]
    heads = [(h, pl.ds(h * HEAD, HEAD)) for h in range(PER)]
    acc[...] = jnp.zeros((PER, HEAD, CHIP), jnp.float32)
    for h, cols in heads:
        grad[h] = nn(out_grad[...], weight[h]).astype(jnp.bfloat16)
        product = grad[h].astype(jnp.float32) * attended[:, cols].astype(jnp.float32)
        row_delta[h] = jnp.sum(product.T, axis=0, keepdims=True)
    for sub in range(SUBS):
        base = block_base(info, sub)
        rows = pl.ds(sub % 2 * TOK, TOK)
        touched = needed(info, base)
        term = terms[sub // 2]

        @pl.when(touched)
        def _(sub=sub, base=base, rows=rows, term=term):
            taken = block_mask(spans, base)
            for h, cols in heads:
                keys = windows[sub // 2][0, rows, cols]
                values = windows[sub // 2][1, rows, cols]
                probs = jnp.exp2(masked_scores(keys, query[:, cols], taken) - log_norm[h])
                dprobs = nt(values, grad[h])
                dscores = (probs * (dprobs - row_delta[h])).astype(jnp.bfloat16)
                acc[h] += tn(keys, dscores)
                term[0, rows, cols] = (SCALE * nn(dscores, query[:, cols])).astype(term.dtype)
                term[1, rows, cols] = nn(probs.astype(jnp.bfloat16), grad[h]).astype(term.dtype)

        @pl.when(jnp.logical_not(touched))
        def _(rows=rows, term=term):
            term[:, rows, :] = jnp.zeros((2, TOK, PER * HEAD), term.dtype)

    for h, cols in heads:
        query_grad[:, cols] = (SCALE * acc[h]).T.astype(jnp.bfloat16)


def smem():
    return pl.BlockSpec(memory_space=pltpu.SMEM)


def whole(shape):
    return pl.BlockSpec(shape, lambda h: (0,) * len(shape))


def head_columns(rows):
    return pl.BlockSpec((rows, PER * HEAD), lambda h: (0, h))


def head_rows(*shape):
    return pl.BlockSpec((PER,) + shape, lambda h: (h, 0, 0))


def window_spec():
    return pl.BlockSpec((2, CHIP, PER * HEAD), lambda h: (0, 0, h))


def forward(info, spans, query, windows):
    return pl.pallas_call(
        forward_kernel,
        grid=(HEADS // 2 // PER,),
        in_specs=[smem(), whole((2, CHIP)), head_columns(CHIP)] + [window_spec() for _ in OFFSETS],
        out_specs=[head_columns(CHIP), head_rows(1, CHIP)],
        out_shape=[
            jax.ShapeDtypeStruct((CHIP, HALF), jnp.bfloat16),
            jax.ShapeDtypeStruct((HEADS // 2, 1, CHIP), jnp.float32),
        ],
        scratch_shapes=[
            pltpu.VMEM((PER, SUBS, TOK, CHIP), jnp.float32),
            pltpu.VMEM((PER, 8, CHIP), jnp.float32),
            pltpu.VMEM((PER, 8, CHIP), jnp.float32),
            pltpu.VMEM((PER, HEAD, CHIP), jnp.float32),
        ],
        compiler_params=pltpu.CompilerParams(vmem_limit_bytes=32 * 1024 * 1024),
        cost_estimate=pl.CostEstimate(
            flops=4 * HALF * CHIP * SUBS * TOK, bytes_accessed=8 * 1024 * 1024, transcendentals=0
        ),
        name="attended",
    )(info, spans, query, *windows)


def backward(info, spans, query, attended, log_norm, out_grad, weight, windows):
    features = out_grad.shape[1]
    return pl.pallas_call(
        backward_kernel,
        grid=(HEADS // 2 // PER,),
        in_specs=[
            smem(),
            whole((2, CHIP)),
            head_columns(CHIP),
            head_columns(CHIP),
            head_rows(1, CHIP),
            whole((CHIP, features)),
            head_rows(features, HEAD),
        ]
        + [window_spec() for _ in OFFSETS],
        out_specs=[head_columns(CHIP)] + [window_spec() for _ in OFFSETS],
        out_shape=[jax.ShapeDtypeStruct((CHIP, HALF), jnp.bfloat16)]
        + [
            jax.ShapeDtypeStruct((2, CHIP, HALF), jnp.float32 if abs(o) < REACH else jnp.bfloat16)
            for o in OFFSETS
        ],
        scratch_shapes=[
            pltpu.VMEM((PER, CHIP, HEAD), jnp.bfloat16),
            pltpu.VMEM((PER, 1, CHIP), jnp.float32),
            pltpu.VMEM((PER, HEAD, CHIP), jnp.float32),
        ],
        compiler_params=pltpu.CompilerParams(vmem_limit_bytes=32 * 1024 * 1024),
        cost_estimate=pl.CostEstimate(
            flops=10 * HALF * CHIP * SUBS * TOK,
            bytes_accessed=16 * 1024 * 1024,
            transcendentals=0,
        ),
        name="gradients",
    )(info, spans, query, attended, log_norm, out_grad, weight, *windows)


def to_chip(block, distance):
    chips = lax.axis_size("y") * lax.axis_size("z")
    route = [(i, i + distance) for i in range(chips) if 0 <= i + distance < chips]
    return lax.ppermute(block, ("y", "z"), route)


def halves(core, matrix):
    own = lax.dynamic_slice_in_dim(matrix, core * HALF, HALF, matrix.ndim - 1)
    other = lax.dynamic_slice_in_dim(matrix, (1 - core) * HALF, HALF, matrix.ndim - 1)
    return own, other


def on_device(query, keys, values, out_grad, out_weight, lengths):
    core = lax.axis_index("c")
    along_x = lax.axis_index("x")
    chip = lax.axis_index("y") * lax.axis_size("z") + lax.axis_index("z")
    size_x, size_y, size_z = (lax.axis_size(a) for a in ("x", "y", "z"))
    features = out_grad.shape[2]

    own_kv, other_kv = halves(core, jnp.stack([keys[0], values[0]]))
    chip_kv = jnp.concatenate([own_kv, lax.ppermute(other_kv, "c", SWAP)], axis=1)
    chip_kv, out_weight = lax.optimization_barrier((chip_kv, out_weight))
    below = to_chip(chip_kv, 1)
    above = to_chip(chip_kv, -1)
    windows = [to_chip(below, 1), below, chip_kv, above, to_chip(above, -1)]
    own_query, other_query = halves(core, query[0])
    chip_query = jnp.concatenate([own_query, lax.ppermute(other_query, "c", SWAP)], axis=0)
    chip_grad = jnp.concatenate([out_grad[0], lax.ppermute(out_grad[0], "c", SWAP)], axis=0)

    rows = out_weight.shape[0]
    piece = lax.dynamic_index_in_dim(
        out_weight.reshape(rows, 2, size_x, HEAD), along_x, 2, keepdims=False
    )
    piece = jnp.broadcast_to(piece.transpose(1, 0, 2)[None], (size_z, 2, rows, HEAD))
    piece = lax.all_to_all(piece.reshape(2 * size_z, rows, HEAD), ("z", "c"), 0, 0)
    piece = piece.reshape(1, 2 * size_z * rows, HEAD)
    piece = jnp.broadcast_to(piece, (size_x * size_y,) + piece.shape[1:])
    weight = lax.all_to_all(piece, ("x", "y"), 0, 0).reshape(size_x, features, HEAD)

    ends = jnp.cumsum(lengths[0])
    starts = ends - lengths[0]
    place = jnp.arange(CHIP, dtype=jnp.int32)
    first = chip * CHIP
    positions = first + jnp.where(core == 0, place, (place + TOK) % CHIP)
    image_start = jnp.max(
        jnp.where(starts[:, None] <= positions[None, :], starts[:, None], 0), axis=0
    )
    image_end = jnp.min(
        jnp.where(ends[:, None] > positions[None, :], ends[:, None], jnp.int32(2**30)), axis=0
    )
    spans = jnp.stack([image_start, image_end])
    info = jnp.stack([first, core, jnp.min(image_start), jnp.max(image_end)]).astype(jnp.int32)

    attended, log_norm = forward(info, spans, chip_query, windows)

    partial = tn(chip_grad, attended).astype(jnp.bfloat16)
    for axis, size in (("x", size_x), ("y", size_y)):
        partial = lax.all_to_all(partial.reshape(size, -1, HALF), axis, 0, 0)
        partial = jnp.sum(partial.astype(jnp.float32), axis=0).astype(jnp.bfloat16)
    partial = partial.reshape(2 * size_z, -1, HALF)
    partial = lax.all_to_all(partial, ("z", "c"), 0, 0).reshape(size_z, 2, -1, HALF)
    partial = jnp.sum(partial.astype(jnp.float32), axis=0)
    weight_grad = jnp.concatenate([partial[0], partial[1]], axis=1)

    query_grad, *terms = backward(
        info, spans, chip_query, attended, log_norm, chip_grad, weight, windows
    )
    total = terms[REACH]
    for side in (1, -1):
        passing = to_chip(terms[REACH + 2 * side], side).astype(jnp.float32)
        passing = (passing + terms[REACH + side]).astype(jnp.bfloat16)
        total = total + to_chip(passing, side).astype(jnp.float32)
    grads = jnp.concatenate([query_grad[None], total.astype(jnp.bfloat16)], axis=0)
    mine = grads[:, :TOK]
    theirs = lax.ppermute(grads[:, TOK:], "c", SWAP)
    low = jnp.where(core == 0, mine, theirs)
    high = jnp.where(core == 0, theirs, mine)
    grads = jnp.concatenate([low, high], axis=2)
    return (grads[0:1], grads[1:2], grads[2:3], weight_grad)


def solution(mesh):
    fine = Mesh(mesh.devices.reshape(4, 4, 8, 2), ("x", "y", "z", "c"))
    tokens = P("x", ("y", "z", "c"), None)
    return jax.shard_map(
        on_device,
        mesh=fine,
        in_specs=(tokens, tokens, tokens, tokens, P(("y", "z", "c"), None), P("x", None)),
        out_specs=(tokens, tokens, tokens, P(("x", "y", "z", "c"), None)),
        check_vma=False,
    )
```

time: 180 us -> 168 us (0.933)
  starting transfers between devices: 68.7 us -> 56.3 us
  blocking collectives: 18.1 us -> 27.9 us
  waiting for transfers between devices: 50.2 us -> 41.3 us
  Pallas kernels: 20 us -> 17.4 us
    ppermute x8, waiting for transfers between devices: 49 us -> 31.5 us  [to_chip(): return lax.ppermute(block, ('y', 'z'), route)]
    all_to_all x0 -> x1, blocking collectives: none -> 10.1 us  [on_device(): partial = lax.all_to_all(partial.reshape(size, -1, HALF), axis, 0, 0)]
    all_to_all x1, starting transfers between devices: 15.3 us -> 6.74 us  [on_device(): partial = lax.all_to_all(partial.reshape(size, -1, HALF), axis, 0, 0)]
    all_to_all x1, waiting for transfers between devices: 1.18 us -> 8.68 us  [on_device(): lax.all_to_all(partial, ('z', 'c'), 0, 0).reshape(size_z, 2, -1, HALF)]
    ppermute x8, starting transfers between devices: 33.1 us -> 28.4 us  [to_chip(): return lax.ppermute(block, ('y', 'z'), route)]
    all_to_all x1, starting transfers between devices: 8.07 us -> 12.5 us  [on_device(): lax.all_to_all(partial, ('z', 'c'), 0, 0).reshape(size_z, 2, -1, HALF)]
    ppermute x1, starting transfers between devices: 4.44 us -> 0.19 us  [on_device(): theirs = lax.ppermute(grads[:, TOK:], 'c', SWAP)]
    pallas_call x2, Pallas kernels: 20 us -> 17.4 us  [the longest x1 10.9 us: backward(): pl.pallas_call(backward_kernel, grid=(HEADS // 2 // PER,), in_specs=[smem...]
  transfers between devices with their start and end apart: 15 -> 15, of which waited for: 6 -> 7; matrix products, arithmetic and copies ran while one was open for 8% -> 9% of each run, Pallas kernels for 11% -> 11%
where the time goes in v2:
time: 168 us; the launch traced here: 165 us
  starting transfers between devices  56.3 us (34%)
  waiting for transfers between devices  41.3 us (25%)
  blocking collectives  27.9 us (17%)
  Pallas kernels  17.4 us (10%)
  other arithmetic  12.1 us (7%)
  local copies, waits for them, and re-layouts  6.01 us (4%)
  matrix products  3.12 us (2%)
    ppermute x8, waiting for transfers between devices, to_chip(): return lax.ppermute(block, ('y', 'z'), route)  31.5 us
    ppermute x8, starting transfers between devices, to_chip(): return lax.ppermute(block, ('y', 'z'), route)  28.4 us
    all_to_all x1, blocking collectives, on_device(): lax.all_to_all(piece.reshape(2 * size_z, rows, HEAD), ('z', 'c'), 0, 0)  17.8 us
    all_to_all x1, starting transfers between devices, on_device(): lax.all_to_all(partial, ('z', 'c'), 0, 0).reshape(size_z, 2, -1, HALF)  12.5 us
    pallas_call x1, Pallas kernels, backward(): pl.pallas_call(backward_kernel, grid=(HEADS // 2 // PER,), in_specs=[smem...  10.9 us
    all_to_all x1, blocking collectives, on_device(): partial = lax.all_to_all(partial.reshape(size, -1, HALF), axis, 0, 0)  10.1 us
    all_to_all x1, waiting for transfers between devices, on_device(): lax.all_to_all(partial, ('z', 'c'), 0, 0).reshape(size_z, 2, -1, HALF)  8.68 us
    all_to_all x1, starting transfers between devices, on_device(): lax.all_to_all(piece, ('x', 'y'), 0, 0).reshape(size_x, features, HEAD)  6.91 us
  transfers between devices with their start and end apart: 15, of which 7 were waited for; matrix products, arithmetic and copies ran while one was open for 9% of the time, Pallas kernels for 11%

profile of v2, /device:TPU:13, one launch (start us, length us, event | category | flops | bytes accessed | tf_op | source)
XLA Modules:
  0.0 165.1 jit_solution(13125888620134684233)
XLA Ops:
  0.6 1.0 constant_dynamic-update-slice_fusion.1
  1.6 1.0 constant_dynamic-update-slice_fusion
  2.7 0.8 collective-permute-start.1
  3.4 1.2 collective-permute-done.1
  4.6 0.0 copy-done.9
  4.8 17.8 %all_to_all.25 = bf16[16,32,128]{2,1,0:T(8,128)(2,1)S(1)} all-to-all(bf16[16,32,128]{2,1,0:T(8,128)(2,1)S(1)} %bitcast.40), channel_id=1, replica_groups=mesh['x'=4,'y'=4,'z'=8,'c'=2] {'z','c'}, dimensions={0} | all-to-all | bytes 262144 | tf_op jit(solution)/shard_map/all_to_all | solution.py:250
  22.6 1.7 %broadcast_in_dim.46 = bf16[16,512,128]{2,1,0:T(8,128)(2,1)} broadcast(bf16[512,128]{1,0:T(8,128)(2,1)S(1)} %bitcast.38), dimensions={1,2} | broadcast | bytes 2228224 | tf_op jit(solution)/shard_map/broadcast_in_dim | solution.py:252
  24.3 6.9 %all-to-all-start.1 = ((bf16[16,512,128]{2,1,0:T(8,128)(2,1)}), bf16[16,512,128]{2,1,0:T(8,128)(2,1)S(1)}, u32[]{:S(2)}, u32[]{:S(2)}) async-start(bf16[16,512,128]{2,1,0:T(8,128)(2,1)} %broadcast_in_dim.46), calls=%async_computation.1 | async-start | bytes 4194304 | tf_op jit(solution)/shard_map/all_to_all | solution.py:253
  31.2 1.9 %collective-permute-start.4 = (bf16[2,256,512]{2,1,0:T(8,128)(2,1)S(1)}, bf16[2,256,512]{2,1,0:T(8,128)(2,1)S(1)}, u32[]{:S(2)}, u32[]{:S(2)}) collective-permute-start(bf16[2,256,512]{2,1,0:T(8,128)(2,1)S(1)} %pad_maximum_fusion.1.rest_2_), channel_id=1, source_target_pairs={{2,0},{4,2},{6,4},{8,6},{10,8},{12,10},{14,12},{16,14},{18,16},{20... | collective-permute-start | bytes 1572872 | tf_op jit(solution)/shard_map/ppermute | solution.py:219
  33.2 3.4 %collective-permute-start.2 = (bf16[2,256,512]{2,1,0:T(8,128)(2,1)S(1)}, bf16[2,256,512]{2,1,0:T(8,128)(2,1)}, u32[]{:S(2)}, u32[]{:S(2)}) collective-permute-start(bf16[2,256,512]{2,1,0:T(8,128)(2,1)S(1)} %pad_maximum_fusion.1.rest_2_), channel_id=1, source_target_pairs={{0,2},{2,4},{4,6},{6,8},{8,10},{10,12},{12,14},{14,16},{16,18},{18... | collective-permute-start | bytes 1572872 | tf_op jit(solution)/shard_map/ppermute | solution.py:219
  36.5 0.0 copy-done.7
  36.5 0.7 dynamic-slice_bitcast_fusion.1
  37.2 0.8 collective-permute-start
  38.0 0.0 collective-permute-start.6
  38.0 0.0 copy-done.10
  38.0 0.1 copy.14
  38.1 0.1 reduce-window.7
  38.2 0.1 reduce.2
  38.3 15.5 %collective-permute-done.4.rest_3_ = bf16[2,256,512]{2,1,0:T(8,128)(2,1)S(1)} collective-permute-done((bf16[2,256,512]{2,1,0:T(8,128)(2,1)S(1)}, bf16[2,256,512]{2,1,0:T(8,128)(2,1)S(1)}, u32[]{:S(2)}, u32[]{:S(2)}) %collective-permute-start.4) | collective-permute-done | bytes 524320 | tf_op jit(solution)/shard_map/ppermute | solution.py:219
  53.8 6.4 %collective-permute-start.5 = (bf16[2,256,512]{2,1,0:T(8,128)(2,1)S(1)}, bf16[2,256,512]{2,1,0:T(8,128)(2,1)}, u32[]{:S(2)}, u32[]{:S(2)}) collective-permute-start(bf16[2,256,512]{2,1,0:T(8,128)(2,1)S(1)} %collective-permute-done.4.rest_3_), channel_id=1, source_target_pairs={{2,0},{4,2},{6,4},{8,6},{10,8},{12,10},{14,12},{16,14},{18,16},{20... | collective-permute-start | bytes 1572872 | tf_op jit(solution)/shard_map/ppermute | solution.py:219
  60.2 0.4 collective-permute-done.2.rest_1_
  60.6 1.9 %collective-permute-start.3 = (bf16[2,256,512]{2,1,0:T(8,128)(2,1)}, bf16[2,256,512]{2,1,0:T(8,128)(2,1)}, u32[]{:S(2)}, u32[]{:S(2)}) collective-permute-start(bf16[2,256,512]{2,1,0:T(8,128)(2,1)} %collective-permute-done.2.rest_1_), channel_id=1, source_target_pairs={{0,2},{2,4},{4,6},{6,8},{8,10},{10,12},{12,14},{14,16},{16,18},{18... | collective-permute-start | bytes 1572872 | tf_op jit(solution)/shard_map/ppermute | solution.py:219
  62.5 0.1 select_reduce_fusion.1
  62.6 0.6 reduce_max.19
  63.3 0.7 reduce_min.18
  63.9 1.4 pad_add_fusion.1.info
  65.3 0.0 collective-permute-done
  65.3 0.0 copy-start.8
  65.4 0.6 copy-done.8
  66.0 0.9 pad_maximum_fusion.4.query
  66.9 5.0 %collective-permute-done.5.rest_4_ = bf16[2,256,512]{2,1,0:T(8,128)(2,1)} collective-permute-done((bf16[2,256,512]{2,1,0:T(8,128)(2,1)S(1)}, bf16[2,256,512]{2,1,0:T(8,128)(2,1)}, u32[]{:S(2)}, u32[]{:S(2)}) %collective-permute-start.5) | collective-permute-done | bytes 524320 | tf_op jit(solution)/shard_map/ppermute | solution.py:219
  71.9 4.2 %collective-permute-done.3.rest_0_ = bf16[2,256,512]{2,1,0:T(8,128)(2,1)} collective-permute-done((bf16[2,256,512]{2,1,0:T(8,128)(2,1)}, bf16[2,256,512]{2,1,0:T(8,128)(2,1)}, u32[]{:S(2)}, u32[]{:S(2)}) %collective-permute-start.3) | collective-permute-done | bytes 524320 | tf_op jit(solution)/shard_map/ppermute | solution.py:219
  76.0 6.5 %attended.1 = (bf16[256,512]{1,0:T(8,128)(2,1)S(1)}, f32[4,1,256]{2,1,0:T(1,128)S(1)}) custom-call(s32[4]{0:T(128)S(1)} %pad_add_fusion.1.info, s32[2,256]{1,0:T(2,128)S(1)} %pad_add_fusion.spans, bf16[256,512]{1,0:T(8,128)(2,1)S(1)} %pad_maximum_fusion.4.query, bf16[2,256,512]{2,1,0:T(8,128)(2,1)} %collective-permute-done.3.rest_0_, ...), custom_call_target="tpu_custom_call" | custom-call | flops 671088640 | bytes 8388608 | tf_op jit(solution)/shard_map/attended/pallas_call | solution.py:157
  82.5 0.0 collective-permute-done.6
  82.6 3.1 %convolution_convert_fusion = bf16[2048,512]{1,0:T(8,128)(2,1)} fusion(bf16[256,512]{1,0:T(8,128)(2,1)S(1)} %get-tuple-element.15.attended, bf16[128,2048]{1,0:T(8,128)(2,1)} %collective-permute-done.6, bf16[128,2048]{1,0:T(8,128)(2,1)S(1)} %bitcast.43), kind=kOutput, calls=%fused_computation | convolution fusion | flops 540016640 | bytes 3407872 | tf_op jit(solution)/shard_map/dot_general | solution.py:33
  85.7 0.7 copy-done.4
  86.4 0.0 all-to-all-done.1
  86.4 6.7 %all-to-all-start.2 = ((bf16[4,512,512]{2,1,0:T(8,128)(2,1)}), bf16[4,512,512]{2,1,0:T(8,128)(2,1)}, u32[]{:S(2)}, u32[]{:S(2)}) async-start(bf16[4,512,512]{2,1,0:T(8,128)(2,1)} %bitcast.36), calls=%async_computation.2 | async-start | bytes 4194304 | tf_op jit(solution)/shard_map/all_to_all | solution.py:273
  93.1 1.3 pad_maximum_fusion.out_grad
  94.5 10.9 %gradients.1 = (bf16[256,512]{1,0:T(8,128)(2,1)S(1)}, bf16[2,256,512]{2,1,0:T(8,128)(2,1)S(1)}, f32[2,256,512]{2,1,0:T(8,128)S(1)}, f32[2,256,512]{2,1,0:T(8,128...) custom-call(s32[4]{0:T(128)S(1)} %pad_add_fusion.1.info, s32[2,256]{1,0:T(2,128)S(1)} %pad_add_fusion.spans, ...), custom_call_target="tpu_custom_call" | custom-call | flops 1677721600 | bytes 16777216 | tf_op jit(solution)/shard_map/gradients/pallas_call | solution.py:182
  105.4 0.0 copy-start.2
  105.4 1.9 %collective-permute-start.7 = (bf16[2,256,512]{2,1,0:T(8,128)(2,1)S(1)}, bf16[2,256,512]{2,1,0:T(8,128)(2,1)S(1)}, u32[]{:S(2)}, u32[]{:S(2)}) collective-permute-start(bf16[2,256,512]{2,1,0:T(8,128)(2,1)S(1)} %get-tuple-element.20), channel_id=1, source_target_pairs={{0,2},{2,4},{4,6},{6,8},{8,10},{10,12},{12,14},{14,16},{16,18},{18... | collective-permute-start | bytes 1572872 | tf_op jit(solution)/shard_map/ppermute | solution.py:219
  107.3 5.5 %collective-permute-start.9 = (bf16[2,256,512]{2,1,0:T(8,128)(2,1)S(1)}, bf16[2,256,512]{2,1,0:T(8,128)(2,1)S(1)}, u32[]{:S(2)}, u32[]{:S(2)}) collective-permute-start(bf16[2,256,512]{2,1,0:T(8,128)(2,1)S(1)} %get-tuple-element.22), channel_id=1, source_target_pairs={{2,0},{4,2},{6,4},{8,6},{10,8},{12,10},{14,12},{16,14},{18,16},{20... | collective-permute-start | bytes 1572872 | tf_op jit(solution)/shard_map/ppermute | solution.py:219
  112.8 6.5 %collective-permute-done.7 = bf16[2,256,512]{2,1,0:T(8,128)(2,1)S(1)} collective-permute-done((bf16[2,256,512]{2,1,0:T(8,128)(2,1)S(1)}, bf16[2,256,512]{2,1,0:T(8,128)(2,1)S(1)}, u32[]{:S(2)}, u32[]{:S(2)}) %collective-permute-start.7) | collective-permute-done | bytes 524320 | tf_op jit(solution)/shard_map/ppermute | solution.py:219
  119.3 1.0 add_convert_fusion.2
  120.2 1.9 %collective-permute-start.8 = (bf16[2,256,512]{2,1,0:T(8,128)(2,1)}, bf16[2,256,512]{2,1,0:T(8,128)(2,1)S(1)}, u32[]{:S(2)}, u32[]{:S(2)}) collective-permute-start(bf16[2,256,512]{2,1,0:T(8,128)(2,1)} %add_convert_fusion.2), channel_id=1, source_target_pairs={{0,2},{2,4},{4,6},{6,8},{8,10},{10,12},{12,14},{14,16},{16,18},{18... | collective-permute-start | bytes 1572872 | tf_op jit(solution)/shard_map/ppermute | solution.py:219
  122.2 0.0 collective-permute-done.9
  122.2 1.0 add_convert_fusion.1
  123.2 5.5 %collective-permute-start.10 = (bf16[2,256,512]{2,1,0:T(8,128)(2,1)}, bf16[2,256,512]{2,1,0:T(8,128)(2,1)S(1)}, u32[]{:S(2)}, u32[]{:S(2)}) collective-permute-start(bf16[2,256,512]{2,1,0:T(8,128)(2,1)} %add_convert_fusion.1), channel_id=1, source_target_pairs={{2,0},{4,2},{6,4},{8,6},{10,8},{12,10},{14,12},{16,14},{18,16},{20... | collective-permute-start | bytes 1572872 | tf_op jit(solution)/shard_map/ppermute | solution.py:219
  128.6 0.0 all-to-all-done.2
  128.7 2.3 %reduce_sum.33 = bf16[512,512]{1,0:T(8,128)(2,1)S(1)} reduce(bf16[4,512,512]{2,1,0:T(8,128)(2,1)} %all-to-all-done.2, bf16[]{:T(256)} %constant.63.clone.1), dimensions={0}, to_apply=%region_5.6 | reduce | flops 786432 | bytes 2621442 | tf_op jit(solution)/shard_map/reduce_sum | solution.py:274
  130.9 0.0 copy-start.3
  130.9 10.1 %all_to_all.26 = bf16[4,128,512]{2,1,0:T(8,128)(2,1)S(1)} all-to-all(bf16[4,128,512]{2,1,0:T(8,128)(2,1)S(1)} %bitcast.37), channel_id=1, replica_groups=mesh['x'=4,'y'=4,'z'=8,'c'=2] {'y'}, dimensions={0} | all-to-all | bytes 1048576 | tf_op jit(solution)/shard_map/all_to_all | solution.py:273
  141.0 0.7 reduce_sum.34
  141.8 12.5 %all-to-all-start.4 = ((bf16[16,8,512]{2,1,0:T(8,128)(2,1)}), bf16[16,8,512]{2,1,0:T(8,128)(2,1)S(1)}, u32[]{:S(2)}, u32[]{:S(2)}) async-start(bf16[16,8,512]{2,1,0:T(8,128)(2,1)} %bitcast.19), calls=%async_computation.4 | async-start | bytes 262144 | tf_op jit(solution)/shard_map/all_to_all | solution.py:276
  154.3 0.0 collective-permute-done.8
  154.3 0.0 collective-permute-done.10
  154.3 0.2 add_convert_fusion
  154.6 0.2 collective-permute-start.11
  154.7 8.7 %all-to-all-done.4 = bf16[16,8,512]{2,1,0:T(8,128)(2,1)S(1)} async-done(((bf16[16,8,512]{2,1,0:T(8,128)(2,1)}), bf16[16,8,512]{2,1,0:T(8,128)(2,1)S(1)}, u32[]{:S(2)}, u32[]{:S(2)}) %all-to-all-start.4) | async-done | bytes 131104 | tf_op jit(solution)/shard_map/all_to_all | solution.py:276
  163.5 0.6 pad_maximum_fusion.5
  164.1 0.0 collective-permute-done.11
  164.1 0.1 broadcast_select_fusion
  164.1 0.9 pad_maximum_fusion.3
  (26 shorter events, 0.3 us)
Async XLA Ops:
  0.6 4.0 %copy-start.9 = (bf16[32,1024]{1,0:T(8,128)(2,1)S(1)}, bf16[32,1024]{1,0:T(8,128)(2,1)}, u32[]{:S(2)}) copy-start(bf16[32,1024]{1,0:T(8,128)(2,1)} %param.10) | copy-start | bytes 196612
  2.7 1.9 %collective-permute-start.1 = (bf16[2,128,512]{2,1,0:T(8,128)(2,1)S(1)}, bf16[2,128,512]{2,1,0:T(8,128)(2,1)S(1)}, u32[]{:S(2)}, u32[]{:S(2)}) collective-permute-start(bf16[2,128,512]{2,1,0:T(8,128)(2,1)S(1)} %get-tuple-element.32), channel_id=1, source_target_pairs={{0,1},{1,0},{2,3},{3,2},{4,5},{5,4},{6,7},{7,6},{8,9},{9,8},{10,11... | collective-permute-start | bytes 786440 | tf_op jit(solution)/shard_map/ppermute | solution.py:236
  24.3 12.2 %copy-start.7 = (bf16[1,128,1024]{2,1,0:T(8,128)(2,1)S(1)}, bf16[1,128,1024]{2,1,0:T(8,128)(2,1)}, u32[]{:S(2)}) copy-start(bf16[1,128,1024]{2,1,0:T(8,128)(2,1)} %param.6) | copy-start | bytes 786436
  24.3 13.7 %copy-start.10 = (s32[1,32]{1,0:T(1,128)S(1)}, s32[1,32]{1,0:T(1,128)}, u32[]{:S(2)}) copy-start(s32[1,32]{1,0:T(1,128)} %param.11) | copy-start | bytes 388
  24.3 62.1 %all-to-all-start.1 = ((bf16[16,512,128]{2,1,0:T(8,128)(2,1)}), bf16[16,512,128]{2,1,0:T(8,128)(2,1)S(1)}, u32[]{:S(2)}, u32[]{:S(2)}) async-start(bf16[16,512,128]{2,1,0:T(8,128)(2,1)} %broadcast_in_dim.46), calls=%async_computation.1 | async-start | bytes 4194304 | tf_op jit(solution)/shard_map/all_to_all | solution.py:253
  31.2 22.5 %collective-permute-start.4 = (bf16[2,256,512]{2,1,0:T(8,128)(2,1)S(1)}, bf16[2,256,512]{2,1,0:T(8,128)(2,1)S(1)}, u32[]{:S(2)}, u32[]{:S(2)}) collective-permute-start(bf16[2,256,512]{2,1,0:T(8,128)(2,1)S(1)} %pad_maximum_fusion.1.rest_2_), channel_id=1, source_target_pairs={{2,0},{4,2},{6,4},{8,6},{10,8},{12,10},{14,12},{16,14},{18,16},{20... | collective-permute-start | bytes 1572872 | tf_op jit(solution)/shard_map/ppermute | solution.py:219
  33.2 27.4 %collective-permute-start.2 = (bf16[2,256,512]{2,1,0:T(8,128)(2,1)S(1)}, bf16[2,256,512]{2,1,0:T(8,128)(2,1)}, u32[]{:S(2)}, u32[]{:S(2)}) collective-permute-start(bf16[2,256,512]{2,1,0:T(8,128)(2,1)S(1)} %pad_maximum_fusion.1.rest_2_), channel_id=1, source_target_pairs={{0,2},{2,4},{4,6},{6,8},{8,10},{10,12},{12,14},{14,16},{16,18},{18... | collective-permute-start | bytes 1572872 | tf_op jit(solution)/shard_map/ppermute | solution.py:219
  37.2 28.1 %collective-permute-start = (bf16[128,512]{1,0:T(8,128)(2,1)}, bf16[128,512]{1,0:T(8,128)(2,1)S(1)}, u32[]{:S(2)}, u32[]{:S(2)}) collective-permute-start(bf16[128,512]{1,0:T(8,128)(2,1)} %get-tuple-element.34), channel_id=1, source_target_pairs={{0,1},{1,0},{2,3},{3,2},{4,5},{5,4},{6,7},{7,6},{8,9},{9,8},{10,11... | collective-permute-start | bytes 393224 | tf_op jit(solution)/shard_map/ppermute | solution.py:242
  38.0 44.5 %collective-permute-start.6 = (bf16[128,2048]{1,0:T(8,128)(2,1)}, bf16[128,2048]{1,0:T(8,128)(2,1)}, u32[]{:S(2)}, u32[]{:S(2)}) collective-permute-start(bf16[128,2048]{1,0:T(8,128)(2,1)} %bitcast.41), channel_id=1, source_target_pairs={{0,1},{1,0},{2,3},{3,2},{4,5},{5,4},{6,7},{7,6},{8,9},{9,8},{10,11... | collective-permute-start | bytes 1572872 | tf_op jit(solution)/shard_map/ppermute | solution.py:243
  53.8 18.1 %collective-permute-start.5 = (bf16[2,256,512]{2,1,0:T(8,128)(2,1)S(1)}, bf16[2,256,512]{2,1,0:T(8,128)(2,1)}, u32[]{:S(2)}, u32[]{:S(2)}) collective-permute-start(bf16[2,256,512]{2,1,0:T(8,128)(2,1)S(1)} %collective-permute-done.4.rest_3_), channel_id=1, source_target_pairs={{2,0},{4,2},{6,4},{8,6},{10,8},{12,10},{14,12},{16,14},{18,16},{20... | collective-permute-start | bytes 1572872 | tf_op jit(solution)/shard_map/ppermute | solution.py:219
  60.6 15.5 %collective-permute-start.3 = (bf16[2,256,512]{2,1,0:T(8,128)(2,1)}, bf16[2,256,512]{2,1,0:T(8,128)(2,1)}, u32[]{:S(2)}, u32[]{:S(2)}) collective-permute-start(bf16[2,256,512]{2,1,0:T(8,128)(2,1)} %collective-permute-done.2.rest_1_), channel_id=1, source_target_pairs={{0,2},{2,4},{4,6},{6,8},{8,10},{10,12},{12,14},{14,16},{16,18},{18... | collective-permute-start | bytes 1572872 | tf_op jit(solution)/shard_map/ppermute | solution.py:219
  63.9 18.6 %copy-start.6 = (bf16[1,128,2048]{2,1,0:T(8,128)(2,1)S(1)}, bf16[1,128,2048]{2,1,0:T(8,128)(2,1)}, u32[]{:S(2)}) copy-start(bf16[1,128,2048]{2,1,0:T(8,128)(2,1)} %param.9) | copy-start | bytes 1572868
  65.3 0.7 copy-start.8
  85.7 0.7 copy-start.4
  86.4 42.3 %all-to-all-start.2 = ((bf16[4,512,512]{2,1,0:T(8,128)(2,1)}), bf16[4,512,512]{2,1,0:T(8,128)(2,1)}, u32[]{:S(2)}, u32[]{:S(2)}) async-start(bf16[4,512,512]{2,1,0:T(8,128)(2,1)} %bitcast.36), calls=%async_computation.2 | async-start | bytes 4194304 | tf_op jit(solution)/shard_map/all_to_all | solution.py:273
  93.1 1.4 copy-start.5
  105.4 17.8 %copy-start = (f32[2,256,512]{2,1,0:T(8,128)}, f32[2,256,512]{2,1,0:T(8,128)S(1)}, u32[]{:S(2)}) copy-start(f32[2,256,512]{2,1,0:T(8,128)S(1)} %get-tuple-element.19) | copy-start | bytes 3145732
  105.4 17.8 %copy-start.2 = (bf16[256,512]{1,0:T(8,128)(2,1)}, bf16[256,512]{1,0:T(8,128)(2,1)S(1)}, u32[]{:S(2)}) copy-start(bf16[256,512]{1,0:T(8,128)(2,1)S(1)} %get-tuple-element.18) | copy-start | bytes 786436
  105.4 13.9 %collective-permute-start.7 = (bf16[2,256,512]{2,1,0:T(8,128)(2,1)S(1)}, bf16[2,256,512]{2,1,0:T(8,128)(2,1)S(1)}, u32[]{:S(2)}, u32[]{:S(2)}) collective-permute-start(bf16[2,256,512]{2,1,0:T(8,128)(2,1)S(1)} %get-tuple-element.20), channel_id=1, source_target_pairs={{0,2},{2,4},{4,6},{6,8},{8,10},{10,12},{12,14},{14,16},{16,18},{18... | collective-permute-start | bytes 1572872 | tf_op jit(solution)/shard_map/ppermute | solution.py:219
  107.3 14.8 %collective-permute-start.9 = (bf16[2,256,512]{2,1,0:T(8,128)(2,1)S(1)}, bf16[2,256,512]{2,1,0:T(8,128)(2,1)S(1)}, u32[]{:S(2)}, u32[]{:S(2)}) collective-permute-start(bf16[2,256,512]{2,1,0:T(8,128)(2,1)S(1)} %get-tuple-element.22), channel_id=1, source_target_pairs={{2,0},{4,2},{6,4},{8,6},{10,8},{12,10},{14,12},{16,14},{18,16},{20... | collective-permute-start | bytes 1572872 | tf_op jit(solution)/shard_map/ppermute | solution.py:219
  120.2 34.0 %collective-permute-start.8 = (bf16[2,256,512]{2,1,0:T(8,128)(2,1)}, bf16[2,256,512]{2,1,0:T(8,128)(2,1)S(1)}, u32[]{:S(2)}, u32[]{:S(2)}) collective-permute-start(bf16[2,256,512]{2,1,0:T(8,128)(2,1)} %add_convert_fusion.2), channel_id=1, source_target_pairs={{0,2},{2,4},{4,6},{6,8},{8,10},{10,12},{12,14},{14,16},{16,18},{18... | collective-permute-start | bytes 1572872 | tf_op jit(solution)/shard_map/ppermute | solution.py:219
  123.2 31.1 %collective-permute-start.10 = (bf16[2,256,512]{2,1,0:T(8,128)(2,1)}, bf16[2,256,512]{2,1,0:T(8,128)(2,1)S(1)}, u32[]{:S(2)}, u32[]{:S(2)}) collective-permute-start(bf16[2,256,512]{2,1,0:T(8,128)(2,1)} %add_convert_fusion.1), channel_id=1, source_target_pairs={{2,0},{4,2},{6,4},{8,6},{10,8},{12,10},{14,12},{16,14},{18,16},{20... | collective-permute-start | bytes 1572872 | tf_op jit(solution)/shard_map/ppermute | solution.py:219
  128.6 25.6 %copy-start.1 = (f32[2,256,512]{2,1,0:T(8,128)S(1)}, f32[2,256,512]{2,1,0:T(8,128)}, u32[]{:S(2)}) copy-start(f32[2,256,512]{2,1,0:T(8,128)} %copy-done) | copy-start | bytes 3145732
  130.9 23.6 %copy-start.3 = (bf16[256,512]{1,0:T(8,128)(2,1)S(1)}, bf16[256,512]{1,0:T(8,128)(2,1)}, u32[]{:S(2)}) copy-start(bf16[256,512]{1,0:T(8,128)(2,1)} %copy-done.2) | copy-start | bytes 786436
  141.8 21.7 %all-to-all-start.4 = ((bf16[16,8,512]{2,1,0:T(8,128)(2,1)}), bf16[16,8,512]{2,1,0:T(8,128)(2,1)S(1)}, u32[]{:S(2)}, u32[]{:S(2)}) async-start(bf16[16,8,512]{2,1,0:T(8,128)(2,1)} %bitcast.19), calls=%async_computation.4 | async-start | bytes 262144 | tf_op jit(solution)/shard_map/all_to_all | solution.py:276
  154.6 9.5 %collective-permute-start.11 = (bf16[3,128,512]{2,1,0:T(8,128)(2,1)S(1)}, bf16[3,128,512]{2,1,0:T(8,128)(2,1)S(1)}, u32[]{:S(2)}, u32[]{:S(2)}) collective-permute-start(bf16[3,128,512]{2,1,0:T(8,128)(2,1)S(1)} %pad_maximum_fusion.2), channel_id=1, source_target_pairs={{0,1},{1,0},{2,3},{3,2},{4,5},{5,4},{6,7},{7,6},{8,9},{9,8},{10,11... | collective-permute-start | bytes 1179656 | tf_op jit(solution)/shard_map/ppermute | solution.py:290

commit v3 on v2

v3 whole, which is shorter than its diff:
```python
import math

import jax
import jax.numpy as jnp
from jax import lax
from jax.experimental import pallas as pl
from jax.experimental.pallas import tpu as pltpu
from jax.sharding import Mesh, PartitionSpec as P

HEADS = 8
HEAD = 128
TOK = 128
CHIP = 2 * TOK
MINE = HEADS // 2
HALF = MINE * HEAD
NEAR = (-1, 0, 1)
FAR = (-2, 2)
SCALE = 1.0 / math.sqrt(HEAD)
LOG2E = math.log2(math.e)
GRAD_PARTS = 0
NEAR_FORWARD = 2013265920
FAR_FORWARD = 2684354560
FAR_BACKWARD = 0
NEAR_BACKWARD = 0
SWAP = [(0, 1), (1, 0)]
COLUMNS = [(h, slice(h * HEAD, (h + 1) * HEAD)) for h in range(MINE)]


def nt(a, b):
    return lax.dot_general(a, b, (((1,), (1,)), ((), ())), preferred_element_type=jnp.float32)


def nn(a, b):
    return lax.dot_general(a, b, (((1,), (0,)), ((), ())), preferred_element_type=jnp.float32)


def tn(a, b):
    return lax.dot_general(a, b, (((0,), (0,)), ((), ())), preferred_element_type=jnp.float32)


def key_blocks(info, offsets, body, other=None):
    for slot, offset in enumerate(offsets):
        for half in range(2):
            parity = info[1] if half == 0 else 1 - info[1]
            base = info[0] + offset * CHIP + parity * TOK
            rows = slice(half * TOK, (half + 1) * TOK)
            needed = jnp.logical_and(base < info[3], base + TOK > info[2])

            @pl.when(needed)
            def _(slot=slot, half=half, rows=rows, base=base):
                body(slot, 2 * slot + half, rows, base)

            if other is not None:

                @pl.when(jnp.logical_not(needed))
                def _(slot=slot, rows=rows):
                    other(slot, rows)


def block_mask(spans, base):
    position = base + lax.broadcasted_iota(jnp.int32, (TOK, CHIP), 0)
    return jnp.logical_and(position >= spans[0:1, :], position < spans[1:2, :])


def masked_scores(keys, query, taken):
    return jnp.where(taken, nt(keys, query) * (SCALE * LOG2E), -1e30)


def by_eights(block):
    return block.reshape(TOK // 8, 8, CHIP)


def over_eights(op, rows):
    return jnp.broadcast_to(op(rows, axis=0, keepdims=True), (8, CHIP))


def score_blocks(info, spans, query, offsets, windows, scores, peak):
    def body(slot, index, rows, base):
        taken = block_mask(spans, base)
        for h, cols in COLUMNS:
            block = masked_scores(windows[slot][0, rows, cols], query[:, cols], taken)
            scores[h, index] = block
            peak[h] = jnp.maximum(peak[h], jnp.max(by_eights(block), axis=0))

    key_blocks(info, offsets, body)
    for h, _ in COLUMNS:
        peak[h] = over_eights(jnp.max, peak[h])


def absorb_blocks(info, offsets, windows, scores, peak, total, acc):
    def body(slot, index, rows, base):
        for h, cols in COLUMNS:
            weights = jnp.exp2(scores[h, index] - peak[h, 0:1, :])
            total[h] += jnp.sum(by_eights(weights), axis=0)
            acc[h] += tn(windows[slot][1, rows, cols], weights.astype(jnp.bfloat16))

    key_blocks(info, offsets, body)


def near_forward_kernel(info, spans, query, below, own, above, peak, total, acc, scores):
    windows = (below, own, above)
    peak[...] = jnp.full(peak.shape, -1e30, jnp.float32)
    total[...] = jnp.zeros(total.shape, jnp.float32)
    acc[...] = jnp.zeros(acc.shape, jnp.float32)
    score_blocks(info, spans, query, NEAR, windows, scores, peak)
    absorb_blocks(info, NEAR, windows, scores, peak, total, acc)


def far_forward_kernel(
    info, spans, query, below, above, near_peak, near_total, near_acc,
    attended, log_norm, scores, peak, total, acc,
):
    windows = (below, above)
    peak[...] = near_peak[...]
    score_blocks(info, spans, query, FAR, windows, scores, peak)
    for h, _ in COLUMNS:
        shrink = jnp.exp2(near_peak[h] - peak[h])
        total[h] = near_total[h] * shrink
        acc[h] = near_acc[h] * shrink[0:1, :]
    absorb_blocks(info, FAR, windows, scores, peak, total, acc)
    for h, cols in COLUMNS:
        row_total = jnp.sum(total[h], axis=0, keepdims=True)
        attended[:, cols] = (acc[h] * (1.0 / row_total)).T.astype(jnp.bfloat16)
        log_norm[h] = peak[h, 0:1, :] + jnp.log(row_total) * LOG2E


def gradient_blocks(
    info, spans, query, grad, log_norm, row_delta, offsets, windows, acc, terms
):
    def body(slot, index, rows, base):
        taken = block_mask(spans, base)
        term = terms[slot]
        for h, cols in COLUMNS:
            keys = windows[slot][0, rows, cols]
            values = windows[slot][1, rows, cols]
            probs = jnp.exp2(masked_scores(keys, query[:, cols], taken) - log_norm[h])
            dprobs = nt(values, grad[:, cols])
            dscores = (probs * (dprobs - row_delta[h])).astype(jnp.bfloat16)
            acc[h] += tn(keys, dscores)
            term[0, rows, cols] = (SCALE * nn(dscores, query[:, cols])).astype(term.dtype)
            term[1, rows, cols] = nn(probs.astype(jnp.bfloat16), grad[:, cols]).astype(term.dtype)

    def other(slot, rows):
        terms[slot][:, rows, :] = jnp.zeros((2, TOK, HALF), terms[slot].dtype)

    key_blocks(info, offsets, body, other)


def grad_parts_kernel(info, own, other, weight, *rest):
    parts = rest[:-1]
    columns = rest[-1]
    for h, cols in COLUMNS:
        columns[:, cols] = weight[h]
    for slot, part in enumerate(parts):
        part[0:TOK, :] = nn(own[slot], columns[...]).astype(jnp.bfloat16)
        part[TOK:CHIP, :] = nn(other[slot], columns[...]).astype(jnp.bfloat16)


def far_backward_kernel(
    info, spans, query, attended, log_norm, below, above, *rest
):
    parts = rest[:-5]
    grad, row_delta, acc, term_below, term_above = rest[-5:]
    acc[...] = jnp.zeros(acc.shape, jnp.float32)
    for h, cols in COLUMNS:
        total = parts[0][:, cols].astype(jnp.float32)
        for part in parts[1:]:
            total = total + part[:, cols].astype(jnp.float32)
        head_grad = total.astype(jnp.bfloat16)
        grad[:, cols] = head_grad
        product = head_grad.astype(jnp.float32) * attended[:, cols].astype(jnp.float32)
        row_delta[h] = jnp.sum(product.T, axis=0, keepdims=True)
    gradient_blocks(
        info, spans, query, grad, log_norm, row_delta, FAR,
        (below, above), acc, (term_below, term_above),
    )


def near_backward_kernel(
    info, spans, query, log_norm, grad, row_delta, far_acc, below, own, above,
    query_grad, term_below, term_own, term_above, acc,
):
    acc[...] = far_acc[...]
    gradient_blocks(
        info, spans, query, grad, log_norm, row_delta, NEAR,
        (below, own, above), acc, (term_below, term_own, term_above),
    )
    for h, cols in COLUMNS:
        query_grad[:, cols] = (SCALE * acc[h]).T.astype(jnp.bfloat16)


def f32(*shape):
    return jax.ShapeDtypeStruct(shape, jnp.float32)


def bf16(*shape):
    return jax.ShapeDtypeStruct(shape, jnp.bfloat16)


EIGHTS = (MINE, 8, CHIP)
ROWS = (MINE, 1, CHIP)
SUMS = (MINE, HEAD, CHIP)
WINDOW = (2, CHIP, HALF)


def kernel(body, name, out_shape, scratch, flops, *operands):
    specs = [pl.BlockSpec(memory_space=pltpu.SMEM)]
    specs += [pl.BlockSpec(memory_space=pltpu.VMEM)] * (len(operands) - 1)
    return pl.pallas_call(
        body,
        in_specs=specs,
        out_specs=[pl.BlockSpec(memory_space=pltpu.VMEM)] * len(out_shape),
        out_shape=out_shape,
        scratch_shapes=[pltpu.VMEM(shape.shape, shape.dtype) for shape in scratch],
        compiler_params=pltpu.CompilerParams(vmem_limit_bytes=16 * 1024 * 1024),
        cost_estimate=pl.CostEstimate(flops=flops, bytes_accessed=0, transcendentals=0),
        name=name,
    )(*operands)


def to_chip(block, distance):
    chips = lax.axis_size("y") * lax.axis_size("z")
    route = [(i, i + distance) for i in range(chips) if 0 <= i + distance < chips]
    return lax.ppermute(block, ("y", "z"), route)


def along(axis, block, distance):
    size = lax.axis_size(axis)
    return lax.ppermute(block, axis, [(i, (i + distance) % size) for i in range(size)])


def swapped(block):
    return lax.ppermute(block, "c", SWAP)


def halves(core, matrix):
    own = lax.dynamic_slice_in_dim(matrix, core * HALF, HALF, matrix.ndim - 1)
    other = lax.dynamic_slice_in_dim(matrix, (1 - core) * HALF, HALF, matrix.ndim - 1)
    return own, other


def image_spans(lengths, core, first):
    ends = jnp.cumsum(lengths)
    starts = ends - lengths
    place = jnp.arange(CHIP, dtype=jnp.int32)
    positions = first + jnp.where(core == 0, place, (place + TOK) % CHIP)
    begun = starts[:, None] <= positions[None, :]
    open_ = ends[:, None] > positions[None, :]
    start = jnp.max(jnp.where(begun, starts[:, None], 0), axis=0)
    end = jnp.min(jnp.where(open_, ends[:, None], jnp.int32(2**30)), axis=0)
    info = jnp.stack([first, core, jnp.min(start), jnp.max(end)]).astype(jnp.int32)
    return info, jnp.stack([start, end])


def on_device(query, keys, values, out_grad, out_weight, lengths):
    core = lax.axis_index("c")
    x, y = lax.axis_index("x"), lax.axis_index("y")
    chip = y * lax.axis_size("z") + lax.axis_index("z")
    size_x, size_y, size_z = (lax.axis_size(a) for a in ("x", "y", "z"))
    quarter = out_grad.shape[2] // size_y

    own_kv, other_kv = halves(core, jnp.stack([keys[0], values[0]]))
    own = jnp.concatenate([own_kv, swapped(other_kv)], axis=1)
    below = to_chip(own, 1)
    above = to_chip(own, -1)

    own_query, other_query = halves(core, query[0])
    chip_query = jnp.concatenate([own_query, swapped(other_query)], axis=0)
    info, spans = image_spans(lengths[0], core, chip * CHIP)

    def quarters(axis, place):
        def piece(distance):
            start = (place + distance) % lax.axis_size(axis) * quarter
            return lax.dynamic_slice_in_dim(out_grad[0], start, quarter, 1)

        got = [piece(0)]
        got += [along(axis, piece(d), d) for d in range(1, lax.axis_size(axis))]
        got = jnp.stack(got)
        return got, swapped(got)

    mine, others = quarters("y", y)

    rows = out_weight.shape[0]
    piece = lax.dynamic_index_in_dim(
        out_weight.reshape(rows, 2, size_x, HEAD), x, 2, keepdims=False
    )
    piece = jnp.broadcast_to(piece.transpose(1, 0, 2)[None], (size_z, 2, rows, HEAD))
    piece = lax.all_to_all(piece.reshape(2 * size_z, rows, HEAD), ("z", "c"), 0, 0)
    piece = jnp.broadcast_to(piece.reshape(1, quarter, HEAD), (size_x, quarter, HEAD))
    weight = lax.all_to_all(piece, "x", 0, 0)

    parts = kernel(
        grad_parts_kernel, "grad_parts", [bf16(CHIP, HALF)] * size_y,
        [bf16(quarter, HALF)], GRAD_PARTS, info, mine, others, weight,
    )
    parts = [parts[0]] + [along("y", parts[d], -d) for d in range(1, size_y)]
    rows_grad = jnp.stack(quarters("x", x), axis=1).reshape(size_x * CHIP, quarter).T

    below, above, info, spans, chip_query = lax.optimization_barrier(
        (below, above, info, spans, chip_query)
    )
    far_below = to_chip(below, 1)
    far_above = to_chip(above, -1)

    near = kernel(
        near_forward_kernel, "near_forward", [f32(*EIGHTS), f32(*EIGHTS), f32(*SUMS)],
        [f32(MINE, 2 * len(NEAR), TOK, CHIP)], NEAR_FORWARD,
        info, spans, chip_query, below, own, above,
    )
    near, rows_grad = lax.optimization_barrier((near, rows_grad))
    attended, log_norm = kernel(
        far_forward_kernel, "far_forward", [bf16(CHIP, HALF), f32(*ROWS)],
        [f32(MINE, 2 * len(FAR), TOK, CHIP), f32(*EIGHTS), f32(*EIGHTS), f32(*SUMS)], FAR_FORWARD,
        info, spans, chip_query, far_below, far_above, *near,
    )
    attended_along = [attended] + [along("x", attended, d) for d in range(1, size_x)]

    grad, row_delta, far_acc, term_far_below, term_far_above = kernel(
        far_backward_kernel, "far_backward",
        [bf16(CHIP, HALF), f32(*ROWS), f32(*SUMS), bf16(*WINDOW), bf16(*WINDOW)],
        [], FAR_BACKWARD,
        info, spans, chip_query, attended, log_norm, far_below, far_above, *parts,
    )
    passed_below = to_chip(term_far_below, -1)
    passed_above = to_chip(term_far_above, 1)
    partial = nn(rows_grad, jnp.concatenate(attended_along, axis=0)).astype(jnp.bfloat16)
    partial, grad = lax.optimization_barrier((partial, grad))
    query_grad, term_below, term_own, term_above = kernel(
        near_backward_kernel, "near_backward",
        [bf16(CHIP, HALF), bf16(*WINDOW), f32(*WINDOW), bf16(*WINDOW)],
        [f32(*SUMS)], NEAR_BACKWARD,
        info, spans, chip_query, log_norm, grad, row_delta, far_acc, below, own, above,
    )
    partial = partial.reshape(size_y, -1, HALF)
    summed = 0.0
    for d in range(size_y):
        piece = lax.dynamic_index_in_dim(partial, (y + d) % size_y, 0, keepdims=False)
        summed = summed + (along("y", piece, d) if d else piece).astype(jnp.float32)
    partial = summed.astype(jnp.bfloat16)
    partial = lax.all_to_all(partial.reshape(2 * size_z, -1, HALF), ("z", "c"), 0, 0)
    partial = jnp.sum(partial.reshape(size_z, 2, -1, HALF).astype(jnp.float32), axis=0)
    weight_grad = jnp.concatenate([partial[0], partial[1]], axis=1)

    total = term_own
    for term, passed, side in ((term_below, passed_below, -1), (term_above, passed_above, 1)):
        both = (term.astype(jnp.float32) + passed.astype(jnp.float32)).astype(jnp.bfloat16)
        total = total + to_chip(both, side).astype(jnp.float32)
    grads = jnp.concatenate([query_grad[None], total.astype(jnp.bfloat16)], axis=0)
    stay = grads[:, :TOK]
    theirs = swapped(grads[:, TOK:])
    low = jnp.where(core == 0, stay, theirs)
    high = jnp.where(core == 0, theirs, stay)
    grads = jnp.concatenate([low, high], axis=2)
    return (grads[0:1], grads[1:2], grads[2:3], weight_grad)


def solution(mesh):
    fine = Mesh(mesh.devices.reshape(4, 4, 8, 2), ("x", "y", "z", "c"))
    tokens = P("x", ("y", "z", "c"), None)
    return jax.shard_map(
        on_device,
        mesh=fine,
        in_specs=(tokens, tokens, tokens, tokens, P(("y", "z", "c"), None), P("x", None)),
        out_specs=(tokens, tokens, tokens, P(("x", "y", "z", "c"), None)),
        check_vma=False,
    )
```

time: 168 us -> 139 us (0.83)
  the two profiles are of different devices: /device:TPU:13 before, /device:TPU:17 now
where the time goes in v3:
time: 139 us; the launch traced here: 138 us
  starting transfers between devices  74.4 us (54%)
  waiting for transfers between devices  32.3 us (23%)
  Pallas kernels  13 us (9%)
  other arithmetic  10.9 us (8%)
  local copies, waits for them, and re-layouts  4.38 us (3%)
  matrix products  1.56 us (1%)
    ppermute x8, starting transfers between devices, to_chip(): return lax.ppermute(block, ('y', 'z'), route)  35.5 us
    ppermute x15, waiting for transfers between devices, along(): lax.ppermute(block, axis, [(i, (i + distance) % size) for i in range(size)])  21.4 us
    ppermute x15, starting transfers between devices, along(): lax.ppermute(block, axis, [(i, (i + distance) % size) for i in range(size)])  18 us
    pallas_call x5, Pallas kernels, kernel(): pl.pallas_call(body, in_specs=specs, out_specs=[pl.BlockSpec(memory_space...  13 us
    all_to_all x1, starting transfers between devices, on_device(): lax.all_to_all(piece.reshape(2 * size_z, rows, HEAD), ('z', 'c'), 0, 0)  8.83 us
    all_to_all x1, waiting for transfers between devices, on_device(): lax.all_to_all(partial.reshape(2 * size_z, -1, HALF), ('z', 'c'), 0, 0)  8.63 us
    all_to_all x1, starting transfers between devices, on_device(): lax.all_to_all(partial.reshape(2 * size_z, -1, HALF), ('z', 'c'), 0, 0)  4.98 us
    ppermute x5, starting transfers between devices, swapped(): return lax.ppermute(block, 'c', SWAP)  3.71 us
  transfers between devices with their start and end apart: 31, of which 5 were waited for; matrix products, arithmetic and copies ran while one was open for 10% of the time, Pallas kernels for 9%

profile of v3, /device:TPU:17, one launch (start us, length us, event | category | flops | bytes accessed | tf_op | source)
XLA Modules:
  0.0 137.8 jit_solution(302274179513774302)
XLA Ops:
  0.8 0.0 copy-start.1
  0.8 1.5 %constant_dynamic-slice_fusion.1 = (bf16[1,128,512]{2,1,0:T(8,128)(2,1)S(1)}, bf16[128,512]{1,0:T(8,128)(2,1)S(1)}, bf16[128,512]{1,0:T(8,128)(2,1)S(1)}, bf16[1...) fusion(bf16[1,128,2048]{2,1,0:T(8,128)(2,1)} %param.9, ...), kind=kLoop, calls=%fused_computation.55 | loop fusion | bytes 2097184 | tf_op jit(solution)/shard_map/dynamic_slice | solution.py:274
  2.2 1.3 collective-permute-start.6
  3.5 2.5 %collective-permute-start.7 = (bf16[128,512]{1,0:T(8,128)(2,1)S(1)}, bf16[128,512]{1,0:T(8,128)(2,1)S(1)}, u32[]{:S(2)}, u32[]{:S(2)}) collective-permute-start(bf16[128,512]{1,0:T(8,128)(2,1)S(1)} %get-tuple-element.75), channel_id=1, source_target_pairs={{0,128},{64,192},{128,0},{192,64},{1,129},{65,193},{129,1},{193,65... | collective-permute-start | bytes 393224 | tf_op jit(solution)/shard_map/ppermute | solution.py:229
  6.0 1.2 collective-permute-start.8
  7.3 1.6 %collective-permute-start = (bf16[2,128,512]{2,1,0:T(8,128)(2,1)S(1)}, bf16[2,128,512]{2,1,0:T(8,128)(2,1)S(1)}, u32[]{:S(2)}, u32[]{:S(2)}) collective-permute-start(bf16[2,128,512]{2,1,0:T(8,128)(2,1)S(1)} %get-tuple-element.83), channel_id=1, source_target_pairs={{0,1},{1,0},{2,3},{3,2},{4,5},{5,4},{6,7},{7,6},{8,9},{9,8},{10,11... | collective-permute-start | bytes 786440 | tf_op jit(solution)/shard_map/ppermute | solution.py:233
  8.9 1.0 collective-permute-start.13
  10.0 0.7 broadcast_in_dim.44
  10.7 8.8 %all-to-all-start = ((bf16[16,32,128]{2,1,0:T(8,128)(2,1)}), bf16[16,32,128]{2,1,0:T(8,128)(2,1)S(1)}, u32[]{:S(2)}, u32[]{:S(2)}) async-start(bf16[16,32,128]{2,1,0:T(8,128)(2,1)} %bitcast.29), calls=%async_computation | async-start | bytes 262144 | tf_op jit(solution)/shard_map/all_to_all | solution.py:288
  19.5 0.1 copy.16
  19.6 0.1 reduce-window.7
  19.6 0.1 reduce
  19.8 0.1 select_reduce_fusion.1
  19.9 0.5 collective-permute-start.14
  20.4 1.1 collective-permute-start.15
  21.5 3.3 %collective-permute-start.1 = (bf16[2,256,512]{2,1,0:T(8,128)(2,1)S(1)}, bf16[2,256,512]{2,1,0:T(8,128)(2,1)S(1)}, u32[]{:S(2)}, u32[]{:S(2)}) collective-permute-start(bf16[2,256,512]{2,1,0:T(8,128)(2,1)S(1)} %pad_maximum_fusion.1.own), channel_id=1, source_target_pairs={{0,2},{2,4},{4,6},{6,8},{8,10},{10,12},{12,14},{14,16},{16,18},{18... | collective-permute-start | bytes 1572872 | tf_op jit(solution)/shard_map/ppermute | solution.py:224
  24.8 4.7 %collective-permute-start.2 = (bf16[2,256,512]{2,1,0:T(8,128)(2,1)S(1)}, bf16[2,256,512]{2,1,0:T(8,128)(2,1)S(1)}, u32[]{:S(2)}, u32[]{:S(2)}) collective-permute-start(bf16[2,256,512]{2,1,0:T(8,128)(2,1)S(1)} %pad_maximum_fusion.1.own), channel_id=1, source_target_pairs={{2,0},{4,2},{6,4},{8,6},{10,8},{12,10},{14,12},{16,14},{18,16},{20... | collective-permute-start | bytes 1572872 | tf_op jit(solution)/shard_map/ppermute | solution.py:224
  29.5 1.1 fusion.18
  30.6 1.2 collective-permute-start.3
  31.8 0.1 collective-permute-start.9
  31.9 1.0 pad_maximum_fusion.3.own
  32.9 0.5 collective-permute-start.16
  33.4 0.7 reduce_min.18
  34.1 0.6 reduce_max.19
  34.7 0.9 broadcast_in_dim.46
  35.6 3.5 %all-to-all-start.1 = ((bf16[4,512,128]{2,1,0:T(8,128)(2,1)}), bf16[4,512,128]{2,1,0:T(8,128)(2,1)S(1)}, u32[]{:S(2)}, u32[]{:S(2)}) async-start(bf16[4,512,128]{2,1,0:T(8,128)(2,1)} %broadcast_in_dim.46), calls=%async_computation.1 | async-start | bytes 1048576 | tf_op jit(solution)/shard_map/all_to_all | solution.py:290
  39.0 1.3 pad_add_fusion.1.info
  40.4 1.9 %collective-permute-start.4 = (bf16[2,256,512]{2,1,0:T(8,128)(2,1)S(1)}, bf16[2,256,512]{2,1,0:T(8,128)(2,1)}, u32[]{:S(2)}, u32[]{:S(2)}) collective-permute-start(bf16[2,256,512]{2,1,0:T(8,128)(2,1)S(1)} %collective-permute-done.1.below), channel_id=1, source_target_pairs={{0,2},{2,4},{4,6},{6,8},{8,10},{10,12},{12,14},{14,16},{16,18},{18... | collective-permute-start | bytes 1572872 | tf_op jit(solution)/shard_map/ppermute | solution.py:224
  42.4 5.6 %collective-permute-start.5 = (bf16[2,256,512]{2,1,0:T(8,128)(2,1)S(1)}, bf16[2,256,512]{2,1,0:T(8,128)(2,1)}, u32[]{:S(2)}, u32[]{:S(2)}) collective-permute-start(bf16[2,256,512]{2,1,0:T(8,128)(2,1)S(1)} %collective-permute-done.2.above), channel_id=1, source_target_pairs={{2,0},{4,2},{6,4},{8,6},{10,8},{12,10},{14,12},{16,14},{18,16},{20... | collective-permute-start | bytes 1572872 | tf_op jit(solution)/shard_map/ppermute | solution.py:224
  47.9 0.6 all-to-all-done.1.weight
  48.6 1.8 %grad_parts.1 = (bf16[256,512]{1,0:T(8,128)(2,1)S(1)}, bf16[256,512]{1,0:T(8,128)(2,1)S(1)}, bf16[256,512]{1,0:T(8,128)(2,1)S(1)}, bf16[256,512]{1,0:T(8,128)(2,1)S(1)}) custom-call(s32[4]{0:T(128)S(1)} %pad_add_fusion.1.info, bf16[4,128,512]{2,1,0:T(8,128)(2,1)S(1)} %pad_maximum_fusion.3.own, bf16[4,128,512]{2,1,0:T(8,128)(2,1)} %collective-permute-done.16.other, ...), custom_call_target="tpu_custom_call" | custom-call | tf_op jit(solution)/shard_map/grad_parts/pallas_call | solution.py:209
  50.5 1.3 collective-permute-start.17
  51.8 0.5 collective-permute-start.18
  52.3 1.4 %collective-permute-start.19 = (bf16[256,512]{1,0:T(8,128)(2,1)S(1)}, bf16[256,512]{1,0:T(8,128)(2,1)S(1)}, u32[]{:S(2)}, u32[]{:S(2)}) collective-permute-start(bf16[256,512]{1,0:T(8,128)(2,1)S(1)} %get-tuple-element.50), channel_id=1, source_target_pairs={{0,16},{16,32},{32,48},{48,0},{1,17},{17,33},{33,49},{49,1},{2,18}... | collective-permute-start | bytes 786440 | tf_op jit(solution)/shard_map/ppermute | solution.py:229
  53.7 1.3 pad_maximum_fusion
  55.0 2.8 %near_forward.1 = (f32[4,8,256]{2,1,0:T(8,128)S(1)}, f32[4,8,256]{2,1,0:T(8,128)S(1)}, f32[4,128,256]{2,1,0:T(8,128)S(1)}) custom-call(s32[4]{0:T(128)S(1)} %pad_add_fusion.1.info, s32[2,256]{1,0:T(2,128)S(1)} %pad_add_fusion.spans, bf16[256,512]{1,0:T(8,128)(2,1)S(1)} %pad_maximum_fusion.6.query, bf16[2,256,512]{2,1,0:T(8,128)(2,1)S(1)} %collective-permute-done.1.below, ...), custom_call_target="tpu_custom_call" | custom-call | flops 2013265920 | tf_op jit(solution)/shard_map/near_forward/pallas_call | solution.py:209
  57.8 1.5 %far_forward.1 = (bf16[256,512]{1,0:T(8,128)(2,1)S(1)}, f32[4,1,256]{2,1,0:T(1,128)S(1)}) custom-call(s32[4]{0:T(128)S(1)} %pad_add_fusion.1.info, s32[2,256]{1,0:T(2,128)S(1)} %pad_add_fusion.spans, bf16[256,512]{1,0:T(8,128)(2,1)S(1)} %pad_maximum_fusion.6.query, bf16[2,256,512]{2,1,0:T(8,128)(2,1)} %collective-permute-done.4.below, ...), custom_call_target="tpu_custom_call" | custom-call | flops 2684354560 | tf_op jit(solution)/shard_map/far_forward/pallas_call | solution.py:209
  59.3 2.5 %collective-permute-start.10 = (bf16[256,512]{1,0:T(8,128)(2,1)S(1)}, bf16[256,512]{1,0:T(8,128)(2,1)S(1)}, u32[]{:S(2)}, u32[]{:S(2)}) collective-permute-start(bf16[256,512]{1,0:T(8,128)(2,1)S(1)} %get-tuple-element.46.attended), channel_id=1, source_target_pairs={{0,64},{64,128},{128,192},{192,0},{1,65},{65,129},{129,193},{193,1... | collective-permute-start | bytes 786440 | tf_op jit(solution)/shard_map/ppermute | solution.py:229
  61.8 2.1 %collective-permute-start.11 = (bf16[256,512]{1,0:T(8,128)(2,1)S(1)}, bf16[256,512]{1,0:T(8,128)(2,1)S(1)}, u32[]{:S(2)}, u32[]{:S(2)}) collective-permute-start(bf16[256,512]{1,0:T(8,128)(2,1)S(1)} %get-tuple-element.46.attended), channel_id=1, source_target_pairs={{0,128},{64,192},{128,0},{192,64},{1,129},{65,193},{129,1},{193,65... | collective-permute-start | bytes 786440 | tf_op jit(solution)/shard_map/ppermute | solution.py:229
  63.9 1.2 collective-permute-start.12
  65.1 4.5 %collective-permute-done.19.rest_3_ = bf16[256,512]{1,0:T(8,128)(2,1)S(1)} collective-permute-done((bf16[256,512]{1,0:T(8,128)(2,1)S(1)}, bf16[256,512]{1,0:T(8,128)(2,1)S(1)}, u32[]{:S(2)}, u32[]{:S(2)}) %collective-permute-start.19) | collective-permute-done | bytes 262176 | tf_op jit(solution)/shard_map/ppermute | solution.py:229
  69.6 1.6 %far_backward.1 = (bf16[256,512]{1,0:T(8,128)(2,1)S(1)}, f32[4,1,256]{2,1,0:T(1,128)S(1)}, f32[4,128,256]{2,1,0:T(8,128)S(1)}, bf16[2,256,512]{2,1,0:T(8,128)(2,1)S(1)}, bf16[2,256,512]{2,1,0:T(8,128)(2,1)S(1)}) custom-call(s32[4]{0:T(128)S(1)} %pad_add_fusion.1.info, s32[2,256]{1,0:T(2,128)S(1)} %pad_add_fusion.spans, ...), custom_call_target="tpu_custom_call" | custom-call | tf_op jit(solution)/shard_map/far_backward/pallas_call | solution.py:209
  71.2 10.0 %collective-permute-start.20 = (bf16[2,256,512]{2,1,0:T(8,128)(2,1)S(1)}, bf16[2,256,512]{2,1,0:T(8,128)(2,1)S(1)}, u32[]{:S(2)}, u32[]{:S(2)}) collective-permute-start(bf16[2,256,512]{2,1,0:T(8,128)(2,1)S(1)} %get-tuple-element.58), channel_id=1, source_target_pairs={{2,0},{4,2},{6,4},{8,6},{10,8},{12,10},{14,12},{16,14},{18,16},{20... | collective-permute-start | bytes 1572872 | tf_op jit(solution)/shard_map/ppermute | solution.py:224
  81.2 1.9 %collective-permute-start.22 = (bf16[2,256,512]{2,1,0:T(8,128)(2,1)S(1)}, bf16[2,256,512]{2,1,0:T(8,128)(2,1)S(1)}, u32[]{:S(2)}, u32[]{:S(2)}) collective-permute-start(bf16[2,256,512]{2,1,0:T(8,128)(2,1)S(1)} %get-tuple-element.60), channel_id=1, source_target_pairs={{0,2},{2,4},{4,6},{6,8},{8,10},{10,12},{12,14},{14,16},{16,18},{18... | collective-permute-start | bytes 1572872 | tf_op jit(solution)/shard_map/ppermute | solution.py:224
  83.1 1.6 %convolution_convert_fusion = bf16[512,512]{1,0:T(8,128)(2,1)} fusion(bf16[512,1024]{0,1:T(8,128)(2,1)S(1)} %bitcast.68, bf16[256,512]{1,0:T(8,128)(2,1)S(1)} %collective-permute-done.12, bf16[256,512]{1,0:T(8,128)(2,1)S(1)} %collective-permute-done.11, bf16[256,512]{1,0:T(8,128)(2,1)S(1)} %collective-permute-done.10, ...), kind=kOutput, calls=%fused_computation | convolution fusion | flops 541327360 | bytes 2621440 | tf_op jit(solution)/shard_map/dot_general | solution.py:34
  84.7 5.3 %near_backward.1 = (bf16[256,512]{1,0:T(8,128)(2,1)S(1)}, bf16[2,256,512]{2,1,0:T(8,128)(2,1)S(1)}, f32[2,256,512]{2,1,0:T(8,128)S(1)}, bf16[2,256,512]{2,1,0:T(8,128)(2,1)S(1)}) custom-call(s32[4]{0:T(128)S(1)} %pad_add_fusion.1.info, s32[2,256]{1,0:T(2,128)S(1)} %pad_add_fusion.spans, bf16[256,512]{1,0:T(8,128)(2,1)S(1)} %pad_maximum_fusion.6.query, ...), custom_call_target="tpu_custom_call" | custom-call | tf_op jit(solution)/shard_map/near_backward/pallas_call | solution.py:209
  90.0 1.7 %collective-permute-done.20 = bf16[2,256,512]{2,1,0:T(8,128)(2,1)S(1)} collective-permute-done((bf16[2,256,512]{2,1,0:T(8,128)(2,1)S(1)}, bf16[2,256,512]{2,1,0:T(8,128)(2,1)S(1)}, u32[]{:S(2)}, u32[]{:S(2)}) %collective-permute-start.20) | collective-permute-done | bytes 524320 | tf_op jit(solution)/shard_map/ppermute | solution.py:224
  91.6 0.1 add_convert_fusion.2
  91.8 6.2 %collective-permute-start.21 = (bf16[2,256,512]{2,1,0:T(8,128)(2,1)S(1)}, bf16[2,256,512]{2,1,0:T(8,128)(2,1)S(1)}, u32[]{:S(2)}, u32[]{:S(2)}) collective-permute-start(bf16[2,256,512]{2,1,0:T(8,128)(2,1)S(1)} %add_convert_fusion.2), channel_id=1, source_target_pairs={{2,0},{4,2},{6,4},{8,6},{10,8},{12,10},{14,12},{16,14},{18,16},{20... | collective-permute-start | bytes 1572872 | tf_op jit(solution)/shard_map/ppermute | solution.py:224
  98.0 0.9 add_convert_fusion.1
  99.0 1.9 %collective-permute-start.23 = (bf16[2,256,512]{2,1,0:T(8,128)(2,1)}, bf16[2,256,512]{2,1,0:T(8,128)(2,1)S(1)}, u32[]{:S(2)}, u32[]{:S(2)}) collective-permute-start(bf16[2,256,512]{2,1,0:T(8,128)(2,1)} %add_convert_fusion.1), channel_id=1, source_target_pairs={{0,2},{2,4},{4,6},{6,8},{8,10},{10,12},{12,14},{14,16},{16,18},{18... | collective-permute-start | bytes 1572872 | tf_op jit(solution)/shard_map/ppermute | solution.py:224
  100.9 1.1 dynamic-slice_bitcast_fusion.2
  102.0 0.1 collective-permute-start.25
  102.1 0.1 collective-permute-start.26
  102.2 1.4 collective-permute-start.27
  103.5 16.8 %collective-permute-done.25 = bf16[128,512]{1,0:T(8,128)(2,1)S(1)} collective-permute-done((bf16[128,512]{1,0:T(8,128)(2,1)S(1)}, bf16[128,512]{1,0:T(8,128)(2,1)S(1)}, u32[]{:S(2)}, u32[]{:S(2)}) %collective-permute-start.25) | collective-permute-done | bytes 131104 | tf_op jit(solution)/shard_map/ppermute | solution.py:229
  120.3 1.7 %fusion.13 = bf16[16,8,512]{2,1,0:T(8,128)(2,1)} fusion(bf16[128,512]{1,0:T(8,128)(2,1)} %collective-permute-done.27, bf16[128,512]{1,0:T(8,128)(2,1)S(1)} %collective-permute-done.26, bf16[128,512]{1,0:T(8,128)(2,1)S(1)} %collective-permute-done.25, bf16[4,128,512]{2,1,0:T(8,128)(2,1)} %bitcast.72, s32[]{:T(128)S(6)} %select_n.161), kind=kLoop, calls=%fused_computation.34 | loop fusion | flops 524288 | bytes 655364 | tf_op jit(solution)/shard_map/reshape | solution.py:340
  122.0 5.0 %all-to-all-start.2 = ((bf16[16,8,512]{2,1,0:T(8,128)(2,1)}), bf16[16,8,512]{2,1,0:T(8,128)(2,1)S(1)}, u32[]{:S(2)}, u32[]{:S(2)}) async-start(bf16[16,8,512]{2,1,0:T(8,128)(2,1)} %fusion.13), calls=%async_computation.2 | async-start | bytes 262144 | tf_op jit(solution)/shard_map/all_to_all | solution.py:340
  127.0 0.2 add_convert_fusion
  127.3 0.3 collective-permute-start.24
  127.6 8.6 %all-to-all-done.2 = bf16[16,8,512]{2,1,0:T(8,128)(2,1)S(1)} async-done(((bf16[16,8,512]{2,1,0:T(8,128)(2,1)}), bf16[16,8,512]{2,1,0:T(8,128)(2,1)S(1)}, u32[]{:S(2)}, u32[]{:S(2)}) %all-to-all-start.2) | async-done | bytes 131104 | tf_op jit(solution)/shard_map/all_to_all | solution.py:340
  136.3 0.6 pad_maximum_fusion.7
  136.9 0.1 broadcast_select_fusion
  136.9 0.9 pad_maximum_fusion.5
  (50 shorter events, 0.4 us)
Async XLA Ops:
  0.7 6.4 %copy-start = (bf16[1,128,1024]{2,1,0:T(8,128)(2,1)S(1)}, bf16[1,128,1024]{2,1,0:T(8,128)(2,1)}, u32[]{:S(2)}) copy-start(bf16[1,128,1024]{2,1,0:T(8,128)(2,1)} %param.7) | copy-start | bytes 786436
  0.8 6.4 %copy-start.1 = (bf16[1,128,1024]{2,1,0:T(8,128)(2,1)S(1)}, bf16[1,128,1024]{2,1,0:T(8,128)(2,1)}, u32[]{:S(2)}) copy-start(bf16[1,128,1024]{2,1,0:T(8,128)(2,1)} %param.8) | copy-start | bytes 786436
  2.2 17.7 %collective-permute-start.6 = (bf16[128,512]{1,0:T(8,128)(2,1)S(1)}, bf16[128,512]{1,0:T(8,128)(2,1)S(1)}, u32[]{:S(2)}, u32[]{:S(2)}) collective-permute-start(bf16[128,512]{1,0:T(8,128)(2,1)S(1)} %get-tuple-element.76), channel_id=1, source_target_pairs={{0,64},{64,128},{128,192},{192,0},{1,65},{65,129},{129,193},{193,1... | collective-permute-start | bytes 393224 | tf_op jit(solution)/shard_map/ppermute | solution.py:229
  3.5 18.0 %collective-permute-start.7 = (bf16[128,512]{1,0:T(8,128)(2,1)S(1)}, bf16[128,512]{1,0:T(8,128)(2,1)S(1)}, u32[]{:S(2)}, u32[]{:S(2)}) collective-permute-start(bf16[128,512]{1,0:T(8,128)(2,1)S(1)} %get-tuple-element.75), channel_id=1, source_target_pairs={{0,128},{64,192},{128,0},{192,64},{1,129},{65,193},{129,1},{193,65... | collective-permute-start | bytes 393224 | tf_op jit(solution)/shard_map/ppermute | solution.py:229
  6.0 18.8 %collective-permute-start.8 = (bf16[128,512]{1,0:T(8,128)(2,1)S(1)}, bf16[128,512]{1,0:T(8,128)(2,1)S(1)}, u32[]{:S(2)}, u32[]{:S(2)}) collective-permute-start(bf16[128,512]{1,0:T(8,128)(2,1)S(1)} %get-tuple-element.74), channel_id=1, source_target_pairs={{0,192},{64,0},{128,64},{192,128},{1,193},{65,1},{129,65},{193,129... | collective-permute-start | bytes 393224 | tf_op jit(solution)/shard_map/ppermute | solution.py:229
  7.1 2.8 %copy-start.3 = (bf16[32,1024]{1,0:T(8,128)(2,1)S(1)}, bf16[32,1024]{1,0:T(8,128)(2,1)}, u32[]{:S(2)}) copy-start(bf16[32,1024]{1,0:T(8,128)(2,1)} %param.10) | copy-start | bytes 196612
  7.2 12.3 %copy-start.4 = (s32[1,32]{1,0:T(1,128)S(1)}, s32[1,32]{1,0:T(1,128)}, u32[]{:S(2)}) copy-start(s32[1,32]{1,0:T(1,128)} %param.11) | copy-start | bytes 388
  7.2 12.6 %copy-start.2 = (bf16[1,128,1024]{2,1,0:T(8,128)(2,1)S(1)}, bf16[1,128,1024]{2,1,0:T(8,128)(2,1)}, u32[]{:S(2)}) copy-start(bf16[1,128,1024]{2,1,0:T(8,128)(2,1)} %param.6) | copy-start | bytes 786436
  7.3 13.1 %collective-permute-start = (bf16[2,128,512]{2,1,0:T(8,128)(2,1)S(1)}, bf16[2,128,512]{2,1,0:T(8,128)(2,1)S(1)}, u32[]{:S(2)}, u32[]{:S(2)}) collective-permute-start(bf16[2,128,512]{2,1,0:T(8,128)(2,1)S(1)} %get-tuple-element.83), channel_id=1, source_target_pairs={{0,1},{1,0},{2,3},{3,2},{4,5},{5,4},{6,7},{7,6},{8,9},{9,8},{10,11... | collective-permute-start | bytes 786440 | tf_op jit(solution)/shard_map/ppermute | solution.py:233
  8.9 21.7 %collective-permute-start.13 = (bf16[128,512]{1,0:T(8,128)(2,1)S(1)}, bf16[128,512]{1,0:T(8,128)(2,1)}, u32[]{:S(2)}, u32[]{:S(2)}) collective-permute-start(bf16[128,512]{1,0:T(8,128)(2,1)S(1)} %get-tuple-element.73), channel_id=1, source_target_pairs={{0,16},{16,32},{32,48},{48,0},{1,17},{17,33},{33,49},{49,1},{2,18}... | collective-permute-start | bytes 393224 | tf_op jit(solution)/shard_map/ppermute | solution.py:229
  10.7 24.0 %all-to-all-start = ((bf16[16,32,128]{2,1,0:T(8,128)(2,1)}), bf16[16,32,128]{2,1,0:T(8,128)(2,1)S(1)}, u32[]{:S(2)}, u32[]{:S(2)}) async-start(bf16[16,32,128]{2,1,0:T(8,128)(2,1)} %bitcast.29), calls=%async_computation | async-start | bytes 262144 | tf_op jit(solution)/shard_map/all_to_all | solution.py:288
  19.9 11.9 %collective-permute-start.14 = (bf16[128,512]{1,0:T(8,128)(2,1)S(1)}, bf16[128,512]{1,0:T(8,128)(2,1)S(1)}, u32[]{:S(2)}, u32[]{:S(2)}) collective-permute-start(bf16[128,512]{1,0:T(8,128)(2,1)S(1)} %get-tuple-element.79), channel_id=1, source_target_pairs={{0,32},{16,48},{32,0},{48,16},{1,33},{17,49},{33,1},{49,17},{2,34}... | collective-permute-start | bytes 393224 | tf_op jit(solution)/shard_map/ppermute | solution.py:229
  20.4 11.5 %collective-permute-start.15 = (bf16[128,512]{1,0:T(8,128)(2,1)S(1)}, bf16[128,512]{1,0:T(8,128)(2,1)S(1)}, u32[]{:S(2)}, u32[]{:S(2)}) collective-permute-start(bf16[128,512]{1,0:T(8,128)(2,1)S(1)} %get-tuple-element.78), channel_id=1, source_target_pairs={{0,48},{16,0},{32,16},{48,32},{1,49},{17,1},{33,17},{49,33},{2,50}... | collective-permute-start | bytes 393224 | tf_op jit(solution)/shard_map/ppermute | solution.py:229
  21.5 18.9 %collective-permute-start.1 = (bf16[2,256,512]{2,1,0:T(8,128)(2,1)S(1)}, bf16[2,256,512]{2,1,0:T(8,128)(2,1)S(1)}, u32[]{:S(2)}, u32[]{:S(2)}) collective-permute-start(bf16[2,256,512]{2,1,0:T(8,128)(2,1)S(1)} %pad_maximum_fusion.1.own), channel_id=1, source_target_pairs={{0,2},{2,4},{4,6},{6,8},{8,10},{10,12},{12,14},{14,16},{16,18},{18... | collective-permute-start | bytes 1572872 | tf_op jit(solution)/shard_map/ppermute | solution.py:224
  24.8 15.6 %collective-permute-start.2 = (bf16[2,256,512]{2,1,0:T(8,128)(2,1)S(1)}, bf16[2,256,512]{2,1,0:T(8,128)(2,1)S(1)}, u32[]{:S(2)}, u32[]{:S(2)}) collective-permute-start(bf16[2,256,512]{2,1,0:T(8,128)(2,1)S(1)} %pad_maximum_fusion.1.own), channel_id=1, source_target_pairs={{2,0},{4,2},{6,4},{8,6},{10,8},{12,10},{14,12},{16,14},{18,16},{20... | collective-permute-start | bytes 1572872 | tf_op jit(solution)/shard_map/ppermute | solution.py:224
  30.6 9.8 %collective-permute-start.3 = (bf16[128,512]{1,0:T(8,128)(2,1)S(1)}, bf16[128,512]{1,0:T(8,128)(2,1)S(1)}, u32[]{:S(2)}, u32[]{:S(2)}) collective-permute-start(bf16[128,512]{1,0:T(8,128)(2,1)S(1)} %get-tuple-element.85), channel_id=1, source_target_pairs={{0,1},{1,0},{2,3},{3,2},{4,5},{5,4},{6,7},{7,6},{8,9},{9,8},{10,11... | collective-permute-start | bytes 393224 | tf_op jit(solution)/shard_map/ppermute | solution.py:233
  31.8 20.5 %collective-permute-start.9 = (bf16[4,128,512]{2,1,0:T(8,128)(2,1)}, bf16[4,128,512]{2,1,0:T(8,128)(2,1)}, u32[]{:S(2)}, u32[]{:S(2)}) collective-permute-start(bf16[4,128,512]{2,1,0:T(8,128)(2,1)} %get-tuple-element.81), channel_id=1, source_target_pairs={{0,1},{1,0},{2,3},{3,2},{4,5},{5,4},{6,7},{7,6},{8,9},{9,8},{10,11... | collective-permute-start | bytes 1572872 | tf_op jit(solution)/shard_map/ppermute | solution.py:233
  32.9 15.7 %collective-permute-start.16 = (bf16[4,128,512]{2,1,0:T(8,128)(2,1)S(1)}, bf16[4,128,512]{2,1,0:T(8,128)(2,1)}, u32[]{:S(2)}, u32[]{:S(2)}) collective-permute-start(bf16[4,128,512]{2,1,0:T(8,128)(2,1)S(1)} %pad_maximum_fusion.3.own), channel_id=1, source_target_pairs={{0,1},{1,0},{2,3},{3,2},{4,5},{5,4},{6,7},{7,6},{8,9},{9,8},{10,11... | collective-permute-start | bytes 1572872 | tf_op jit(solution)/shard_map/ppermute | solution.py:233
  35.6 13.0 %all-to-all-start.1 = ((bf16[4,512,128]{2,1,0:T(8,128)(2,1)}), bf16[4,512,128]{2,1,0:T(8,128)(2,1)S(1)}, u32[]{:S(2)}, u32[]{:S(2)}) async-start(bf16[4,512,128]{2,1,0:T(8,128)(2,1)} %broadcast_in_dim.46), calls=%async_computation.1 | async-start | bytes 1048576 | tf_op jit(solution)/shard_map/all_to_all | solution.py:290
  40.4 17.4 %collective-permute-start.4 = (bf16[2,256,512]{2,1,0:T(8,128)(2,1)S(1)}, bf16[2,256,512]{2,1,0:T(8,128)(2,1)}, u32[]{:S(2)}, u32[]{:S(2)}) collective-permute-start(bf16[2,256,512]{2,1,0:T(8,128)(2,1)S(1)} %collective-permute-done.1.below), channel_id=1, source_target_pairs={{0,2},{2,4},{4,6},{6,8},{8,10},{10,12},{12,14},{14,16},{16,18},{18... | collective-permute-start | bytes 1572872 | tf_op jit(solution)/shard_map/ppermute | solution.py:224
  42.4 15.4 %collective-permute-start.5 = (bf16[2,256,512]{2,1,0:T(8,128)(2,1)S(1)}, bf16[2,256,512]{2,1,0:T(8,128)(2,1)}, u32[]{:S(2)}, u32[]{:S(2)}) collective-permute-start(bf16[2,256,512]{2,1,0:T(8,128)(2,1)S(1)} %collective-permute-done.2.above), channel_id=1, source_target_pairs={{2,0},{4,2},{6,4},{8,6},{10,8},{12,10},{14,12},{16,14},{18,16},{20... | collective-permute-start | bytes 1572872 | tf_op jit(solution)/shard_map/ppermute | solution.py:224
  50.5 13.4 %collective-permute-start.17 = (bf16[256,512]{1,0:T(8,128)(2,1)S(1)}, bf16[256,512]{1,0:T(8,128)(2,1)S(1)}, u32[]{:S(2)}, u32[]{:S(2)}) collective-permute-start(bf16[256,512]{1,0:T(8,128)(2,1)S(1)} %get-tuple-element.48), channel_id=1, source_target_pairs={{0,48},{16,0},{32,16},{48,32},{1,49},{17,1},{33,17},{49,33},{2,50}... | collective-permute-start | bytes 786440 | tf_op jit(solution)/shard_map/ppermute | solution.py:229
  51.8 13.3 %collective-permute-start.18 = (bf16[256,512]{1,0:T(8,128)(2,1)S(1)}, bf16[256,512]{1,0:T(8,128)(2,1)S(1)}, u32[]{:S(2)}, u32[]{:S(2)}) collective-permute-start(bf16[256,512]{1,0:T(8,128)(2,1)S(1)} %get-tuple-element.49), channel_id=1, source_target_pairs={{0,32},{16,48},{32,0},{48,16},{1,33},{17,49},{33,1},{49,17},{2,34}... | collective-permute-start | bytes 786440 | tf_op jit(solution)/shard_map/ppermute | solution.py:229
  52.3 17.3 %collective-permute-start.19 = (bf16[256,512]{1,0:T(8,128)(2,1)S(1)}, bf16[256,512]{1,0:T(8,128)(2,1)S(1)}, u32[]{:S(2)}, u32[]{:S(2)}) collective-permute-start(bf16[256,512]{1,0:T(8,128)(2,1)S(1)} %get-tuple-element.50), channel_id=1, source_target_pairs={{0,16},{16,32},{32,48},{48,0},{1,17},{17,33},{33,49},{49,1},{2,18}... | collective-permute-start | bytes 786440 | tf_op jit(solution)/shard_map/ppermute | solution.py:229
  59.3 23.8 %collective-permute-start.10 = (bf16[256,512]{1,0:T(8,128)(2,1)S(1)}, bf16[256,512]{1,0:T(8,128)(2,1)S(1)}, u32[]{:S(2)}, u32[]{:S(2)}) collective-permute-start(bf16[256,512]{1,0:T(8,128)(2,1)S(1)} %get-tuple-element.46.attended), channel_id=1, source_target_pairs={{0,64},{64,128},{128,192},{192,0},{1,65},{65,129},{129,193},{193,1... | collective-permute-start | bytes 786440 | tf_op jit(solution)/shard_map/ppermute | solution.py:229
  61.8 21.4 %collective-permute-start.11 = (bf16[256,512]{1,0:T(8,128)(2,1)S(1)}, bf16[256,512]{1,0:T(8,128)(2,1)S(1)}, u32[]{:S(2)}, u32[]{:S(2)}) collective-permute-start(bf16[256,512]{1,0:T(8,128)(2,1)S(1)} %get-tuple-element.46.attended), channel_id=1, source_target_pairs={{0,128},{64,192},{128,0},{192,64},{1,129},{65,193},{129,1},{193,65... | collective-permute-start | bytes 786440 | tf_op jit(solution)/shard_map/ppermute | solution.py:229
  63.9 19.2 %collective-permute-start.12 = (bf16[256,512]{1,0:T(8,128)(2,1)S(1)}, bf16[256,512]{1,0:T(8,128)(2,1)S(1)}, u32[]{:S(2)}, u32[]{:S(2)}) collective-permute-start(bf16[256,512]{1,0:T(8,128)(2,1)S(1)} %get-tuple-element.46.attended), channel_id=1, source_target_pairs={{0,192},{64,0},{128,64},{192,128},{1,193},{65,1},{129,65},{193,129... | collective-permute-start | bytes 786440 | tf_op jit(solution)/shard_map/ppermute | solution.py:229
  71.2 20.4 %collective-permute-start.20 = (bf16[2,256,512]{2,1,0:T(8,128)(2,1)S(1)}, bf16[2,256,512]{2,1,0:T(8,128)(2,1)S(1)}, u32[]{:S(2)}, u32[]{:S(2)}) collective-permute-start(bf16[2,256,512]{2,1,0:T(8,128)(2,1)S(1)} %get-tuple-element.58), channel_id=1, source_target_pairs={{2,0},{4,2},{6,4},{8,6},{10,8},{12,10},{14,12},{16,14},{18,16},{20... | collective-permute-start | bytes 1572872 | tf_op jit(solution)/shard_map/ppermute | solution.py:224
  81.2 16.8 %collective-permute-start.22 = (bf16[2,256,512]{2,1,0:T(8,128)(2,1)S(1)}, bf16[2,256,512]{2,1,0:T(8,128)(2,1)S(1)}, u32[]{:S(2)}, u32[]{:S(2)}) collective-permute-start(bf16[2,256,512]{2,1,0:T(8,128)(2,1)S(1)} %get-tuple-element.60), channel_id=1, source_target_pairs={{0,2},{2,4},{4,6},{6,8},{8,10},{10,12},{12,14},{14,16},{16,18},{18... | collective-permute-start | bytes 1572872 | tf_op jit(solution)/shard_map/ppermute | solution.py:224
  91.8 35.2 %collective-permute-start.21 = (bf16[2,256,512]{2,1,0:T(8,128)(2,1)S(1)}, bf16[2,256,512]{2,1,0:T(8,128)(2,1)S(1)}, u32[]{:S(2)}, u32[]{:S(2)}) collective-permute-start(bf16[2,256,512]{2,1,0:T(8,128)(2,1)S(1)} %add_convert_fusion.2), channel_id=1, source_target_pairs={{2,0},{4,2},{6,4},{8,6},{10,8},{12,10},{14,12},{16,14},{18,16},{20... | collective-permute-start | bytes 1572872 | tf_op jit(solution)/shard_map/ppermute | solution.py:224
  99.0 28.1 %collective-permute-start.23 = (bf16[2,256,512]{2,1,0:T(8,128)(2,1)}, bf16[2,256,512]{2,1,0:T(8,128)(2,1)S(1)}, u32[]{:S(2)}, u32[]{:S(2)}) collective-permute-start(bf16[2,256,512]{2,1,0:T(8,128)(2,1)} %add_convert_fusion.1), channel_id=1, source_target_pairs={{0,2},{2,4},{4,6},{6,8},{8,10},{10,12},{12,14},{14,16},{16,18},{18... | collective-permute-start | bytes 1572872 | tf_op jit(solution)/shard_map/ppermute | solution.py:224
  102.0 18.4 %collective-permute-start.25 = (bf16[128,512]{1,0:T(8,128)(2,1)S(1)}, bf16[128,512]{1,0:T(8,128)(2,1)S(1)}, u32[]{:S(2)}, u32[]{:S(2)}) collective-permute-start(bf16[128,512]{1,0:T(8,128)(2,1)S(1)} %get-tuple-element.69), channel_id=1, source_target_pairs={{0,16},{16,32},{32,48},{48,0},{1,17},{17,33},{33,49},{49,1},{2,18}... | collective-permute-start | bytes 393224 | tf_op jit(solution)/shard_map/ppermute | solution.py:229
  102.1 18.3 %collective-permute-start.26 = (bf16[128,512]{1,0:T(8,128)(2,1)S(1)}, bf16[128,512]{1,0:T(8,128)(2,1)S(1)}, u32[]{:S(2)}, u32[]{:S(2)}) collective-permute-start(bf16[128,512]{1,0:T(8,128)(2,1)S(1)} %get-tuple-element.71), channel_id=1, source_target_pairs={{0,32},{16,48},{32,0},{48,16},{1,33},{17,49},{33,1},{49,17},{2,34}... | collective-permute-start | bytes 393224 | tf_op jit(solution)/shard_map/ppermute | solution.py:229
  102.2 18.2 %collective-permute-start.27 = (bf16[128,512]{1,0:T(8,128)(2,1)S(1)}, bf16[128,512]{1,0:T(8,128)(2,1)}, u32[]{:S(2)}, u32[]{:S(2)}) collective-permute-start(bf16[128,512]{1,0:T(8,128)(2,1)S(1)} %get-tuple-element.70), channel_id=1, source_target_pairs={{0,48},{16,0},{32,16},{48,32},{1,49},{17,1},{33,17},{49,33},{2,50}... | collective-permute-start | bytes 393224 | tf_op jit(solution)/shard_map/ppermute | solution.py:229
  122.0 14.2 %all-to-all-start.2 = ((bf16[16,8,512]{2,1,0:T(8,128)(2,1)}), bf16[16,8,512]{2,1,0:T(8,128)(2,1)S(1)}, u32[]{:S(2)}, u32[]{:S(2)}) async-start(bf16[16,8,512]{2,1,0:T(8,128)(2,1)} %fusion.13), calls=%async_computation.2 | async-start | bytes 262144 | tf_op jit(solution)/shard_map/all_to_all | solution.py:340
  127.3 9.6 %collective-permute-start.24 = (bf16[3,128,512]{2,1,0:T(8,128)(2,1)S(1)}, bf16[3,128,512]{2,1,0:T(8,128)(2,1)S(1)}, u32[]{:S(2)}, u32[]{:S(2)}) collective-permute-start(bf16[3,128,512]{2,1,0:T(8,128)(2,1)S(1)} %pad_maximum_fusion.4), channel_id=1, source_target_pairs={{0,1},{1,0},{2,3},{3,2},{4,5},{5,4},{6,7},{7,6},{8,9},{9,8},{10,11... | collective-permute-start | bytes 1179656 | tf_op jit(solution)/shard_map/ppermute | solution.py:233

commit v4 on v3

--- a/solution.py
+++ b/solution.py
@@ -97,6 +97,30 @@
     key_blocks(info, offsets, body)
 
 
+def spans_kernel(place, lengths, spans, info):
+    first, core = place[0], place[1]
+    index = lax.broadcasted_iota(jnp.int32, (1, CHIP), 1)
+    swapped_index = jnp.where(index < TOK, index + TOK, index - TOK)
+    positions = first + jnp.where(core == 0, index, swapped_index)
+    start = jnp.zeros((1, CHIP), jnp.int32)
+    end = jnp.zeros((1, CHIP), jnp.int32)
+    begin, low, high = jnp.int32(0), jnp.int32(0), jnp.int32(0)
+    for image in range(lengths.shape[1]):
+        finish = begin + lengths[0, image]
+        begun = positions >= begin
+        start = jnp.where(begun, begin, start)
+        end = jnp.where(begun, finish, end)
+        low = jnp.where(first >= begin, begin, low)
+        high = jnp.where(first + CHIP - 1 >= begin, finish, high)
+        begin = finish
+    spans[0:1, :] = start
+    spans[1:2, :] = end
+    info[0] = first
+    info[1] = core
+    info[2] = low
+    info[3] = high
+
+
 def near_forward_kernel(info, spans, query, below, own, above, peak, total, acc, scores):
     windows = (below, own, above)
     peak[...] = jnp.full(peak.shape, -1e30, jnp.float32)
@@ -203,13 +227,21 @@
 WINDOW = (2, CHIP, HALF)
 
 
+def i32(*shape):
+    return jax.ShapeDtypeStruct(shape, jnp.int32)
+
+
+def memory(array):
+    scalars = array.dtype == jnp.int32 and array.shape != (2, CHIP)
+    return pl.BlockSpec(memory_space=pltpu.SMEM if scalars else pltpu.VMEM)
+
+
 def kernel(body, name, out_shape, scratch, flops, *operands):
-    specs = [pl.BlockSpec(memory_space=pltpu.SMEM)]
-    specs += [pl.BlockSpec(memory_space=pltpu.VMEM)] * (len(operands) - 1)
+    specs = [memory(x) for x in operands]
     return pl.pallas_call(
         body,
         in_specs=specs,
-        out_specs=[pl.BlockSpec(memory_space=pltpu.VMEM)] * len(out_shape),
+        out_specs=[memory(x) for x in out_shape],
         out_shape=out_shape,
         scratch_shapes=[pltpu.VMEM(shape.shape, shape.dtype) for shape in scratch],
         compiler_params=pltpu.CompilerParams(vmem_limit_bytes=16 * 1024 * 1024),
@@ -239,19 +271,6 @@
     return own, other
 
 
-def image_spans(lengths, core, first):
-    ends = jnp.cumsum(lengths)
-    starts = ends - lengths
-    place = jnp.arange(CHIP, dtype=jnp.int32)
-    positions = first + jnp.where(core == 0, place, (place + TOK) % CHIP)
-    begun = starts[:, None] <= positions[None, :]
-    open_ = ends[:, None] > positions[None, :]
-    start = jnp.max(jnp.where(begun, starts[:, None], 0), axis=0)
-    end = jnp.min(jnp.where(open_, ends[:, None], jnp.int32(2**30)), axis=0)
-    info = jnp.stack([first, core, jnp.min(start), jnp.max(end)]).astype(jnp.int32)
-    return info, jnp.stack([start, end])
-
-
 def on_device(query, keys, values, out_grad, out_weight, lengths):
     core = lax.axis_index("c")
     x, y = lax.axis_index("x"), lax.axis_index("y")
@@ -259,26 +278,30 @@
     size_x, size_y, size_z = (lax.axis_size(a) for a in ("x", "y", "z"))
     quarter = out_grad.shape[2] // size_y
 
-    own_kv, other_kv = halves(core, jnp.stack([keys[0], values[0]]))
+    own_kv, other_kv = (
+        jnp.stack(pair) for pair in zip(halves(core, keys[0]), halves(core, values[0]))
+    )
     own = jnp.concatenate([own_kv, swapped(other_kv)], axis=1)
+    own, later_grad = lax.optimization_barrier((own, out_grad[0]))
     below = to_chip(own, 1)
     above = to_chip(own, -1)
 
     own_query, other_query = halves(core, query[0])
     chip_query = jnp.concatenate([own_query, swapped(other_query)], axis=0)
-    info, spans = image_spans(lengths[0], core, chip * CHIP)
-
-    def quarters(axis, place):
+    place = jnp.stack([chip * CHIP, core]).astype(jnp.int32)
+    spans, info = kernel(spans_kernel, "spans", [i32(2, CHIP), i32(4)], [], 0, place, lengths)
+
+    def quarters(axis, place, matrix):
         def piece(distance):
             start = (place + distance) % lax.axis_size(axis) * quarter
-            return lax.dynamic_slice_in_dim(out_grad[0], start, quarter, 1)
+            return lax.dynamic_slice_in_dim(matrix, start, quarter, 1)
 
         got = [piece(0)]
         got += [along(axis, piece(d), d) for d in range(1, lax.axis_size(axis))]
         got = jnp.stack(got)
         return got, swapped(got)
 
-    mine, others = quarters("y", y)
+    mine, others = quarters("y", y, out_grad[0])
 
     rows = out_weight.shape[0]
     piece = lax.dynamic_index_in_dim(
@@ -294,7 +317,7 @@
         [bf16(quarter, HALF)], GRAD_PARTS, info, mine, others, weight,
     )
     parts = [parts[0]] + [along("y", parts[d], -d) for d in range(1, size_y)]
-    rows_grad = jnp.stack(quarters("x", x), axis=1).reshape(size_x * CHIP, quarter).T
+    rows_grad = jnp.stack(quarters("x", x, later_grad), axis=1).reshape(size_x * CHIP, quarter).T
 
     below, above, info, spans, chip_query = lax.optimization_barrier(
         (below, above, info, spans, chip_query)

time: 139 us -> 135 us (0.971)
  the two profiles are of different devices: /device:TPU:17 before, /device:TPU:13 now
where the time goes in v4:
time: 135 us; the launch traced here: 133 us
  starting transfers between devices  73.5 us (54%)
  waiting for transfers between devices  29.4 us (22%)
  Pallas kernels  14 us (10%)
  other arithmetic  7.03 us (5%)
  local copies, waits for them, and re-layouts  6.1 us (5%)
  matrix products  1.55 us (1%)
    ppermute x8, starting transfers between devices, to_chip(): return lax.ppermute(block, ('y', 'z'), route)  25.6 us
    ppermute x15, starting transfers between devices, along(): lax.ppermute(block, axis, [(i, (i + distance) % size) for i in range(size)])  18.6 us
    ppermute x15, waiting for transfers between devices, along(): lax.ppermute(block, axis, [(i, (i + distance) % size) for i in range(size)])  15.9 us
    pallas_call x6, Pallas kernels, kernel(): pl.pallas_call(body, in_specs=specs, out_specs=[memory(x) for x in out_sh...  14 us
    all_to_all x1, starting transfers between devices, on_device(): lax.all_to_all(partial.reshape(2 * size_z, -1, HALF), ('z', 'c'), 0, 0)  10.3 us
    all_to_all x1, starting transfers between devices, on_device(): lax.all_to_all(piece.reshape(2 * size_z, rows, HEAD), ('z', 'c'), 0, 0)  9.4 us
    all_to_all x1, waiting for transfers between devices, on_device(): lax.all_to_all(partial.reshape(2 * size_z, -1, HALF), ('z', 'c'), 0, 0)  8.63 us
    all_to_all x1, starting transfers between devices, on_device(): weight = lax.all_to_all(piece, 'x', 0, 0)  6.18 us
  transfers between devices with their start and end apart: 31, of which 6 were waited for; matrix products, arithmetic and copies ran while one was open for 9% of the time, Pallas kernels for 11%

profile of v4, /device:TPU:13, one launch (start us, length us, event | category | flops | bytes accessed | tf_op | source)
XLA Modules:
  0.0 132.6 jit_solution(10422667272404489670)
XLA Ops:
  0.6 1.2 constant_dynamic-slice_fusion.7
  1.8 0.0 copy-start.4
  1.9 0.8 collective-permute-start
  2.7 0.7 constant_dynamic-slice_fusion.1
  3.4 1.3 collective-permute-start.13
  4.7 0.7 collective-permute-start.14
  5.4 2.1 %collective-permute-start.15 = (bf16[128,512]{1,0:T(8,128)(2,1)S(1)}, bf16[128,512]{1,0:T(8,128)(2,1)S(1)}, u32[]{:S(2)}, u32[]{:S(2)}) collective-permute-start(bf16[128,512]{1,0:T(8,128)(2,1)S(1)} %get-tuple-element.80), channel_id=1, source_target_pairs={{0,48},{16,0},{32,16},{48,32},{1,49},{17,1},{33,17},{49,33},{2,50}... | collective-permute-start | bytes 393224 | tf_op jit(solution)/shard_map/ppermute | solution.py:261
  7.6 0.7 broadcast_in_dim.16
  8.3 9.4 %all-to-all-start = ((bf16[16,32,128]{2,1,0:T(8,128)(2,1)}), bf16[16,32,128]{2,1,0:T(8,128)(2,1)S(1)}, u32[]{:S(2)}, u32[]{:S(2)}) async-start(bf16[16,32,128]{2,1,0:T(8,128)(2,1)} %bitcast.22), calls=%async_computation | async-start | bytes 262144 | tf_op jit(solution)/shard_map/all_to_all | solution.py:311
  17.7 0.0 collective-permute-done
  17.7 0.0 copy-start.3
  17.7 3.4 %collective-permute-start.1 = (bf16[2,256,512]{2,1,0:T(8,128)(2,1)S(1)}, bf16[2,256,512]{2,1,0:T(8,128)(2,1)S(1)}, u32[]{:S(2)}, u32[]{:S(2)}) collective-permute-start(bf16[2,256,512]{2,1,0:T(8,128)(2,1)S(1)} %pad_maximum_fusion.1.own), channel_id=1, source_target_pairs={{0,2},{2,4},{4,6},{6,8},{8,10},{10,12},{12,14},{14,16},{16,18},{18... | collective-permute-start | bytes 1572872 | tf_op jit(solution)/shard_map/ppermute | solution.py:256
  21.2 4.1 %collective-permute-start.2 = (bf16[2,256,512]{2,1,0:T(8,128)(2,1)S(1)}, bf16[2,256,512]{2,1,0:T(8,128)(2,1)S(1)}, u32[]{:S(2)}, u32[]{:S(2)}) collective-permute-start(bf16[2,256,512]{2,1,0:T(8,128)(2,1)S(1)} %pad_maximum_fusion.1.own), channel_id=1, source_target_pairs={{2,0},{4,2},{6,4},{8,6},{10,8},{12,10},{14,12},{16,14},{18,16},{20... | collective-permute-start | bytes 1572872 | tf_op jit(solution)/shard_map/ppermute | solution.py:256
  25.3 0.8 dynamic-slice_bitcast_fusion.6
  26.1 0.9 collective-permute-start.6
  27.0 0.5 collective-permute-start.7
  27.5 0.9 collective-permute-start.8
  28.4 0.7 dynamic-slice_bitcast_fusion.8
  29.0 0.1 pad_maximum_fusion.3.own
  29.1 0.9 broadcast_in_dim.18
  30.0 6.2 %all-to-all-start.1 = ((bf16[4,512,128]{2,1,0:T(8,128)(2,1)}), bf16[4,512,128]{2,1,0:T(8,128)(2,1)S(1)}, u32[]{:S(2)}, u32[]{:S(2)}) async-start(bf16[4,512,128]{2,1,0:T(8,128)(2,1)} %broadcast_in_dim.18), calls=%async_computation.1 | async-start | bytes 1048576 | tf_op jit(solution)/shard_map/all_to_all | solution.py:313
  36.2 1.8 %collective-permute-start.3 = (bf16[128,512]{1,0:T(8,128)(2,1)}, bf16[128,512]{1,0:T(8,128)(2,1)S(1)}, u32[]{:S(2)}, u32[]{:S(2)}) collective-permute-start(bf16[128,512]{1,0:T(8,128)(2,1)} %get-tuple-element.89), channel_id=1, source_target_pairs={{0,1},{1,0},{2,3},{3,2},{4,5},{5,4},{6,7},{7,6},{8,9},{9,8},{10,11... | collective-permute-start | bytes 393224 | tf_op jit(solution)/shard_map/ppermute | solution.py:265
  38.0 0.1 collective-permute-start.16
  38.1 1.1 fusion.15
  39.2 0.4 collective-permute-start.9
  39.6 0.1 pad_add_fusion.place
  39.7 1.2 spans.1
  40.9 1.9 %collective-permute-start.4 = (bf16[2,256,512]{2,1,0:T(8,128)(2,1)S(1)}, bf16[2,256,512]{2,1,0:T(8,128)(2,1)}, u32[]{:S(2)}, u32[]{:S(2)}) collective-permute-start(bf16[2,256,512]{2,1,0:T(8,128)(2,1)S(1)} %collective-permute-done.1.below), channel_id=1, source_target_pairs={{0,2},{2,4},{4,6},{6,8},{8,10},{10,12},{12,14},{14,16},{16,18},{18... | collective-permute-start | bytes 1572872 | tf_op jit(solution)/shard_map/ppermute | solution.py:256
  42.9 5.5 %collective-permute-start.5 = (bf16[2,256,512]{2,1,0:T(8,128)(2,1)S(1)}, bf16[2,256,512]{2,1,0:T(8,128)(2,1)}, u32[]{:S(2)}, u32[]{:S(2)}) collective-permute-start(bf16[2,256,512]{2,1,0:T(8,128)(2,1)S(1)} %collective-permute-done.2.above), channel_id=1, source_target_pairs={{2,0},{4,2},{6,4},{8,6},{10,8},{12,10},{14,12},{16,14},{18,16},{20... | collective-permute-start | bytes 1572872 | tf_op jit(solution)/shard_map/ppermute | solution.py:256
  48.4 1.8 %grad_parts.1 = (bf16[256,512]{1,0:T(8,128)(2,1)S(1)}, bf16[256,512]{1,0:T(8,128)(2,1)S(1)}, bf16[256,512]{1,0:T(8,128)(2,1)S(1)}, bf16[256,512]{1,0:T(8,128)(2,1)S(1)}) custom-call(s32[4]{0:T(128)S(1)} %get-tuple-element.40.info, bf16[4,128,512]{2,1,0:T(8,128)(2,1)S(1)} %pad_maximum_fusion.3.own, bf16[4,128,512]{2,1,0:T(8,128)(2,1)} %collective-permute-done.16.other, ...), custom_call_target="tpu_custom_call" | custom-call | tf_op jit(solution)/shard_map/grad_parts/pallas_call | solution.py:241
  50.2 0.1 collective-permute-start.17
  50.3 1.3 collective-permute-start.18
  51.6 2.6 %near_forward.1 = (f32[4,8,256]{2,1,0:T(8,128)S(1)}, f32[4,8,256]{2,1,0:T(8,128)S(1)}, f32[4,128,256]{2,1,0:T(8,128)S(1)}) custom-call(s32[4]{0:T(128)S(1)} %get-tuple-element.40.info, s32[2,256]{1,0:T(2,128)S(1)} %get-tuple-element.41.spans, bf16[256,512]{1,0:T(8,128)(2,1)S(1)} %pad_maximum_fusion.7.query, ...), custom_call_target="tpu_custom_call" | custom-call | flops 2013265920 | tf_op jit(solution)/shard_map/near_forward/pallas_call | solution.py:241
  54.2 1.9 %collective-permute-start.19 = (bf16[256,512]{1,0:T(8,128)(2,1)S(1)}, bf16[256,512]{1,0:T(8,128)(2,1)S(1)}, u32[]{:S(2)}, u32[]{:S(2)}) collective-permute-start(bf16[256,512]{1,0:T(8,128)(2,1)S(1)} %get-tuple-element.58), channel_id=1, source_target_pairs={{0,16},{16,32},{32,48},{48,0},{1,17},{17,33},{33,49},{49,1},{2,18}... | collective-permute-start | bytes 786440 | tf_op jit(solution)/shard_map/ppermute | solution.py:261
  56.1 1.1 pad_maximum_fusion
  57.2 1.3 %collective-permute-done.4.below = bf16[2,256,512]{2,1,0:T(8,128)(2,1)} collective-permute-done((bf16[2,256,512]{2,1,0:T(8,128)(2,1)S(1)}, bf16[2,256,512]{2,1,0:T(8,128)(2,1)}, u32[]{:S(2)}, u32[]{:S(2)}) %collective-permute-start.4) | collective-permute-done | bytes 524320 | tf_op jit(solution)/shard_map/ppermute | solution.py:256
  58.6 0.8 collective-permute-done.5.above
  59.3 1.5 %far_forward.1 = (bf16[256,512]{1,0:T(8,128)(2,1)S(1)}, f32[4,1,256]{2,1,0:T(1,128)S(1)}) custom-call(s32[4]{0:T(128)S(1)} %get-tuple-element.40.info, s32[2,256]{1,0:T(2,128)S(1)} %get-tuple-element.41.spans, bf16[256,512]{1,0:T(8,128)(2,1)S(1)} %pad_maximum_fusion.7.query, bf16[2,256,512]{2,1,0:T(8,128)(2,1)} %collective-permute-done.4.below, ...), custom_call_target="tpu_custom_call" | custom-call | flops 2684354560 | tf_op jit(solution)/shard_map/far_forward/pallas_call | solution.py:241
  60.8 1.0 collective-permute-start.10
  61.8 0.6 collective-permute-start.11
  62.4 0.7 collective-permute-start.12
  63.1 7.0 %collective-permute-done.19.rest_3_ = bf16[256,512]{1,0:T(8,128)(2,1)S(1)} collective-permute-done((bf16[256,512]{1,0:T(8,128)(2,1)S(1)}, bf16[256,512]{1,0:T(8,128)(2,1)S(1)}, u32[]{:S(2)}, u32[]{:S(2)}) %collective-permute-start.19) | collective-permute-done | bytes 262176 | tf_op jit(solution)/shard_map/ppermute | solution.py:261
  70.1 1.6 %far_backward.1 = (bf16[256,512]{1,0:T(8,128)(2,1)S(1)}, f32[4,1,256]{2,1,0:T(1,128)S(1)}, f32[4,128,256]{2,1,0:T(8,128)S(1)}, bf16[2,256,512]{2,1,0:T(8,128)(2,1)S(1)}, bf16[2,256,512]{2,1,0:T(8,128)(2,1)S(1)}) custom-call(s32[4]{0:T(128)S(1)} %get-tuple-element.40.info, s32[2,256]{1,0:T(2,128)S(1)} %get-tuple-element.41.spans, ...), custom_call_target="tpu_custom_call" | custom-call | tf_op jit(solution)/shard_map/far_backward/pallas_call | solution.py:241
  71.7 1.9 %collective-permute-start.20 = (bf16[2,256,512]{2,1,0:T(8,128)(2,1)S(1)}, bf16[2,256,512]{2,1,0:T(8,128)(2,1)S(1)}, u32[]{:S(2)}, u32[]{:S(2)}) collective-permute-start(bf16[2,256,512]{2,1,0:T(8,128)(2,1)S(1)} %get-tuple-element.66), channel_id=1, source_target_pairs={{2,0},{4,2},{6,4},{8,6},{10,8},{12,10},{14,12},{16,14},{18,16},{20... | collective-permute-start | bytes 1572872 | tf_op jit(solution)/shard_map/ppermute | solution.py:256
  73.6 3.4 %collective-permute-start.22 = (bf16[2,256,512]{2,1,0:T(8,128)(2,1)S(1)}, bf16[2,256,512]{2,1,0:T(8,128)(2,1)S(1)}, u32[]{:S(2)}, u32[]{:S(2)}) collective-permute-start(bf16[2,256,512]{2,1,0:T(8,128)(2,1)S(1)} %get-tuple-element.68), channel_id=1, source_target_pairs={{0,2},{2,4},{4,6},{6,8},{8,10},{10,12},{12,14},{14,16},{16,18},{18... | collective-permute-start | bytes 1572872 | tf_op jit(solution)/shard_map/ppermute | solution.py:256
  77.0 1.6 %convolution_convert_fusion = bf16[512,512]{1,0:T(8,128)(2,1)} fusion(bf16[512,1024]{0,1:T(8,128)(2,1)S(1)} %bitcast.59, bf16[256,512]{1,0:T(8,128)(2,1)S(1)} %collective-permute-done.12, bf16[256,512]{1,0:T(8,128)(2,1)S(1)} %collective-permute-done.11, bf16[256,512]{1,0:T(8,128)(2,1)S(1)} %collective-permute-done.10, ...), kind=kOutput, calls=%fused_computation | convolution fusion | flops 541327360 | bytes 2621440 | tf_op jit(solution)/shard_map/dot_general | solution.py:34
  78.6 5.3 %near_backward.1 = (bf16[256,512]{1,0:T(8,128)(2,1)S(1)}, bf16[2,256,512]{2,1,0:T(8,128)(2,1)S(1)}, f32[2,256,512]{2,1,0:T(8,128)S(1)}, bf16[2,256,512]{2,1,0:T(8,128)(2,1)S(1)}) custom-call(s32[4]{0:T(128)S(1)} %get-tuple-element.40.info, s32[2,256]{1,0:T(2,128)S(1)} %get-tuple-element.41.spans, bf16[256,512]{1,0:T(8,128)(2,1)S(1)} %pad_maximum_fusion.7.query, ...), custom_call_target="tpu_custom_call" | custom-call | tf_op jit(solution)/shard_map/near_backward/pallas_call | solution.py:241
  83.8 2.7 %collective-permute-done.20 = bf16[2,256,512]{2,1,0:T(8,128)(2,1)S(1)} collective-permute-done((bf16[2,256,512]{2,1,0:T(8,128)(2,1)S(1)}, bf16[2,256,512]{2,1,0:T(8,128)(2,1)S(1)}, u32[]{:S(2)}, u32[]{:S(2)}) %collective-permute-start.20) | collective-permute-done | bytes 524320 | tf_op jit(solution)/shard_map/ppermute | solution.py:256
  86.6 0.1 add_convert_fusion.2
  86.7 3.5 %collective-permute-start.21 = (bf16[2,256,512]{2,1,0:T(8,128)(2,1)S(1)}, bf16[2,256,512]{2,1,0:T(8,128)(2,1)S(1)}, u32[]{:S(2)}, u32[]{:S(2)}) collective-permute-start(bf16[2,256,512]{2,1,0:T(8,128)(2,1)S(1)} %add_convert_fusion.2), channel_id=1, source_target_pairs={{2,0},{4,2},{6,4},{8,6},{10,8},{12,10},{14,12},{16,14},{18,16},{20... | collective-permute-start | bytes 1572872 | tf_op jit(solution)/shard_map/ppermute | solution.py:256
  90.2 0.9 add_convert_fusion.1
  91.1 1.9 %collective-permute-start.23 = (bf16[2,256,512]{2,1,0:T(8,128)(2,1)}, bf16[2,256,512]{2,1,0:T(8,128)(2,1)S(1)}, u32[]{:S(2)}, u32[]{:S(2)}) collective-permute-start(bf16[2,256,512]{2,1,0:T(8,128)(2,1)} %add_convert_fusion.1), channel_id=1, source_target_pairs={{0,2},{2,4},{4,6},{6,8},{8,10},{10,12},{12,14},{14,16},{16,18},{18... | collective-permute-start | bytes 1572872 | tf_op jit(solution)/shard_map/ppermute | solution.py:256
  93.1 1.1 dynamic-slice_bitcast_fusion.2
  94.2 4.8 %collective-permute-start.25 = (bf16[128,512]{1,0:T(8,128)(2,1)S(1)}, bf16[128,512]{1,0:T(8,128)(2,1)S(1)}, u32[]{:S(2)}, u32[]{:S(2)}) collective-permute-start(bf16[128,512]{1,0:T(8,128)(2,1)S(1)} %get-tuple-element.75), channel_id=1, source_target_pairs={{0,16},{16,32},{32,48},{48,0},{1,17},{17,33},{33,49},{49,1},{2,18}... | collective-permute-start | bytes 393224 | tf_op jit(solution)/shard_map/ppermute | solution.py:261
  99.0 1.9 %collective-permute-start.27 = (bf16[128,512]{1,0:T(8,128)(2,1)S(1)}, bf16[128,512]{1,0:T(8,128)(2,1)}, u32[]{:S(2)}, u32[]{:S(2)}) collective-permute-start(bf16[128,512]{1,0:T(8,128)(2,1)S(1)} %get-tuple-element.76), channel_id=1, source_target_pairs={{0,48},{16,0},{32,16},{48,32},{1,49},{17,1},{33,17},{49,33},{2,50}... | collective-permute-start | bytes 393224 | tf_op jit(solution)/shard_map/ppermute | solution.py:261
  100.9 8.8 %collective-permute-done.25 = bf16[128,512]{1,0:T(8,128)(2,1)S(1)} collective-permute-done((bf16[128,512]{1,0:T(8,128)(2,1)S(1)}, bf16[128,512]{1,0:T(8,128)(2,1)S(1)}, u32[]{:S(2)}, u32[]{:S(2)}) %collective-permute-start.25) | collective-permute-done | bytes 131104 | tf_op jit(solution)/shard_map/ppermute | solution.py:261
  109.7 1.7 %fusion.13 = bf16[16,8,512]{2,1,0:T(8,128)(2,1)} fusion(bf16[128,512]{1,0:T(8,128)(2,1)} %collective-permute-done.27, bf16[128,512]{1,0:T(8,128)(2,1)S(1)} %collective-permute-done.26, bf16[128,512]{1,0:T(8,128)(2,1)S(1)} %collective-permute-done.25, bf16[4,128,512]{2,1,0:T(8,128)(2,1)} %bitcast.63, s32[]{:T(128)S(6)} %select_n.128), kind=kLoop, calls=%fused_computation.35 | loop fusion | flops 524288 | bytes 655364 | tf_op jit(solution)/shard_map/reshape | solution.py:363
  111.4 10.3 %all-to-all-start.2 = ((bf16[16,8,512]{2,1,0:T(8,128)(2,1)}), bf16[16,8,512]{2,1,0:T(8,128)(2,1)S(1)}, u32[]{:S(2)}, u32[]{:S(2)}) async-start(bf16[16,8,512]{2,1,0:T(8,128)(2,1)} %fusion.13), calls=%async_computation.2 | async-start | bytes 262144 | tf_op jit(solution)/shard_map/all_to_all | solution.py:363
  121.7 0.2 add_convert_fusion
  122.0 0.3 collective-permute-start.24
  122.3 8.6 %all-to-all-done.2 = bf16[16,8,512]{2,1,0:T(8,128)(2,1)S(1)} async-done(((bf16[16,8,512]{2,1,0:T(8,128)(2,1)}), bf16[16,8,512]{2,1,0:T(8,128)(2,1)S(1)}, u32[]{:S(2)}, u32[]{:S(2)}) %all-to-all-start.2) | async-done | bytes 131104 | tf_op jit(solution)/shard_map/all_to_all | solution.py:363
  131.0 0.6 pad_maximum_fusion.8
  131.6 0.1 broadcast_select_fusion
  131.7 0.9 pad_maximum_fusion.5
  (42 shorter events, 0.3 us)
Async XLA Ops:
  0.6 2.0 %copy-start.1 = (bf16[1,128,2048]{2,1,0:T(8,128)(2,1)S(1)}, bf16[1,128,2048]{2,1,0:T(8,128)(2,1)}, u32[]{:S(2)}) copy-start(bf16[1,128,2048]{2,1,0:T(8,128)(2,1)} %param.9) | copy-start | bytes 1572868
  1.8 5.7 %copy-start.4 = (bf16[32,1024]{1,0:T(8,128)(2,1)S(1)}, bf16[32,1024]{1,0:T(8,128)(2,1)}, u32[]{:S(2)}) copy-start(bf16[32,1024]{1,0:T(8,128)(2,1)} %param.10) | copy-start | bytes 196612
  1.9 15.8 %collective-permute-start = (bf16[2,128,512]{2,1,0:T(8,128)(2,1)S(1)}, bf16[2,128,512]{2,1,0:T(8,128)(2,1)S(1)}, u32[]{:S(2)}, u32[]{:S(2)}) collective-permute-start(bf16[2,128,512]{2,1,0:T(8,128)(2,1)S(1)} %pad_maximum_fusion.6), channel_id=1, source_target_pairs={{0,1},{1,0},{2,3},{3,2},{4,5},{5,4},{6,7},{7,6},{8,9},{9,8},{10,11... | collective-permute-start | bytes 786440 | tf_op jit(solution)/shard_map/ppermute | solution.py:265
  3.4 22.7 %collective-permute-start.13 = (bf16[128,512]{1,0:T(8,128)(2,1)}, bf16[128,512]{1,0:T(8,128)(2,1)S(1)}, u32[]{:S(2)}, u32[]{:S(2)}) collective-permute-start(bf16[128,512]{1,0:T(8,128)(2,1)} %get-tuple-element.79), channel_id=1, source_target_pairs={{0,16},{16,32},{32,48},{48,0},{1,17},{17,33},{33,49},{49,1},{2,18}... | collective-permute-start | bytes 393224 | tf_op jit(solution)/shard_map/ppermute | solution.py:261
  4.7 22.3 %collective-permute-start.14 = (bf16[128,512]{1,0:T(8,128)(2,1)}, bf16[128,512]{1,0:T(8,128)(2,1)S(1)}, u32[]{:S(2)}, u32[]{:S(2)}) collective-permute-start(bf16[128,512]{1,0:T(8,128)(2,1)} %get-tuple-element.81), channel_id=1, source_target_pairs={{0,32},{16,48},{32,0},{48,16},{1,33},{17,49},{33,1},{49,17},{2,34}... | collective-permute-start | bytes 393224 | tf_op jit(solution)/shard_map/ppermute | solution.py:261
  5.4 22.1 %collective-permute-start.15 = (bf16[128,512]{1,0:T(8,128)(2,1)S(1)}, bf16[128,512]{1,0:T(8,128)(2,1)S(1)}, u32[]{:S(2)}, u32[]{:S(2)}) collective-permute-start(bf16[128,512]{1,0:T(8,128)(2,1)S(1)} %get-tuple-element.80), channel_id=1, source_target_pairs={{0,48},{16,0},{32,16},{48,32},{1,49},{17,1},{33,17},{49,33},{2,50}... | collective-permute-start | bytes 393224 | tf_op jit(solution)/shard_map/ppermute | solution.py:261
  8.3 20.8 %all-to-all-start = ((bf16[16,32,128]{2,1,0:T(8,128)(2,1)}), bf16[16,32,128]{2,1,0:T(8,128)(2,1)S(1)}, u32[]{:S(2)}, u32[]{:S(2)}) async-start(bf16[16,32,128]{2,1,0:T(8,128)(2,1)} %bitcast.22), calls=%async_computation | async-start | bytes 262144 | tf_op jit(solution)/shard_map/all_to_all | solution.py:311
  17.7 10.7 %copy-start.3 = (bf16[1,128,1024]{2,1,0:T(8,128)(2,1)S(1)}, bf16[1,128,1024]{2,1,0:T(8,128)(2,1)}, u32[]{:S(2)}) copy-start(bf16[1,128,1024]{2,1,0:T(8,128)(2,1)} %param.6) | copy-start | bytes 786436
  17.7 23.2 %collective-permute-start.1 = (bf16[2,256,512]{2,1,0:T(8,128)(2,1)S(1)}, bf16[2,256,512]{2,1,0:T(8,128)(2,1)S(1)}, u32[]{:S(2)}, u32[]{:S(2)}) collective-permute-start(bf16[2,256,512]{2,1,0:T(8,128)(2,1)S(1)} %pad_maximum_fusion.1.own), channel_id=1, source_target_pairs={{0,2},{2,4},{4,6},{6,8},{8,10},{10,12},{12,14},{14,16},{16,18},{18... | collective-permute-start | bytes 1572872 | tf_op jit(solution)/shard_map/ppermute | solution.py:256
  21.2 19.8 %collective-permute-start.2 = (bf16[2,256,512]{2,1,0:T(8,128)(2,1)S(1)}, bf16[2,256,512]{2,1,0:T(8,128)(2,1)S(1)}, u32[]{:S(2)}, u32[]{:S(2)}) collective-permute-start(bf16[2,256,512]{2,1,0:T(8,128)(2,1)S(1)} %pad_maximum_fusion.1.own), channel_id=1, source_target_pairs={{2,0},{4,2},{6,4},{8,6},{10,8},{12,10},{14,12},{16,14},{18,16},{20... | collective-permute-start | bytes 1572872 | tf_op jit(solution)/shard_map/ppermute | solution.py:256
  26.1 10.1 %collective-permute-start.6 = (bf16[128,512]{1,0:T(8,128)(2,1)}, bf16[128,512]{1,0:T(8,128)(2,1)S(1)}, u32[]{:S(2)}, u32[]{:S(2)}) collective-permute-start(bf16[128,512]{1,0:T(8,128)(2,1)} %get-tuple-element.87), channel_id=1, source_target_pairs={{0,64},{64,128},{128,192},{192,0},{1,65},{65,129},{129,193},{193,1... | collective-permute-start | bytes 393224 | tf_op jit(solution)/shard_map/ppermute | solution.py:261
  27.0 11.0 %collective-permute-start.7 = (bf16[128,512]{1,0:T(8,128)(2,1)}, bf16[128,512]{1,0:T(8,128)(2,1)S(1)}, u32[]{:S(2)}, u32[]{:S(2)}) collective-permute-start(bf16[128,512]{1,0:T(8,128)(2,1)} %get-tuple-element.86), channel_id=1, source_target_pairs={{0,128},{64,192},{128,0},{192,64},{1,129},{65,193},{129,1},{193,65... | collective-permute-start | bytes 393224 | tf_op jit(solution)/shard_map/ppermute | solution.py:261
  27.5 10.6 %collective-permute-start.8 = (bf16[128,512]{1,0:T(8,128)(2,1)}, bf16[128,512]{1,0:T(8,128)(2,1)S(1)}, u32[]{:S(2)}, u32[]{:S(2)}) collective-permute-start(bf16[128,512]{1,0:T(8,128)(2,1)} %get-tuple-element.85), channel_id=1, source_target_pairs={{0,192},{64,0},{128,64},{192,128},{1,193},{65,1},{129,65},{193,129... | collective-permute-start | bytes 393224 | tf_op jit(solution)/shard_map/ppermute | solution.py:261
  30.0 18.4 %all-to-all-start.1 = ((bf16[4,512,128]{2,1,0:T(8,128)(2,1)}), bf16[4,512,128]{2,1,0:T(8,128)(2,1)S(1)}, u32[]{:S(2)}, u32[]{:S(2)}) async-start(bf16[4,512,128]{2,1,0:T(8,128)(2,1)} %broadcast_in_dim.18), calls=%async_computation.1 | async-start | bytes 1048576 | tf_op jit(solution)/shard_map/all_to_all | solution.py:313
  36.2 3.5 %copy-start = (s32[1,32]{1,0:T(1,128)S(1)}, s32[1,32]{1,0:T(1,128)}, u32[]{:S(2)}) copy-start(s32[1,32]{1,0:T(1,128)} %lengths.1) | copy-start | bytes 388
  36.2 4.7 %collective-permute-start.3 = (bf16[128,512]{1,0:T(8,128)(2,1)}, bf16[128,512]{1,0:T(8,128)(2,1)S(1)}, u32[]{:S(2)}, u32[]{:S(2)}) collective-permute-start(bf16[128,512]{1,0:T(8,128)(2,1)} %get-tuple-element.89), channel_id=1, source_target_pairs={{0,1},{1,0},{2,3},{3,2},{4,5},{5,4},{6,7},{7,6},{8,9},{9,8},{10,11... | collective-permute-start | bytes 393224 | tf_op jit(solution)/shard_map/ppermute | solution.py:265
  38.0 10.4 %collective-permute-start.16 = (bf16[4,128,512]{2,1,0:T(8,128)(2,1)S(1)}, bf16[4,128,512]{2,1,0:T(8,128)(2,1)}, u32[]{:S(2)}, u32[]{:S(2)}) collective-permute-start(bf16[4,128,512]{2,1,0:T(8,128)(2,1)S(1)} %pad_maximum_fusion.3.own), channel_id=1, source_target_pairs={{0,1},{1,0},{2,3},{3,2},{4,5},{5,4},{6,7},{7,6},{8,9},{9,8},{10,11... | collective-permute-start | bytes 1572872 | tf_op jit(solution)/shard_map/ppermute | solution.py:265
  39.2 15.0 %collective-permute-start.9 = (bf16[4,128,512]{2,1,0:T(8,128)(2,1)}, bf16[4,128,512]{2,1,0:T(8,128)(2,1)}, u32[]{:S(2)}, u32[]{:S(2)}) collective-permute-start(bf16[4,128,512]{2,1,0:T(8,128)(2,1)} %get-tuple-element.83), channel_id=1, source_target_pairs={{0,1},{1,0},{2,3},{3,2},{4,5},{5,4},{6,7},{7,6},{8,9},{9,8},{10,11... | collective-permute-start | bytes 1572872 | tf_op jit(solution)/shard_map/ppermute | solution.py:265
  40.9 17.6 %collective-permute-start.4 = (bf16[2,256,512]{2,1,0:T(8,128)(2,1)S(1)}, bf16[2,256,512]{2,1,0:T(8,128)(2,1)}, u32[]{:S(2)}, u32[]{:S(2)}) collective-permute-start(bf16[2,256,512]{2,1,0:T(8,128)(2,1)S(1)} %collective-permute-done.1.below), channel_id=1, source_target_pairs={{0,2},{2,4},{4,6},{6,8},{8,10},{10,12},{12,14},{14,16},{16,18},{18... | collective-permute-start | bytes 1572872 | tf_op jit(solution)/shard_map/ppermute | solution.py:256
  42.9 16.5 %collective-permute-start.5 = (bf16[2,256,512]{2,1,0:T(8,128)(2,1)S(1)}, bf16[2,256,512]{2,1,0:T(8,128)(2,1)}, u32[]{:S(2)}, u32[]{:S(2)}) collective-permute-start(bf16[2,256,512]{2,1,0:T(8,128)(2,1)S(1)} %collective-permute-done.2.above), channel_id=1, source_target_pairs={{2,0},{4,2},{6,4},{8,6},{10,8},{12,10},{14,12},{16,14},{18,16},{20... | collective-permute-start | bytes 1572872 | tf_op jit(solution)/shard_map/ppermute | solution.py:256
  50.2 12.1 %collective-permute-start.17 = (bf16[256,512]{1,0:T(8,128)(2,1)S(1)}, bf16[256,512]{1,0:T(8,128)(2,1)S(1)}, u32[]{:S(2)}, u32[]{:S(2)}) collective-permute-start(bf16[256,512]{1,0:T(8,128)(2,1)S(1)} %get-tuple-element.56), channel_id=1, source_target_pairs={{0,48},{16,0},{32,16},{48,32},{1,49},{17,1},{33,17},{49,33},{2,50}... | collective-permute-start | bytes 786440 | tf_op jit(solution)/shard_map/ppermute | solution.py:261
  50.3 5.8 %copy-start.2 = (bf16[4,1,128,512]{3,2,1,0:T(8,128)(2,1)S(1)}, bf16[4,1,128,512]{3,2,1,0:T(8,128)(2,1)}, u32[]{:S(2)}) copy-start(bf16[4,1,128,512]{3,2,1,0:T(8,128)(2,1)} %get-tuple-element.82) | copy-start | bytes 1572868
  50.3 12.7 %collective-permute-start.18 = (bf16[256,512]{1,0:T(8,128)(2,1)S(1)}, bf16[256,512]{1,0:T(8,128)(2,1)S(1)}, u32[]{:S(2)}, u32[]{:S(2)}) collective-permute-start(bf16[256,512]{1,0:T(8,128)(2,1)S(1)} %get-tuple-element.57), channel_id=1, source_target_pairs={{0,32},{16,48},{32,0},{48,16},{1,33},{17,49},{33,1},{49,17},{2,34}... | collective-permute-start | bytes 786440 | tf_op jit(solution)/shard_map/ppermute | solution.py:261
  54.2 15.8 %collective-permute-start.19 = (bf16[256,512]{1,0:T(8,128)(2,1)S(1)}, bf16[256,512]{1,0:T(8,128)(2,1)S(1)}, u32[]{:S(2)}, u32[]{:S(2)}) collective-permute-start(bf16[256,512]{1,0:T(8,128)(2,1)S(1)} %get-tuple-element.58), channel_id=1, source_target_pairs={{0,16},{16,32},{32,48},{48,0},{1,17},{17,33},{33,49},{49,1},{2,18}... | collective-permute-start | bytes 786440 | tf_op jit(solution)/shard_map/ppermute | solution.py:261
  60.8 16.2 %collective-permute-start.10 = (bf16[256,512]{1,0:T(8,128)(2,1)S(1)}, bf16[256,512]{1,0:T(8,128)(2,1)S(1)}, u32[]{:S(2)}, u32[]{:S(2)}) collective-permute-start(bf16[256,512]{1,0:T(8,128)(2,1)S(1)} %get-tuple-element.54.attended), channel_id=1, source_target_pairs={{0,64},{64,128},{128,192},{192,0},{1,65},{65,129},{129,193},{193,1... | collective-permute-start | bytes 786440 | tf_op jit(solution)/shard_map/ppermute | solution.py:261
  61.8 15.2 %collective-permute-start.11 = (bf16[256,512]{1,0:T(8,128)(2,1)S(1)}, bf16[256,512]{1,0:T(8,128)(2,1)S(1)}, u32[]{:S(2)}, u32[]{:S(2)}) collective-permute-start(bf16[256,512]{1,0:T(8,128)(2,1)S(1)} %get-tuple-element.54.attended), channel_id=1, source_target_pairs={{0,128},{64,192},{128,0},{192,64},{1,129},{65,193},{129,1},{193,65... | collective-permute-start | bytes 786440 | tf_op jit(solution)/shard_map/ppermute | solution.py:261
  62.4 14.6 %collective-permute-start.12 = (bf16[256,512]{1,0:T(8,128)(2,1)S(1)}, bf16[256,512]{1,0:T(8,128)(2,1)S(1)}, u32[]{:S(2)}, u32[]{:S(2)}) collective-permute-start(bf16[256,512]{1,0:T(8,128)(2,1)S(1)} %get-tuple-element.54.attended), channel_id=1, source_target_pairs={{0,192},{64,0},{128,64},{192,128},{1,193},{65,1},{129,65},{193,129... | collective-permute-start | bytes 786440 | tf_op jit(solution)/shard_map/ppermute | solution.py:261
  71.7 14.9 %collective-permute-start.20 = (bf16[2,256,512]{2,1,0:T(8,128)(2,1)S(1)}, bf16[2,256,512]{2,1,0:T(8,128)(2,1)S(1)}, u32[]{:S(2)}, u32[]{:S(2)}) collective-permute-start(bf16[2,256,512]{2,1,0:T(8,128)(2,1)S(1)} %get-tuple-element.66), channel_id=1, source_target_pairs={{2,0},{4,2},{6,4},{8,6},{10,8},{12,10},{14,12},{16,14},{18,16},{20... | collective-permute-start | bytes 1572872 | tf_op jit(solution)/shard_map/ppermute | solution.py:256
  73.6 16.6 %collective-permute-start.22 = (bf16[2,256,512]{2,1,0:T(8,128)(2,1)S(1)}, bf16[2,256,512]{2,1,0:T(8,128)(2,1)S(1)}, u32[]{:S(2)}, u32[]{:S(2)}) collective-permute-start(bf16[2,256,512]{2,1,0:T(8,128)(2,1)S(1)} %get-tuple-element.68), channel_id=1, source_target_pairs={{0,2},{2,4},{4,6},{6,8},{8,10},{10,12},{12,14},{14,16},{16,18},{18... | collective-permute-start | bytes 1572872 | tf_op jit(solution)/shard_map/ppermute | solution.py:256
  86.7 35.0 %collective-permute-start.21 = (bf16[2,256,512]{2,1,0:T(8,128)(2,1)S(1)}, bf16[2,256,512]{2,1,0:T(8,128)(2,1)S(1)}, u32[]{:S(2)}, u32[]{:S(2)}) collective-permute-start(bf16[2,256,512]{2,1,0:T(8,128)(2,1)S(1)} %add_convert_fusion.2), channel_id=1, source_target_pairs={{2,0},{4,2},{6,4},{8,6},{10,8},{12,10},{14,12},{16,14},{18,16},{20... | collective-permute-start | bytes 1572872 | tf_op jit(solution)/shard_map/ppermute | solution.py:256
  91.1 30.6 %collective-permute-start.23 = (bf16[2,256,512]{2,1,0:T(8,128)(2,1)}, bf16[2,256,512]{2,1,0:T(8,128)(2,1)S(1)}, u32[]{:S(2)}, u32[]{:S(2)}) collective-permute-start(bf16[2,256,512]{2,1,0:T(8,128)(2,1)} %add_convert_fusion.1), channel_id=1, source_target_pairs={{0,2},{2,4},{4,6},{6,8},{8,10},{10,12},{12,14},{14,16},{16,18},{18... | collective-permute-start | bytes 1572872 | tf_op jit(solution)/shard_map/ppermute | solution.py:256
  94.2 15.5 %collective-permute-start.25 = (bf16[128,512]{1,0:T(8,128)(2,1)S(1)}, bf16[128,512]{1,0:T(8,128)(2,1)S(1)}, u32[]{:S(2)}, u32[]{:S(2)}) collective-permute-start(bf16[128,512]{1,0:T(8,128)(2,1)S(1)} %get-tuple-element.75), channel_id=1, source_target_pairs={{0,16},{16,32},{32,48},{48,0},{1,17},{17,33},{33,49},{49,1},{2,18}... | collective-permute-start | bytes 393224 | tf_op jit(solution)/shard_map/ppermute | solution.py:261
  99.0 10.7 %collective-permute-start.26 = (bf16[128,512]{1,0:T(8,128)(2,1)S(1)}, bf16[128,512]{1,0:T(8,128)(2,1)S(1)}, u32[]{:S(2)}, u32[]{:S(2)}) collective-permute-start(bf16[128,512]{1,0:T(8,128)(2,1)S(1)} %get-tuple-element.77), channel_id=1, source_target_pairs={{0,32},{16,48},{32,0},{48,16},{1,33},{17,49},{33,1},{49,17},{2,34}... | collective-permute-start | bytes 393224 | tf_op jit(solution)/shard_map/ppermute | solution.py:261
  99.0 10.7 %collective-permute-start.27 = (bf16[128,512]{1,0:T(8,128)(2,1)S(1)}, bf16[128,512]{1,0:T(8,128)(2,1)}, u32[]{:S(2)}, u32[]{:S(2)}) collective-permute-start(bf16[128,512]{1,0:T(8,128)(2,1)S(1)} %get-tuple-element.76), channel_id=1, source_target_pairs={{0,48},{16,0},{32,16},{48,32},{1,49},{17,1},{33,17},{49,33},{2,50}... | collective-permute-start | bytes 393224 | tf_op jit(solution)/shard_map/ppermute | solution.py:261
  111.4 19.5 %all-to-all-start.2 = ((bf16[16,8,512]{2,1,0:T(8,128)(2,1)}), bf16[16,8,512]{2,1,0:T(8,128)(2,1)S(1)}, u32[]{:S(2)}, u32[]{:S(2)}) async-start(bf16[16,8,512]{2,1,0:T(8,128)(2,1)} %fusion.13), calls=%async_computation.2 | async-start | bytes 262144 | tf_op jit(solution)/shard_map/all_to_all | solution.py:363
  122.0 9.6 %collective-permute-start.24 = (bf16[3,128,512]{2,1,0:T(8,128)(2,1)S(1)}, bf16[3,128,512]{2,1,0:T(8,128)(2,1)S(1)}, u32[]{:S(2)}, u32[]{:S(2)}) collective-permute-start(bf16[3,128,512]{2,1,0:T(8,128)(2,1)S(1)} %pad_maximum_fusion.4), channel_id=1, source_target_pairs={{0,1},{1,0},{2,3},{3,2},{4,5},{5,4},{6,7},{7,6},{8,9},{9,8},{10,11... | collective-permute-start | bytes 1179656 | tf_op jit(solution)/shard_map/ppermute | solution.py:265
